TPU v7x, 128 devices: a whole 4x4x4 slice. The times are simulated.
128 devices in a mesh: dp: 4 (over y), expert: 32 (over z, x, core).
Axes of the slice: x: 4, y: 4, z: 4, core: 2. Of those that a mesh axis runs over, the one named last changes fastest.
Arguments:
- tokens: bfloat16 [3072, 7168], P(('dp', 'expert')), may hold values from -6 to 6
- grad_out: bfloat16 [3072, 7168], P(('dp', 'expert')), may hold values from -6 to 6
- route_ids: int32 [3072, 8], P(('dp', 'expert')), may hold values from 0 to 127, all different within a row; in each aligned block of 24 rows (0 to 23, 24 to 47, ...) at most 2 rows name the same one
- route_weight: bfloat16 [3072, 8], P(('dp', 'expert')), may hold values from 0.049804688 to 1
- cluster_of: int32 [128], replicated, may hold values from 0 to 7, as said below
- gate_basis: bfloat16 [8, 512, 7168], P(None, 'expert', 'dp'), may hold values from -0.0625 to 0.0625
- up_basis: bfloat16 [8, 512, 7168], P(None, 'expert', 'dp'), may hold values from -0.0625 to 0.0625
- down_basis: bfloat16 [8, 512, 7168], P(None, 'expert', 'dp'), may hold values from -0.25 to 0.25
- gate_factor: bfloat16 [128, 512, 2048], P('expert', None, 'dp'), may hold values from -0.25 to 0.25
- up_factor: bfloat16 [128, 512, 2048], P('expert', None, 'dp'), may hold values from -0.25 to 0.25
- down_factor: bfloat16 [128, 2048, 512], P('expert', 'dp'), may hold values from -0.125 to 0.125
Outputs:
- grad_tokens: bfloat16 [3072, 7168], P(('dp', 'expert'))
- grad_route: float32 [3072, 8], P(('dp', 'expert'))
- grad_gate_basis: float32 [8, 512, 7168], P(None, 'expert', 'dp')
- grad_up_basis: float32 [8, 512, 7168], P(None, 'expert', 'dp')
- grad_down_basis: float32 [8, 512, 7168], P(None, 'expert', 'dp')
- grad_gate_factor: float32 [128, 512, 2048], P('expert', None, 'dp')
- grad_up_factor: float32 [128, 512, 2048], P('expert', None, 'dp')
- grad_down_factor: float32 [128, 2048, 512], P('expert', 'dp')
Inputs may be any that keep to these rules, and one draw needn't show every extreme that they name: `route_ids`: each token names 8 different experts. Among the 24 tokens of one block no expert is named more than 2 times, and in every draw some expert is named exactly 2 times in some block. `cluster_of`: never falls from one expert to the next; all 4 experts of each group of 4 consecutive experts share one cluster; every cluster holds 1 to 13 such groups, and one holds exactly 13.
All inputs are finite; a program needn't handle non-finite values.
Results may differ from a plain program's by a relative error of at most 0.013.
Values may be sent and summed in bfloat16 or wider, within the bound.
A program may use at most 128 MiB of HBM per device.

v0:
```python
import jax
import jax.numpy as jnp
from jax import lax
from jax.sharding import PartitionSpec as P


def silu_pair(pre):
    sig = jax.nn.sigmoid(pre)
    return (pre * sig, sig * (1.0 + pre * (1.0 - sig)))


def dp_total(terms):
    return lax.psum(terms, "dp")


def body(
    tokens,
    grad_out,
    route_ids,
    route_weight,
    cluster_of,
    gate_basis,
    up_basis,
    down_basis,
    gate_factor,
    up_factor,
    down_factor,
):
    fl = jnp.float32
    bf = jnp.bfloat16
    n_dp = lax.axis_size("dp")
    n_ex = lax.axis_size("expert")
    tok_rows, model_width = tokens.shape
    top_count = route_ids.shape[1]
    local_count = gate_factor.shape[0]
    experts = local_count * n_ex
    capacity = max(2, 5 * tok_rows * top_count // (4 * experts))
    slice_width = model_width // n_dp
    slot_cells = experts * capacity
    lane_rows = local_count * capacity
    sources = n_dp * n_ex
    total_rows = sources * lane_rows
    clusters = gate_basis.shape[0]
    rank = gate_factor.shape[1]
    flat_ids = route_ids.reshape(-1)
    matches = (flat_ids[:, None] == jnp.arange(experts, dtype=jnp.int32)[None, :]).astype(jnp.int32)
    slot_rank = jnp.sum(matches * jnp.cumsum(matches, axis=0), axis=1) - 1
    target = (flat_ids * capacity + slot_rank).reshape(tok_rows, top_count)
    placed = target[None, :, :] == jnp.arange(slot_cells, dtype=jnp.int32)[:, None, None]
    spread = jnp.any(placed, axis=2).astype(bf)
    slot_weight = jnp.sum(
        jnp.where(placed, route_weight[None].astype(fl), 0.0), axis=(1, 2)
    ).astype(bf)
    send_x = (
        jnp.einsum(
            "ct,tqf->qcf",
            spread,
            tokens.reshape(tok_rows, n_dp, slice_width),
            preferred_element_type=fl,
        )
        .astype(bf)
        .reshape(n_dp, n_ex, lane_rows, slice_width)
    )
    send_dy = (
        jnp.einsum(
            "ct,tqf->qcf",
            spread,
            grad_out.reshape(tok_rows, n_dp, slice_width),
            preferred_element_type=fl,
        )
        .astype(bf)
        .reshape(n_dp, n_ex, lane_rows, slice_width)
    )
    send_w = jnp.broadcast_to(slot_weight.reshape(1, n_ex, lane_rows), (n_dp, n_ex, lane_rows))
    got_x, got_dy, got_w = (
        lax.all_to_all(
            send_x.reshape(sources, lane_rows, slice_width),
            ("dp", "expert"),
            split_axis=0,
            concat_axis=0,
            tiled=True,
        ),
        lax.all_to_all(
            send_dy.reshape(sources, lane_rows, slice_width),
            ("dp", "expert"),
            split_axis=0,
            concat_axis=0,
            tiled=True,
        ),
        lax.all_to_all(
            send_w.reshape(sources, lane_rows),
            ("dp", "expert"),
            split_axis=0,
            concat_axis=0,
            tiled=True,
        ),
    )
    x_rows = got_x.reshape(total_rows, slice_width)
    dy_rows = got_dy.reshape(total_rows, slice_width)
    weight_rows = got_w.reshape(total_rows)
    group_cluster = cluster_of.reshape(n_ex, local_count)[:, 0]
    pick_table = (group_cluster[:, None] == jnp.arange(clusters, dtype=jnp.int32)[None, :]).astype(
        bf
    )
    stacked = jnp.stack([gate_basis, up_basis, down_basis])
    outgoing = jnp.einsum("jc,bcrf->jbrf", pick_table, stacked, preferred_element_type=fl).astype(
        bf
    )
    basis_rows = lax.all_to_all(outgoing, "expert", split_axis=0, concat_axis=2, tiled=True)
    gate_rows = basis_rows[0, 0]
    up_rows = basis_rows[0, 1]
    down_rows = basis_rows[0, 2]
    shape_four = (sources, local_count, capacity, rank)
    first_sums = dp_total(
        (
            jnp.einsum("nf,rf->nr", x_rows, gate_rows, preferred_element_type=fl),
            jnp.einsum("nf,rf->nr", x_rows, up_rows, preferred_element_type=fl),
        )
    )
    rank_gate = first_sums[0].astype(bf).reshape(shape_four)
    rank_up = first_sums[1].astype(bf).reshape(shape_four)
    gate_pre = jnp.einsum("sekr,erf->sekf", rank_gate, gate_factor, preferred_element_type=fl)
    up_pre = jnp.einsum("sekr,erf->sekf", rank_up, up_factor, preferred_element_type=fl)
    act, slope = silu_pair(gate_pre)
    hidden = (act * up_pre).astype(bf)
    mixed_sum = dp_total(
        (jnp.einsum("sekf,efr->sekr", hidden, down_factor, preferred_element_type=fl),)
    )
    mixed = mixed_sum[0].astype(bf).reshape(total_rows, rank)
    y_rows = jnp.dot(mixed, down_rows, preferred_element_type=fl)
    partial_dots = jnp.sum(y_rows * dy_rows.astype(fl), axis=1)
    upstream = (weight_rows[:, None].astype(fl) * dy_rows.astype(fl)).astype(bf)
    term_down = jnp.einsum("nr,nf->rf", mixed, upstream, preferred_element_type=fl)
    mixed_back = dp_total(
        (jnp.einsum("nf,rf->nr", upstream, down_rows, preferred_element_type=fl),)
    )
    grad_mixed = mixed_back[0].astype(bf).reshape(shape_four)
    grad_down_factor = jnp.einsum("sekf,sekr->efr", hidden, grad_mixed, preferred_element_type=fl)
    grad_hidden = jnp.einsum("sekr,efr->sekf", grad_mixed, down_factor, preferred_element_type=fl)
    grad_gate_pre = (grad_hidden * up_pre * slope).astype(bf)
    grad_up_pre = (grad_hidden * act).astype(bf)
    grad_gate_factor = jnp.einsum(
        "sekr,sekf->erf", rank_gate, grad_gate_pre, preferred_element_type=fl
    )
    grad_up_factor = jnp.einsum("sekr,sekf->erf", rank_up, grad_up_pre, preferred_element_type=fl)
    rank_back = dp_total(
        (
            jnp.einsum("sekf,erf->sekr", grad_gate_pre, gate_factor, preferred_element_type=fl),
            jnp.einsum("sekf,erf->sekr", grad_up_pre, up_factor, preferred_element_type=fl),
        )
    )
    grad_hg = rank_back[0].astype(bf).reshape(total_rows, rank)
    grad_hu = rank_back[1].astype(bf).reshape(total_rows, rank)
    term_gate = jnp.einsum("nr,nf->rf", grad_hg, x_rows, preferred_element_type=fl)
    term_up = jnp.einsum("nr,nf->rf", grad_hu, x_rows, preferred_element_type=fl)
    grad_x = (
        jnp.dot(grad_hg, gate_rows, preferred_element_type=fl)
        + jnp.dot(grad_hu, up_rows, preferred_element_type=fl)
    ).astype(bf)
    group_terms = jnp.stack([term_gate, term_up, term_down]).astype(bf)[None]
    gathered_terms = lax.all_to_all(group_terms, "expert", split_axis=2, concat_axis=0, tiled=True)
    cluster_grads = jnp.einsum(
        "jc,jbrf->cbrf", pick_table, gathered_terms, preferred_element_type=fl
    )
    returned = lax.all_to_all(
        grad_x.reshape(sources, lane_rows, slice_width),
        ("dp", "expert"),
        split_axis=0,
        concat_axis=0,
        tiled=True,
    )
    returned_dots = lax.all_to_all(
        partial_dots.reshape(sources, lane_rows),
        ("dp", "expert"),
        split_axis=0,
        concat_axis=0,
        tiled=True,
    )
    returned = returned.reshape(n_dp, slot_cells, slice_width)
    cell_scores = jnp.sum(returned_dots.reshape(n_dp, slot_cells), axis=0)
    grad_tokens = (
        jnp.einsum("ct,qcf->tqf", spread, returned, preferred_element_type=fl)
        .reshape(tok_rows, model_width)
        .astype(bf)
    )
    grad_route = jnp.sum(jnp.where(placed, cell_scores[:, None, None], 0.0), axis=0)
    return (
        grad_tokens,
        grad_route,
        cluster_grads[:, 0],
        cluster_grads[:, 1],
        cluster_grads[:, 2],
        grad_gate_factor,
        grad_up_factor,
        grad_down_factor,
    )


def solution(mesh):
    in_specs = (
        P(("dp", "expert"), None),
        P(("dp", "expert"), None),
        P(("dp", "expert"), None),
        P(("dp", "expert"), None),
        P(),
        P(None, "expert", "dp"),
        P(None, "expert", "dp"),
        P(None, "expert", "dp"),
        P("expert", None, "dp"),
        P("expert", None, "dp"),
        P("expert", "dp", None),
    )
    out_specs = (
        P(("dp", "expert"), None),
        P(("dp", "expert"), None),
        P(None, "expert", "dp"),
        P(None, "expert", "dp"),
        P(None, "expert", "dp"),
        P("expert", None, "dp"),
        P("expert", None, "dp"),
        P("expert", "dp", None),
    )
    return jax.shard_map(body, mesh=mesh, in_specs=in_specs, out_specs=out_specs, check_vma=False)
```

profile of v0, /device:TPU:0, one launch (start us, length us, event | category | flops | bytes accessed | tf_op | source)
XLA Modules:
  0.0 679.8 jit_solution(6809882957792762071)
XLA Ops:
  0.6 0.9 reshape.174
  1.7 1.2 copy.216
  2.8 1.4 copy_bitcast_fusion
  4.3 1.9 convolution_convert_fusion.1
  6.1 5.4 copy.159
  11.5 8.5 %all-to-all-start.2 = ((bf16[32,3,16,1792]{3,2,1,0:T(8,128)(2,1)}), bf16[32,3,16,1792]{3,2,1,0:T(8,128)(2,1)}, u32[]{:S(2)}, u32[]{:S(2)}) async-start(bf16[32,3,16,1792]{3,2,1,0:T(8,128)(2,1)} %copy.159), calls=%async_computation.2 | async-start | bytes 11010048 | tf_op jit(solution)/shard_map/all_to_all | solution.py:109
  21.0 3.0 convolution_convert_fusion.2
  24.0 64.7 %all-to-all-done.2 = bf16[32,3,16,1792]{3,2,1,0:T(8,128)(2,1)} async-done(((bf16[32,3,16,1792]{3,2,1,0:T(8,128)(2,1)}), bf16[32,3,16,1792]{3,2,1,0:T(8,128)(2,1)}, u32[]{:S(2)}, u32[]{:S(2)}) %all-to-all-start.2) | async-done | bytes 5505056 | tf_op jit(solution)/shard_map/all_to_all | solution.py:109
  88.8 6.1 all-to-all-start.3
  94.8 3.0 convolution_convert_fusion.3
  97.8 5.5 copy.160
  103.3 38.4 %all-to-all-done.3 = bf16[128,8,1792]{2,1,0:T(8,128)(2,1)} async-done(((bf16[128,8,1792]{2,1,0:T(8,128)(2,1)}), bf16[128,8,1792]{2,1,0:T(8,128)(2,1)}, u32[]{:S(2)}, u32[]{:S(2)}) %all-to-all-start.3) | async-done | bytes 3670048 | tf_op jit(solution)/shard_map/all_to_all | solution.py:76
  141.7 5.8 all-to-all-start.1
  147.5 6.0 fusion.11
  153.5 6.0 fusion.13
  159.5 100.6 %all-reduce.7 = (bf16[1024,512]{1,0:T(8,128)(2,1)S(1)}, bf16[1024,512]{1,0:T(8,128)(2,1)}) all-reduce(f32[1024,512]{1,0:T(8,128)} %fusion.11, f32[1024,512]{1,0:T(8,128)} %fusion.13), channel_id=1, replica_groups=mesh['dp'=4,'expert'=32] {'dp'}, use_global_device_ids=true, to_apply=%region_7.8 | all-reduce | flops 1048576 | bytes 6291456 | tf_op jit(solution)/shard_map/psum | solution.py:13
  260.1 1.2 reshape.179
  261.3 2.5 copy.173
  263.8 2.2 reshape.178
  266.1 3.7 copy.174
  269.8 2.5 fusion.40
  272.3 2.2 fusion.57
  274.5 1.0 copy-done.3
  275.5 2.0 fusion.62
  277.5 42.7 %all-reduce.8 = bf16[128,4,2,512]{3,0,2,1:T(8,128)(2,1)} all-reduce(f32[128,4,2,512]{3,0,2,1:T(8,128)} %fusion.62), channel_id=1, replica_groups=mesh['dp'=4,'expert'=32] {'dp'}, use_global_device_ids=true, to_apply=%region_10.11 | all-reduce | flops 524288 | bytes 3145728 | tf_op jit(solution)/shard_map/psum | solution.py:13
  320.2 3.3 copy.168
  323.5 2.3 reshape.184
  325.7 5.1 fusion.2
  330.8 0.7 all_to_all.56
  331.5 9.5 %all-to-all-start.5 = ((f32[128,1,8]{2,1,0:T(1,128)}), f32[128,1,8]{2,1,0:T(1,128)S(1)}, u32[]{:S(2)}, u32[]{:S(2)}) async-start(f32[128,1,8]{2,1,0:T(1,128)} %bitcast.44), calls=%async_computation.5 | async-start | bytes 131072 | tf_op jit(solution)/shard_map/all_to_all | solution.py:172
  341.1 9.1 %all-to-all-done.5 = f32[128,1,8]{2,1,0:T(1,128)S(1)} async-done(((f32[128,1,8]{2,1,0:T(1,128)}), f32[128,1,8]{2,1,0:T(1,128)S(1)}, u32[]{:S(2)}, u32[]{:S(2)}) %all-to-all-start.5) | async-done | bytes 4128 | tf_op jit(solution)/shard_map/all_to_all | solution.py:172
  350.7 0.8 reduce.5
  352.3 13.9 %all_to_all.69 = bf16[128,1,8]{2,1,0:T(2,128)(2,1)S(1)} all-to-all(bf16[128,1,8]{2,1,0:T(2,128)(2,1)S(1)} %copy.154), channel_id=1, replica_groups=mesh['dp'=4,'expert'=32] {'dp','expert'}, dimensions={0} | all-to-all | bytes 4096 | tf_op jit(solution)/shard_map/all_to_all | solution.py:90
  366.2 6.0 fusion.18
  372.3 42.8 %all-reduce.9 = bf16[1024,512]{1,0:T(8,128)(2,1)} all-reduce(f32[1024,512]{1,0:T(8,128)} %fusion.18), channel_id=1, replica_groups=mesh['dp'=4,'expert'=32] {'dp'}, use_global_device_ids=true, to_apply=%region_5.6 | all-reduce | flops 524288 | bytes 3145728 | tf_op jit(solution)/shard_map/psum | solution.py:13
  415.1 2.2 reshape.175
  417.4 4.3 fusion.58
  421.7 2.1 fusion.59
  423.8 1.0 copy-done.2
  424.8 2.1 fusion.65
  426.8 74.2 %all-reduce.10 = (bf16[128,4,2,512]{3,0,2,1:T(8,128)(2,1)S(1)}, bf16[128,4,2,512]{3,0,2,1:T(8,128)(2,1)}) all-reduce(f32[128,4,2,512]{3,0,2,1:T(8,128)} %fusion.65, f32[128,4,2,512]{3,0,2,1:T(8,128)} %fusion.59), channel_id=1, replica_groups=mesh['dp'=4,'expert'=32] {'dp'}, use_global_device_ids=true, to_apply=%region_8.9 | all-reduce | flops 1048576 | bytes 6291456 | tf_op jit(solution)/shard_map/psum | solution.py:13
  501.1 1.1 copy.165
  502.6 2.7 copy.166
  505.3 1.2 reshape.181
  506.5 3.7 fusion.68
  510.2 5.4 fusion.15
  515.6 6.9 %all-to-all-start.4 = ((bf16[128,8,1792]{2,1,0:T(8,128)(2,1)}), bf16[128,8,1792]{2,1,0:T(8,128)(2,1)}, u32[]{:S(2)}, u32[]{:S(2)}) async-start(bf16[128,8,1792]{2,1,0:T(8,128)(2,1)} %fusion.15), calls=%async_computation.4 | async-start | bytes 7340032 | tf_op jit(solution)/shard_map/all_to_all | solution.py:165
  522.5 4.5 fusion.29
  527.1 4.2 fusion.32
  531.3 4.4 fusion.35
  535.7 3.0 pad_maximum_fusion
  538.7 10.2 %copy.170 = bf16[1,3,512,1792]{3,1,0,2:T(4,128)(2,1)} copy(bf16[1,3,512,1792]{3,2,1,0:T(8,128)(2,1)} %pad_maximum_fusion) | data formatting | bytes 11010048 | tf_op jit(solution)/shard_map/stack | solution.py:160
  548.9 20.5 %all-to-all-done.4 = bf16[128,8,1792]{2,1,0:T(8,128)(2,1)} async-done(((bf16[128,8,1792]{2,1,0:T(8,128)(2,1)}), bf16[128,8,1792]{2,1,0:T(8,128)(2,1)}, u32[]{:S(2)}, u32[]{:S(2)}) %all-to-all-start.4) | async-done | bytes 3670048 | tf_op jit(solution)/shard_map/all_to_all | solution.py:165
  569.4 5.1 all-to-all-start.6
  575.2 2.7 convolution_bitcast_fusion.1
  577.9 2.7 convolution_bitcast_fusion.2
  580.7 3.0 convolution_bitcast_fusion
  583.7 6.0 copy.167
  589.7 3.8 convolution_convert_fusion
  593.5 73.3 %all-to-all-done.6 = bf16[1,3,512,1792]{3,1,0,2:T(4,128)(2,1)} async-done(((bf16[1,3,512,1792]{3,1,0,2:T(4,128)(2,1)}), bf16[1,3,512,1792]{3,1,0,2:T(4,128)(2,1)}, u32[]{:S(2)}, u32[]{:S(2)}) %all-to-all-start.6) | async-done | bytes 5505056 | tf_op jit(solution)/shard_map/all_to_all | solution.py:161
  666.8 9.0 %fusion.3 = f32[8,3,16,1792]{3,0,2,1:T(8,128)S(1)} fusion(bf16[1,3,32,16,1792]{4,1,3,2,0:T(4,128)(2,1)} %bitcast.49, s32[32]{0:T(128)S(1)} %slice_reduce_fusion), kind=kOutput, calls=%fused_computation.8 | convolution fusion | flops 44040448 | bytes 8257664 | tf_op jit(solution)/shard_map/jc,jbrf->cbrf/dot_general | solution.py:162
  676.0 1.2 copy.180
  677.2 1.2 copy.179
  678.4 1.2 copy.178
  (76 shorter events, 3.8 us)
Async XLA Ops:
  0.6 274.8 %copy-start = (bf16[4,512,512]{2,1,0:T(8,128)(2,1)S(1)}, bf16[4,512,512]{2,1,0:T(8,128)(2,1)}, u32[]{:S(2)}) copy-start(bf16[4,512,512]{2,1,0:T(8,128)(2,1)} %param.21) | copy-start | bytes 6291460
  11.5 8.5 %copy-start.21 = (s32[24,8]{0,1:T(8,128)S(1)}, s32[24,8]{0,1:T(8,128)}, u32[]{:S(2)}) copy-start(s32[24,8]{0,1:T(8,128)} %param.13) | copy-start | bytes 2308
  11.5 9.5 %copy-start.19 = (bf16[24,7168]{1,0:T(8,128)(2,1)S(1)}, bf16[24,7168]{1,0:T(8,128)(2,1)}, u32[]{:S(2)}) copy-start(bf16[24,7168]{1,0:T(8,128)(2,1)} %param.11) | copy-start | bytes 1032196
  11.5 77.2 %all-to-all-start.2 = ((bf16[32,3,16,1792]{3,2,1,0:T(8,128)(2,1)}), bf16[32,3,16,1792]{3,2,1,0:T(8,128)(2,1)}, u32[]{:S(2)}, u32[]{:S(2)}) async-start(bf16[32,3,16,1792]{3,2,1,0:T(8,128)(2,1)} %copy.159), calls=%async_computation.2 | async-start | bytes 11010048 | tf_op jit(solution)/shard_map/all_to_all | solution.py:109
  88.8 6.1 copy-start.20
  88.8 52.9 %all-to-all-start.3 = ((bf16[128,8,1792]{2,1,0:T(8,128)(2,1)}), bf16[128,8,1792]{2,1,0:T(8,128)(2,1)}, u32[]{:S(2)}, u32[]{:S(2)}) async-start(bf16[128,8,1792]{2,1,0:T(8,128)(2,1)} %bitcast.220), calls=%async_computation.3 | async-start | bytes 7340032 | tf_op jit(solution)/shard_map/all_to_all | solution.py:76
  141.7 184.0 %all-to-all-start.1 = ((bf16[128,8,1792]{2,1,0:T(8,128)(2,1)}), bf16[128,8,1792]{2,1,0:T(8,128)(2,1)}, u32[]{:S(2)}, u32[]{:S(2)}) async-start(bf16[128,8,1792]{2,1,0:T(8,128)(2,1)} %bitcast.219), calls=%async_computation.1 | async-start | bytes 7340032 | tf_op jit(solution)/shard_map/all_to_all | solution.py:83
  269.8 2.5 copy-start.10
  269.8 2.5 copy-start.12
  272.3 2.2 copy-start.14
  274.5 1.0 copy-start.3
  325.7 15.3 %copy-start.22 = (bf16[24,8]{0,1:T(8,128)(2,1)S(1)}, bf16[24,8]{0,1:T(8,128)(2,1)}, u32[]{:S(2)}) copy-start(bf16[24,8]{0,1:T(8,128)(2,1)} %param.14) | copy-start | bytes 1156
  331.5 18.7 %all-to-all-start.5 = ((f32[128,1,8]{2,1,0:T(1,128)}), f32[128,1,8]{2,1,0:T(1,128)S(1)}, u32[]{:S(2)}, u32[]{:S(2)}) async-start(f32[128,1,8]{2,1,0:T(1,128)} %bitcast.44), calls=%async_computation.5 | async-start | bytes 131072 | tf_op jit(solution)/shard_map/all_to_all | solution.py:172
  417.4 4.3 copy-start.11
  421.6 2.1 copy-start.8
  421.7 2.1 copy-start.6
  421.7 3.1 copy-start.2
  502.6 7.6 %copy-start.16 = (bf16[1024,512]{1,0:T(8,128)(2,1)}, bf16[1024,512]{1,0:T(8,128)(2,1)S(1)}, u32[]{:S(2)}) copy-start(bf16[1024,512]{1,0:T(8,128)(2,1)S(1)} %reshape.180) | copy-start | bytes 3145732
  506.5 3.7 copy-start.18
  515.6 53.8 %all-to-all-start.4 = ((bf16[128,8,1792]{2,1,0:T(8,128)(2,1)}), bf16[128,8,1792]{2,1,0:T(8,128)(2,1)}, u32[]{:S(2)}, u32[]{:S(2)}) async-start(bf16[128,8,1792]{2,1,0:T(8,128)(2,1)} %fusion.15), calls=%async_computation.4 | async-start | bytes 7340032 | tf_op jit(solution)/shard_map/all_to_all | solution.py:165
  522.5 4.6 copy-start.17
  527.1 4.2 copy-start.15
  548.9 26.3 %copy-start.9 = (bf16[128,4,2,512]{3,0,2,1:T(8,128)(2,1)S(1)}, bf16[128,4,2,512]{3,0,2,1:T(8,128)(2,1)}, u32[]{:S(2)}) copy-start(bf16[128,4,2,512]{3,0,2,1:T(8,128)(2,1)} %copy-done.8) | copy-start | bytes 3145732
  548.9 26.3 %copy-start.13 = (bf16[128,4,2,512]{0,3,2,1:T(8,128)(2,1)S(1)}, bf16[128,4,2,512]{0,3,2,1:T(8,128)(2,1)}, u32[]{:S(2)}) copy-start(bf16[128,4,2,512]{0,3,2,1:T(8,128)(2,1)} %copy.174) | copy-start | bytes 3145732
  569.4 97.4 %all-to-all-start.6 = ((bf16[1,3,512,1792]{3,1,0,2:T(4,128)(2,1)}), bf16[1,3,512,1792]{3,1,0,2:T(4,128)(2,1)}, u32[]{:S(2)}, u32[]{:S(2)}) async-start(bf16[1,3,512,1792]{3,1,0,2:T(4,128)(2,1)} %copy.170), calls=%async_computation.6 | async-start | bytes 14680064 | tf_op jit(solution)/shard_map/all_to_all | solution.py:161
  575.2 2.7 copy-start.7
  577.9 2.7 copy-start.4
  577.9 2.7 copy-start.5
  676.0 3.6 copy-start.1
where the time goes:
time: 689 us; the launch traced here: 680 us
  blocking collectives  274 us (40%)
  waiting for transfers between devices  206 us (30%)
  matrix products  89.6 us (13%)
  local copies, waits for them, and re-layouts  62.3 us (9%)
  starting transfers between devices  41.8 us (6%)
    psum x4, blocking collectives, dp_total(): return lax.psum(terms, 'dp')  260 us
    all_to_all x1, waiting for transfers between devices, body(): lax.all_to_all(group_terms, 'expert', split_axis=2, concat_axis=0, tiled=...  73.3 us
    all_to_all x1, waiting for transfers between devices, body(): lax.all_to_all(outgoing, 'expert', split_axis=0, concat_axis=2, tiled=True)  64.7 us
    all_to_all x1, waiting for transfers between devices, body(): lax.all_to_all(send_x.reshape(sources, lane_rows, slice_width), ('dp', 'e...  38.4 us
    all_to_all x1, waiting for transfers between devices, body(): lax.all_to_all(grad_x.reshape(sources, lane_rows, slice_width), ('dp', 'e...  20.5 us
    all_to_all x1, blocking collectives, body(): lax.all_to_all(send_w.reshape(sources, lane_rows), ('dp', 'expert'), spli...  13.9 us
  transfers between devices with their start and end apart: 6, of which 5 were waited for; matrix products, arithmetic and copies ran while one was open for 14% of the time, Pallas kernels for 0%

commit v1 on v0

v1 whole, which is shorter than its diff:
```python
import jax
import jax.numpy as jnp
from jax import lax
from jax.experimental import pallas as pl
from jax.experimental.pallas import tpu as pltpu
from jax.sharding import PartitionSpec as P

FL = jnp.float32
BF = jnp.bfloat16
MIB = 1024 * 1024


def dot(a, b, ca, cb):
    return lax.dot_general(a, b, (((ca,), (cb,)), ((), ())), preferred_element_type=FL)


def one_hot(slot_ref, j, tokens):
    row = slot_ref[pl.ds(j, 1), :]
    lanes = row.shape[1]
    grid = lax.broadcasted_iota(jnp.int32, (tokens, lanes), 0)
    return jnp.where(grid == row, 1.0, 0.0).astype(BF)


def pick_kernel(cluster, rows, slots, weights, out):
    groups, tokens, rank = out.shape[0], rows.shape[2], out.shape[3]

    def step(j, carry):
        c = cluster[j]
        own = rows[:, pl.ds(pl.multiple_of(c * rank, rank), rank), :].reshape(3 * rank, tokens)
        got = dot(own, one_hot(slots, j, tokens), 1, 0).reshape(3, rank, -1)
        got = jnp.concatenate([got[:2], got[2:] * weights[pl.ds(j, 1), :]], axis=0).astype(BF)
        half = got.shape[2] // 2
        out[j, 0] = got[:, :, :half]
        out[j, 1] = got[:, :, half:]
        return carry

    lax.fori_loop(0, groups, step, 0)


def pick(cluster, rows, slots, weights, rank):
    groups, lanes = slots.shape
    vmem = pl.BlockSpec(memory_space=pltpu.VMEM)
    return pl.pallas_call(
        pick_kernel,
        out_shape=jax.ShapeDtypeStruct((groups, 2, 3, rank, lanes // 2), BF),
        in_specs=[pl.BlockSpec(memory_space=pltpu.SMEM), vmem, vmem, vmem],
        out_specs=vmem,
        name="pick",
        compiler_params=pltpu.CompilerParams(vmem_limit_bytes=40 * MIB),
    )(cluster, rows, slots, weights)


def combine_kernel(cluster, parts, slots, weights, out, total):
    groups, rank, tokens = parts.shape[1], parts.shape[4], out.shape[2]
    total[...] = jnp.zeros_like(total)

    def step(j, carry):
        c = cluster[j]
        got = parts[0, j].astype(FL)
        for i in range(1, parts.shape[0]):
            got = got + parts[i, j].astype(FL)
        got = jnp.concatenate([got[0], got[1]], axis=2)
        got = jnp.concatenate([got[:2], got[2:] * weights[pl.ds(j, 1), :]], axis=0)
        got = got.astype(BF).reshape(3 * rank, -1)
        add = dot(got, one_hot(slots, j, tokens), 1, 1).reshape(3, rank, tokens)
        total[:, pl.ds(pl.multiple_of(c * rank, rank), rank), :] += add
        return carry

    lax.fori_loop(0, groups, step, 0)
    out[...] = total[...].astype(BF)


def combine(cluster, parts, slots, weights, clusters, tokens):
    rank = parts.shape[4]
    vmem = pl.BlockSpec(memory_space=pltpu.VMEM)
    shape = (3, clusters * rank, tokens)
    return pl.pallas_call(
        combine_kernel,
        out_shape=jax.ShapeDtypeStruct(shape, BF),
        in_specs=[pl.BlockSpec(memory_space=pltpu.SMEM), vmem, vmem, vmem],
        out_specs=vmem,
        scratch_shapes=[pltpu.VMEM(shape, FL)],
        name="combine",
        compiler_params=pltpu.CompilerParams(vmem_limit_bytes=40 * MIB),
    )(cluster, parts, slots, weights)


def mix(tiles):
    first, second = [], []
    for k in range(0, len(tiles), 2):
        a, b = tiles[k], tiles[k + 1]
        h = a.shape[-1] // 2
        first.append(jnp.concatenate([a[:, :h], b[:, :h]], axis=1))
        second.append(jnp.concatenate([a[:, h:], b[:, h:]], axis=1))
    return jnp.concatenate(first, axis=1), jnp.concatenate(second, axis=1)


def split_tiles(a):
    return [a[:, k : k + 128] for k in range(0, a.shape[1], 128)]


def expert_kernel(slots, gate, up, down, part, route, d_gate, d_up, d_down):
    rows = [mix(split_tiles(slots[0, k])) for k in range(3)]
    results = []
    for e in range(2):
        hg, hu, gm = rows[0][e], rows[1][e], rows[2][e]
        gf, uf, df = gate[e], up[e], down[e]
        gate_pre = dot(gf, hg, 0, 0)
        up_pre = dot(uf, hu, 0, 0)
        sig = 1.0 / (1.0 + jnp.exp(-gate_pre))
        act = gate_pre * sig
        slope = sig * (1.0 + gate_pre * (1.0 - sig))
        hidden = (act * up_pre).astype(BF)
        mixed = dot(df, hidden, 0, 0)
        grad_hidden = dot(df, gm, 1, 0)
        grad_gate_pre = (grad_hidden * up_pre * slope).astype(BF)
        grad_up_pre = (grad_hidden * act).astype(BF)
        route[0, e : e + 1] = jnp.sum(mixed * gm.astype(FL), axis=0, keepdims=True)
        d_down[e] = dot(hidden, gm, 1, 1)
        d_gate[e] = dot(hg, grad_gate_pre, 1, 1)
        d_up[e] = dot(hu, grad_up_pre, 1, 1)
        grad_hg = dot(gf, grad_gate_pre, 1, 0)
        grad_hu = dot(uf, grad_up_pre, 1, 0)
        results.append((grad_hg.astype(BF), grad_hu.astype(BF), mixed.astype(BF)))
    for k in range(3):
        tiles = []
        for a, b in zip(split_tiles(results[0][k]), split_tiles(results[1][k])):
            h = a.shape[-1] // 2
            tiles.append(jnp.concatenate([a[:, :h], b[:, :h]], axis=1))
            tiles.append(jnp.concatenate([a[:, h:], b[:, h:]], axis=1))
        part[0, k] = jnp.concatenate(tiles, axis=1)


def experts_step(slots, gate, up, down):
    count, rank, units = gate.shape
    lanes = slots.shape[3]

    def block(shape):
        return pl.BlockSpec((shape[0] // 2,) + shape[1:], lambda g: (g,) + (0,) * (len(shape) - 1))

    outs = [
        (slots.shape, BF),
        ((2, 2, lanes // 2), FL),
        (gate.shape, FL),
        (up.shape, FL),
        (down.shape, FL),
    ]
    return pl.pallas_call(
        expert_kernel,
        grid=(2,),
        out_shape=[jax.ShapeDtypeStruct(s, d) for s, d in outs],
        in_specs=[block(a.shape) for a in (slots, gate, up, down)],
        out_specs=[block(s) for s, _ in outs],
        name="experts_step",
        compiler_params=pltpu.CompilerParams(vmem_limit_bytes=56 * MIB),
    )(slots, gate, up, down)


def slot_tables(route_ids, route_weight, cells):
    flat = route_ids.reshape(-1)
    pairs = flat.shape[0]
    at = jnp.arange(pairs, dtype=jnp.int32)
    earlier = (flat[:, None] == flat[None, :]) & (at[None, :] < at[:, None])
    slot = jnp.sum(earlier.astype(jnp.int32), axis=1)
    placed = (flat * 2 + slot)[:, None] == jnp.arange(cells, dtype=jnp.int32)[None, :]
    token = at // route_ids.shape[1] + 1
    cell_token = jnp.sum(jnp.where(placed, token[:, None], 0), axis=0)
    cell_weight = jnp.sum(
        jnp.where(placed, route_weight.reshape(-1)[:, None].astype(FL), 0.0), axis=0
    )
    return placed, cell_token, cell_weight


def body(
    tokens,
    grad_out,
    route_ids,
    route_weight,
    cluster_of,
    gate_basis,
    up_basis,
    down_basis,
    gate_factor,
    up_factor,
    down_factor,
):
    n_dp = lax.axis_size("dp")
    n_ex = lax.axis_size("expert")
    tok_rows, width = tokens.shape
    local = gate_factor.shape[0]
    lane_rows = local * 2
    cells = n_ex * lane_rows
    clusters, rank, part_width = gate_basis.shape
    plane_tokens = n_ex * tok_rows
    all_rank = n_ex * rank

    placed, cell_token, cell_weight = slot_tables(route_ids, route_weight, cells)
    table = jnp.concatenate([cell_token.astype(FL), cell_weight]).reshape(4, 128)
    tables = lax.all_gather(table, "expert").reshape(n_ex, 2, n_ex, local, 2)
    tables = tables.transpose(1, 2, 3, 0, 4).reshape(2, n_ex, n_ex * lane_rows)
    block = (jnp.arange(n_ex * lane_rows, dtype=jnp.int32) // 2) % n_ex
    named = tables[0].astype(jnp.int32)
    slots = jnp.where(named > 0, named - 1 + tok_rows * block[None, :], -1)
    weights = tables[1]
    cluster = cluster_of.reshape(n_ex, local)[:, 0]

    x_all = lax.all_gather(tokens, "expert", axis=0, tiled=True)
    dy_all = lax.all_gather(grad_out, "expert", axis=0, tiled=True)
    bases = jnp.stack([gate_basis, up_basis, down_basis]).reshape(3, clusters * rank, part_width)
    bases = lax.all_gather(bases, "dp", axis=2, tiled=True)
    gate_up = bases[:2].reshape(2 * clusters * rank, width)
    down = bases[2]
    first = dot(gate_up, x_all, 1, 1).astype(BF).reshape(2, clusters * rank, plane_tokens)
    back = dot(down, dy_all, 1, 1).astype(BF)[None]
    picked = pick(cluster, jnp.concatenate([first, back]), slots, weights, rank)

    sent = jnp.broadcast_to(picked[None], (n_dp,) + picked.shape)
    sent = sent.reshape((n_dp * n_ex,) + picked.shape[1:])
    got = lax.all_to_all(sent, ("dp", "expert"), split_axis=0, concat_axis=0, tiled=True)
    got = got.reshape(n_dp, n_ex, 2, 3, rank, -1).transpose(2, 3, 1, 4, 0, 5)
    got = got.reshape(2, 3, all_rank, -1)
    part, route, d_gate_factor, d_up_factor, d_down_factor = experts_step(
        got, gate_factor, up_factor, down_factor
    )

    home = part.reshape(2, 3, n_ex, rank, n_dp, -1).transpose(4, 2, 0, 1, 3, 5)
    home = home.reshape((n_dp * n_ex,) + picked.shape[1:])
    home = lax.all_to_all(home, ("dp", "expert"), split_axis=0, concat_axis=0, tiled=True)
    home = home.reshape((n_dp, n_ex) + picked.shape[1:])
    summed = combine(cluster, home, slots, weights, clusters, plane_tokens)

    dots = route.reshape(local, n_dp, n_ex, 2).transpose(1, 2, 0, 3).reshape(n_dp * n_ex, lane_rows)
    dots = lax.all_to_all(dots, ("dp", "expert"), split_axis=0, concat_axis=0, tiled=True)
    scores = jnp.sum(dots.reshape(n_dp, cells), axis=0)
    scores = scores / jnp.where(cell_weight > 0.0, cell_weight, 1.0)
    grad_route = jnp.sum(jnp.where(placed, scores[None, :], 0.0), axis=1).reshape(route_ids.shape)

    back_up = summed[:2].reshape(2 * clusters * rank, plane_tokens)
    grad_gate_up = dot(back_up, x_all, 1, 0).astype(BF).reshape(2, clusters * rank, width)
    grad_down = dot(summed[2], dy_all, 1, 0).astype(BF)[None]
    terms = jnp.concatenate([grad_gate_up, grad_down])
    terms = lax.psum_scatter(terms, "dp", scatter_dimension=2, tiled=True).astype(FL)
    grad_x = dot(back_up, gate_up, 0, 0).astype(BF)
    grad_tokens = lax.psum_scatter(grad_x, "expert", scatter_dimension=0, tiled=True)
    shape = gate_basis.shape
    return (
        grad_tokens,
        grad_route,
        terms[0].reshape(shape),
        terms[1].reshape(shape),
        terms[2].reshape(shape),
        d_gate_factor,
        d_up_factor,
        d_down_factor,
    )


def solution(mesh):
    rows = P(("dp", "expert"), None)
    basis = P(None, "expert", "dp")
    factor = P("expert", None, "dp")
    low = P("expert", "dp", None)
    in_specs = (rows, rows, rows, rows, P(), basis, basis, basis, factor, factor, low)
    out_specs = (rows, rows, basis, basis, basis, factor, factor, low)
    return jax.shard_map(body, mesh=mesh, in_specs=in_specs, out_specs=out_specs, check_vma=False)
```

time: 689 us -> 517 us (0.75); the launches traced: 680 us -> 516 us
  blocking collectives: 274 us -> 135 us
  waiting for transfers between devices: 206 us -> 275 us
  matrix products: 89.6 us -> 34.1 us
  starting transfers between devices: 41.8 us -> 0.2 us
  local copies, waits for them, and re-layouts: 62.3 us -> 23.3 us
  Pallas kernels: 0 us -> 28.4 us
  between operations: 1.24 us -> 14.1 us
    psum x4 -> x0, blocking collectives: 260 us -> none  [dp_total(): return lax.psum(terms, 'dp')]
    all_to_all x6 -> x0, waiting for transfers between devices: 206 us -> none  [the longest x1 73.3 us: body(): lax.all_to_all(group_terms, 'expert', split_axis=2, concat_axis=0, tiled=...]
    all_gather x0 -> x3, waiting for transfers between devices: none -> 144 us  [the longest x1 58 us: body(): dy_all = lax.all_gather(grad_out, 'expert', axis=0, tiled=True)]
    reduce_scatter x0 -> x2, waiting for transfers between devices: none -> 130 us  [the longest x1 101 us: body(): lax.psum_scatter(grad_x, 'expert', scatter_dimension=0, tiled=True)]
    all_to_all x1 -> x3, blocking collectives: 13.9 us -> 109 us  [the longest x1 49.6 us: body(): lax.all_to_all(sent, ('dp', 'expert'), split_axis=0, concat_axis=0, tiled...]
    dot_general x23 -> x5, matrix products: 89.6 us -> 34.1 us  [dot(): lax.dot_general(a, b, (((ca,), (cb,)), ((), ())), preferred_element_type=FL)]
    all_to_all x6 -> x0, starting transfers between devices: 41.8 us -> none  [the longest x1 9.45 us: body(): lax.all_to_all(partial_dots.reshape(sources, lane_rows), ('dp', 'expert')...]
    pallas_call x0 -> x3, Pallas kernels: none -> 28.4 us  [the longest x1 11.9 us: experts_step(): pl.pallas_call(expert_kernel, grid=(2,), out_shape=[jax.ShapeDtypeStruct(...]
  transfers between devices with their start and end apart: 6 -> 5, of which waited for: 5 -> 5; matrix products, arithmetic and copies ran while one was open for 14% -> 6% of each run, Pallas kernels for 0% -> 0%
where the time goes in v1:
time: 517 us; the launch traced here: 516 us
  waiting for transfers between devices  275 us (53%)
  blocking collectives  135 us (26%)
  matrix products  34.1 us (7%)
  Pallas kernels  28.4 us (5%)
  local copies, waits for them, and re-layouts  23.3 us (5%)
  between operations  14.1 us (3%)
  other arithmetic  6.98 us (1%)
    reduce_scatter x1, waiting for transfers between devices, body(): lax.psum_scatter(grad_x, 'expert', scatter_dimension=0, tiled=True)  101 us
    all_gather x1, waiting for transfers between devices, body(): dy_all = lax.all_gather(grad_out, 'expert', axis=0, tiled=True)  58 us
    all_gather x1, waiting for transfers between devices, body(): x_all = lax.all_gather(tokens, 'expert', axis=0, tiled=True)  52.6 us
    all_to_all x1, blocking collectives, body(): lax.all_to_all(sent, ('dp', 'expert'), split_axis=0, concat_axis=0, tiled...  49.6 us
    all_to_all x1, blocking collectives, body(): lax.all_to_all(home, ('dp', 'expert'), split_axis=0, concat_axis=0, tiled...  46 us
    dot_general x5, matrix products, dot(): lax.dot_general(a, b, (((ca,), (cb,)), ((), ())), preferred_element_type=FL)  34.1 us
    all_gather x1, waiting for transfers between devices, body(): bases = lax.all_gather(bases, 'dp', axis=2, tiled=True)  32.9 us
    reduce_scatter x1, waiting for transfers between devices, body(): lax.psum_scatter(terms, 'dp', scatter_dimension=2, tiled=True).astype(FL)  29 us
  transfers between devices with their start and end apart: 5, of which 5 were waited for; matrix products, arithmetic and copies ran while one was open for 6% of the time, Pallas kernels for 0%

profile of v1, /device:TPU:0, one launch (start us, length us, event | category | flops | bytes accessed | tf_op | source)
XLA Modules:
  0.0 516.2 jit_solution(11219700400828523913)
XLA Ops:
  7.2 0.0 all-gather.4.cloned.1.call-start
  7.2 2.5 pad_maximum_fusion.1
  9.8 0.0 all-gather.8.cloned.1.call-start
  9.8 0.7 all-gather.8.cloned.1.call-update
  10.5 0.0 all-gather.6.cloned.1.call-start
  10.6 0.7 all-gather.6.cloned.1.call-update
  11.3 0.0 reduce-scatter.5.cloned.1.call-start
  11.3 0.1 copy.84
  11.4 0.1 reshape.156
  11.5 0.2 convert_reduce_fusion
  11.7 0.1 select_reduce_fusion.2
  11.9 0.1 copy.85
  11.9 0.1 reshape.169
  12.0 0.1 select_reduce_fusion.1
  12.2 25.6 %all_gather.15 = f32[32,4,128]{2,1,0:T(4,128)S(1)} all-gather(f32[1,4,128]{2,1,0:T(4,128)S(1)} %maximum_bitcast_fusion), channel_id=1, replica_groups=mesh['dp'=4,'expert'=32] {'expert'}, dimensions={0}, use_global_device_ids=true | all-gather | bytes 67584 | tf_op jit(solution)/shard_map/all_gather | solution.py:199
  37.7 0.1 copy.86
  37.9 0.1 copy.103
  38.0 0.1 copy.89
  38.1 0.1 copy.90
  38.2 0.2 copy.88
  38.4 0.1 gt.21
  38.5 0.1 copy.91
  38.6 0.1 copy.92
  38.7 0.1 copy.93.weights
  38.8 0.1 reshape.153
  38.9 0.1 slice_reduce_fusion.cluster
  39.0 32.9 %all-gather.4.cloned.1.call-done = bf16[3,128,7168]{2,1,0:T(8,128)(2,1)} async-done(((bf16[3,128,1792]{2,1,0:T(8,128)(2,1)}), bf16[3,128,7168]{2,1,0:T(8,128)(2,1)}) %all-gather.4.cloned.1.call-update) | async-done | bytes 5505040 | tf_op jit(solution)/shard_map/all_gather | solution.py:210
  71.9 4.1 slice.43
  76.0 58.0 %all-gather.8.cloned.1.call-done = bf16[768,7168]{1,0:T(8,128)(2,1)} async-done(((bf16[24,7168]{1,0:T(8,128)(2,1)}), bf16[768,7168]{1,0:T(8,128)(2,1)}) %all-gather.8.cloned.1.call-update) | async-done | bytes 11010064 | tf_op jit(solution)/shard_map/all_gather | solution.py:208
  134.0 8.4 %fusion.3 = bf16[1,128,768]{2,1,0:T(8,128)(2,1)S(1)} fusion(bf16[768,7168]{1,0:T(8,128)(2,1)} %all-gather.8.cloned.1.call-done, bf16[3,128,7168]{2,1,0:T(8,128)(2,1)} %all-gather.4.cloned.1.call-done), kind=kOutput, calls=%fused_computation.10 | convolution fusion | flops 1409384448 | bytes 13041664 | tf_op jit(solution)/shard_map/dot_general | solution.py:14
  142.4 52.6 %all-gather.6.cloned.1.call-done = bf16[768,7168]{1,0:T(8,128)(2,1)} async-done(((bf16[24,7168]{1,0:T(8,128)(2,1)}), bf16[768,7168]{1,0:T(8,128)(2,1)}) %all-gather.6.cloned.1.call-update) | async-done | bytes 11010064 | tf_op jit(solution)/shard_map/all_gather | solution.py:207
  195.1 8.3 %convolution_convert_fusion.2 = bf16[256,768]{1,0:T(8,128)(2,1)S(1)} fusion(bf16[256,7168]{1,0:T(8,128)(2,1)} %bitcast.60, bf16[768,7168]{1,0:T(8,128)(2,1)} %all-gather.6.cloned.1.call-done), kind=kOutput, calls=%fused_computation.8 | convolution fusion | flops 2818768896 | bytes 15073280 | tf_op jit(solution)/shard_map/dot_general | solution.py:14
  203.3 0.1 pad_maximum_fusion.2.rows
  203.4 7.1 %pick.1 = bf16[32,2,3,16,128]{4,3,2,1,0:T(8,128)(2,1)S(1)} custom-call(s32[32]{0:T(128)S(1)} %slice_reduce_fusion.cluster, bf16[3,128,768]{2,1,0:T(8,128)(2,1)S(1)} %pad_maximum_fusion.2.rows, s32[32,256]{1,0:T(8,128)S(1)} %add_select_fusion.slots, f32[32,256]{1,0:T(8,128)S(1)} %copy.93.weights), custom_call_target="tpu_custom_call" | custom-call | tf_op jit(solution)/shard_map/pick/pallas_call | solution.py:43
  210.6 0.5 broadcast_in_dim.64
  211.1 49.6 %all_to_all.19 = bf16[128,2,3,16,128]{4,3,2,1,0:T(8,128)(2,1)S(1)} all-to-all(bf16[128,2,3,16,128]{4,3,2,1,0:T(8,128)(2,1)S(1)} %bitcast.59), channel_id=1, replica_groups=mesh['dp'=4,'expert'=32] {'dp','expert'}, dimensions={0} | all-to-all | bytes 6291456 | tf_op jit(solution)/shard_map/all_to_all | solution.py:219
  260.6 4.0 copy.94
  264.7 3.3 reshape.160.slots
  267.9 11.9 %experts_step.1 = (bf16[2,3,512,512]{3,2,1,0:T(8,128)(2,1)}, f32[2,2,256]{2,1,0:T(2,128)}, f32[4,512,512]{2,1,0:T(8,128)}, f32[4,512,512]{2,1,0:T(8,128)}, f32[4,512,512]{2,1,0:T(8,128)}) custom-call(bf16[2,3,512,512]{3,2,1,0:T(8,128)(2,1)} %reshape.160.slots, bf16[4,512,512]{2,1,0:T(8,128)(2,1)} %gate.1, bf16[4,512,512]{2,1,0:T(8,128)(2,1)} %up.1, ...), custom_call_target="tpu_custom_call" | custom-call | tf_op jit(solution)/shard_map/experts_step/pallas_call | solution.py:148
  279.9 3.8 reshape.161
  283.6 0.5 copy.95
  284.2 46.0 %all_to_all.20 = bf16[128,2,3,16,128]{4,3,2,1,0:T(8,128)(2,1)S(1)} all-to-all(bf16[128,2,3,16,128]{4,3,2,1,0:T(8,128)(2,1)S(1)} %bitcast.58), channel_id=1, replica_groups=mesh['dp'=4,'expert'=32] {'dp','expert'}, dimensions={0} | all-to-all | bytes 6291456 | tf_op jit(solution)/shard_map/all_to_all | solution.py:228
  330.2 9.4 %combine.1 = bf16[3,128,768]{2,1,0:T(8,128)(2,1)S(1)} custom-call(s32[32]{0:T(128)S(1)} %slice_reduce_fusion.cluster, bf16[4,32,2,3,16,128]{5,4,3,2,1,0:T(8,128)(2,1)S(1)} %bitcast.55, s32[32,256]{1,0:T(8,128)S(1)} %add_select_fusion.slots, f32[32,256]{1,0:T(8,128)S(1)} %copy.93.weights), custom_call_target="tpu_custom_call" | custom-call | tf_op jit(solution)/shard_map/combine/pallas_call | solution.py:77
  339.6 5.9 %fusion = bf16[1,128,7168]{2,1,0:T(8,128)(2,1)S(1)} fusion(bf16[768,7168]{1,0:T(8,128)(2,1)} %all-gather.8.cloned.1.call-done, bf16[3,128,768]{2,1,0:T(8,128)(2,1)S(1)} %combine.1), kind=kOutput, calls=%fused_computation.3 | convolution fusion | flops 1410203648 | bytes 13041664 | tf_op jit(solution)/shard_map/dot_general | solution.py:14
  345.6 0.2 slice-done.2
  345.8 3.3 convolution_convert_fusion
  349.1 2.8 pad_maximum_fusion
  351.9 0.0 reduce-scatter.3.cloned.1.call-start
  352.0 8.2 %bitcast_convert_fusion = bf16[768,7168]{1,0:T(8,128)(2,1)} fusion(bf16[3,128,768]{2,1,0:T(8,128)(2,1)S(1)} %combine.1, bf16[3,128,7168]{2,1,0:T(8,128)(2,1)} %all-gather.4.cloned.1.call-done), kind=kOutput, calls=%fused_computation | convolution fusion | flops 2824077312 | bytes 15269888 | tf_op jit(solution)/shard_map/dot_general | solution.py:14
  360.2 0.7 copy-done
  360.9 0.2 reshape.164
  361.1 0.2 copy.98
  361.2 0.1 all_to_all.14
  361.3 0.1 copy.99
  361.4 13.4 %all_to_all.21 = f32[128,1,8]{2,1,0:T(1,128)S(1)} all-to-all(f32[128,1,8]{2,1,0:T(1,128)S(1)} %copy.99), channel_id=1, replica_groups=mesh['dp'=4,'expert'=32] {'dp','expert'}, dimensions={0} | all-to-all | bytes 8192 | tf_op jit(solution)/shard_map/all_to_all | solution.py:233
  374.8 0.5 broadcast.128
  375.3 0.8 reduce.5
  376.1 0.1 reshape.165
  376.2 0.2 select_reduce_fusion
  376.4 0.1 reshape.166
  376.5 0.7 copy.100
  377.2 29.0 %reduce-scatter.5.cloned.1.call-done = bf16[3,128,1792]{2,1,0:T(8,128)(2,1)} async-done(((bf16[3,128,7168]{2,1,0:T(8,128)(2,1)}), bf16[3,128,1792]{2,1,0:T(8,128)(2,1)}) %reduce-scatter.5.cloned.1.call-update) | async-done | bytes 1376272 | tf_op jit(solution)/shard_map/reduce_scatter | solution.py:242
  406.2 2.9 fusion.12
  409.1 100.5 %reduce-scatter.3.cloned.1.call-done = bf16[24,7168]{1,0:T(8,128)(2,1)} async-done(((bf16[768,7168]{1,0:T(8,128)(2,1)}), bf16[24,7168]{1,0:T(8,128)(2,1)}) %reduce-scatter.3.cloned.1.call-update) | async-done | bytes 344080 | tf_op jit(solution)/shard_map/reduce_scatter | solution.py:244
  (27 shorter events, 0.2 us)
Async XLA Ops:
  7.2 4.2 copy-start.1
  7.2 4.7 copy-start.2
  7.2 64.7 %all-gather.4.cloned.1.call-start = ((), (), s32[]{:S(2)}) async-start(), calls=%async_computation.5 | async-start | bytes 6881280 | tf_op jit(solution)/shard_map/all_gather | solution.py:210
  7.2 31.5 %copy-start.3 = (s32[128]{0:T(128)S(1)}, s32[128]{0:T(128)}, u32[]{:S(2)}) copy-start(s32[128]{0:T(128)} %param.15) | copy-start | bytes 1540
  9.8 124.2 %all-gather.8.cloned.1.call-start = ((), (), s32[]{:S(2)}) async-start(), calls=%async_computation.7 | async-start | bytes 11354112 | tf_op jit(solution)/shard_map/all_gather | solution.py:208
  10.5 184.5 %all-gather.6.cloned.1.call-start = ((), (), s32[]{:S(2)}) async-start(), calls=%async_computation.6 | async-start | bytes 11354112 | tf_op jit(solution)/shard_map/all_gather | solution.py:207
  11.3 395.0 %reduce-scatter.5.cloned.1.call-start = ((), (), s32[]{:S(2)}) async-start(), calls=%async_computation.9 | async-start | bytes 6881280 | tf_op jit(solution)/shard_map/reduce_scatter | solution.py:242
  330.2 15.4 %slice-start = ((s8[11010048]{0:T(1024)(128)(4,1)}), s8[4194304]{0:T(1024)(128)(4,1)S(1)}, s32[]{:S(2)}) async-start(s8[11010048]{0:T(1024)(128)(4,1)} %bitcast.77), calls=%async_computation.10 | async-start | bytes 8388608
  339.6 6.0 %slice-start.1 = ((s8[11010048]{0:T(1024)(128)(4,1)}), s8[4194304]{0:T(1024)(128)(4,1)S(1)}, s32[]{:S(2)}) async-start(s8[11010048]{0:T(1024)(128)(4,1)} %bitcast.77), calls=%async_computation.11 | async-start | bytes 8388608
  339.6 6.1 %slice-start.2 = ((s8[11010048]{0:T(1024)(128)(4,1)}), s8[2621440]{0:T(1024)(128)(4,1)S(1)}, s32[]{:S(2)}) async-start(s8[11010048]{0:T(1024)(128)(4,1)} %bitcast.77), calls=%async_computation.12 | async-start | bytes 5242880
  351.9 157.8 %reduce-scatter.3.cloned.1.call-start = ((), (), s32[]{:S(2)}) async-start(), calls=%async_computation.8 | async-start | bytes 11354112 | tf_op jit(solution)/shard_map/reduce_scatter | solution.py:244
  360.2 0.7 copy-start
Sparse Core Ops, SparseCore 0:
  10.3 61.5 all-gather.3
  74.1 59.8 all-gather.7
  136.3 58.7 all-gather.5
  352.0 54.1 reduce-scatter.4
  410.5 99.1 reduce-scatter.2

commit v2 on v1

--- a/solution.py
+++ b/solution.py
@@ -156,6 +156,281 @@
     )(slots, gate, up, down)
 
 
+def plane_place():
+    e = lax.axis_index("expert")
+    return e // 8, (e // 2) % 4, e % 2
+
+
+def slab_of(z, x, core):
+    return core * 16 + z * 4 + x
+
+
+class Copies:
+    def __init__(self, send, recv):
+        self.send, self.recv, self.count, self.sent = send, recv, 0, []
+        self.row = lax.axis_index("dp")
+        self.z, self.x, self.core = plane_place()
+
+    def make(self, src, dst, m, target):
+        return pltpu.make_async_remote_copy(
+            src_ref=src,
+            dst_ref=dst,
+            send_sem=self.send.at[m],
+            recv_sem=self.recv.at[m],
+            device_id=target,
+            device_id_type=pl.DeviceIdType.MESH,
+        )
+
+    def push(self, src, dst, target, land):
+        m = self.count
+        self.count += 1
+        copy = self.make(src, dst, m, target)
+        copy.start()
+        self.sent.append(copy)
+        return self.make(land, land, m, target).wait_recv
+
+    def device(self, dz, dx, flip=False):
+        z, x = (self.z + dz + 4) % 4, (self.x + dx + 4) % 4
+        core = 1 - self.core if flip else self.core
+        return (self.row, (z * 4 + x) * 2 + core)
+
+    def slab(self, dz, dx, flip=False):
+        z, x = (self.z + dz + 4) % 4, (self.x + dx + 4) % 4
+        core = 1 - self.core if flip else self.core
+        return slab_of(z, x, core)
+
+    def row_device(self, dy):
+        e = (self.z * 4 + self.x) * 2 + self.core
+        return ((self.row + dy + 4) % 4, e)
+
+    def finish(self):
+        for copy in self.sent:
+            copy.wait_send()
+
+
+def meet(targets):
+    barrier = pltpu.get_barrier_semaphore()
+    for target in targets:
+        pl.semaphore_signal(
+            barrier, inc=1, device_id=target, device_id_type=pl.DeviceIdType.MESH
+        )
+    pl.semaphore_wait(barrier, len(targets))
+
+
+OFFSETS = (0, -1, 1, 2)
+
+
+class SlabGather:
+    def __init__(self, copies, own, out, z_first, halves):
+        self.c, self.own, self.out, self.z_first, self.halves = copies, own, out, z_first, halves
+        self.across, self.done = [], []
+        self.cols = own.shape[-1] // 2
+
+    def at(self, p, q):
+        return (p, q) if self.z_first else (q, p)
+
+    def ref(self, p, q, flip=False):
+        return self.out.at[self.c.slab(*self.at(p, q), flip)]
+
+    def half(self, ref, h):
+        return ref.at[:, pl.ds(h * self.cols, self.cols)] if self.halves else ref
+
+    def to(self, p, q, src, dst, land):
+        return self.c.push(src, dst, self.c.device(*self.at(p, q)), land)
+
+    def cross(self, p, q, src=None):
+        ref = self.ref(p, q)
+        target = self.c.device(0, 0, True)
+        self.done.append(
+            self.c.push(ref if src is None else src, ref, target, self.ref(p, q, True))
+        )
+
+    def spread(self, p, src=None):
+        ref = self.ref(p, 0)
+        src = ref if src is None else src
+        ahead = self.to(0, 1, src, ref, self.ref(p, -1))
+        behind = self.to(0, -1, src, ref, self.ref(p, 1))
+        self.across.append((p, ahead, behind))
+
+    def start(self):
+        me = self.ref(0, 0)
+        self.from_behind = self.to(1, 0, self.own, me, self.ref(-1, 0))
+        self.from_ahead = self.to(-1, 0, self.own, me, self.ref(1, 0))
+
+    def start_own(self):
+        self.spread(0, self.own)
+        self.cross(0, 0, self.own)
+
+    def first(self):
+        self.from_behind()
+        ref, far = self.ref(-1, 0), self.ref(2, 0)
+        self.far = [self.to(1, 0, self.half(ref, 0), self.half(ref, 0), self.half(far, 0))]
+        self.spread(-1)
+        self.cross(-1, 0)
+
+    def second(self):
+        self.from_ahead()
+        if self.halves:
+            ref, far = self.ref(1, 0), self.ref(2, 0)
+            self.far.append(self.to(-1, 0, self.half(ref, 1), self.half(ref, 1), self.half(far, 1)))
+        self.spread(1)
+        self.cross(1, 0)
+
+    def third(self):
+        for wait in self.far:
+            wait()
+        self.spread(2)
+        self.cross(2, 0)
+
+    def ring(self, k):
+        p, ahead, behind = self.across[k]
+        if k == 0:
+            self.last = []
+        ahead()
+        if k < 2:
+            ref = self.ref(p, -1)
+            self.last.append((p, self.to(0, 1, ref, ref, self.ref(p, 2))))
+        self.cross(p, -1)
+        behind()
+        if k >= 2:
+            ref = self.ref(p, 1)
+            self.last.append((p, self.to(0, -1, ref, ref, self.ref(p, 2))))
+        self.cross(p, 1)
+
+    def end(self, k):
+        p, wait = self.last[k]
+        wait()
+        self.cross(p, 2)
+
+    def finish(self):
+        for wait in self.done:
+            wait()
+
+
+def gather_kernel(
+    x, dy, gate, up, down, table, xs, dys, tables, bases, other, send, recv, local
+):
+    c = Copies(send, recv)
+    width = gate.shape[1]
+    mine = c.slab(0, 0)
+    sources = (gate, up, down)
+
+    def columns(k, dy_, rows=None):
+        at = pl.ds(pl.multiple_of(((c.row + dy_ + 4) % 4) * width, 128), width)
+        ref = bases.at[k, :, at] if rows is None else bases.at[k, rows, at]
+        return ref
+
+    def other_columns(k, dy_):
+        at = pl.ds(pl.multiple_of(((c.row + dy_ + 4) % 4) * width, 128), width)
+        return other.at[k, :, at]
+
+    here = [
+        pltpu.make_async_copy(x, xs.at[mine], local.at[0]),
+        pltpu.make_async_copy(dy, dys.at[mine], local.at[1]),
+        pltpu.make_async_copy(table, tables.at[mine], local.at[2]),
+    ]
+    for k in range(3):
+        here.append(pltpu.make_async_copy(sources[k], columns(k, 0), local.at[3 + k]))
+    for copy in here:
+        copy.start()
+    meet(
+        [c.device(0, 1), c.device(0, -1), c.device(1, 0), c.device(-1, 0)]
+        + [c.device(0, 0, True), c.row_device(1), c.row_device(-1)]
+    )
+    parts = [
+        SlabGather(c, table, tables, True, False),
+        SlabGather(c, x, xs, True, True),
+        SlabGather(c, dy, dys, False, True),
+    ]
+    for part in parts:
+        part.start()
+    basis_waits, basis_done, basis_far = [], [], []
+
+    def basis_cross(k, dy_):
+        if k < 2:
+            ref = columns(k, dy_)
+            src = sources[k] if dy_ == 0 else ref
+            land = other_columns(k, dy_)
+            basis_done.append(c.push(src, land, c.device(0, 0, True), land))
+
+    for k in range(3):
+        ref = columns(k, 0)
+        basis_waits.append(
+            (
+                c.push(sources[k], ref, c.row_device(1), columns(k, -1)),
+                c.push(sources[k], ref, c.row_device(-1), columns(k, 1)),
+            )
+        )
+    for part in parts:
+        part.start_own()
+    for k in range(3):
+        basis_cross(k, 0)
+    for part in parts:
+        part.first()
+    for part in parts:
+        part.second()
+    for part in parts:
+        part.third()
+    half = gate.shape[0] // 2
+    for step in range(4):
+        for part in parts:
+            part.ring(step)
+        if step < 3:
+            ahead, behind = basis_waits[step]
+            low, high = pl.ds(0, half), pl.ds(half, half)
+            ahead()
+            ref = columns(step, -1, low)
+            far = [c.push(ref, ref, c.row_device(1), columns(step, 2, low))]
+            basis_cross(step, -1)
+            behind()
+            ref = columns(step, 1, high)
+            far.append(c.push(ref, ref, c.row_device(-1), columns(step, 2, high)))
+            basis_cross(step, 1)
+            basis_far.append(far)
+    for k in range(3):
+        for wait in basis_far[k]:
+            wait()
+        basis_cross(k, 2)
+    for step in range(4):
+        for part in parts:
+            part.end(step)
+    for part in parts:
+        part.finish()
+    for wait in basis_done:
+        wait()
+    for copy in here:
+        copy.wait()
+    c.finish()
+
+
+GATHER_COPIES = 32 + 32 + 31 + 20
+
+
+def gather_inputs(x, dy, gate, up, down, table, n_ex):
+    rows, width = gate.shape
+    slabs = jax.ShapeDtypeStruct((n_ex,) + x.shape, BF)
+    anywhere = pl.BlockSpec(memory_space=pl.ANY)
+    return pl.pallas_call(
+        gather_kernel,
+        out_shape=[
+            slabs,
+            slabs,
+            jax.ShapeDtypeStruct((n_ex,) + table.shape, FL),
+            jax.ShapeDtypeStruct((3, rows, 4 * width), BF),
+            jax.ShapeDtypeStruct((2, rows, 4 * width), BF),
+        ],
+        in_specs=[anywhere] * 6,
+        out_specs=[anywhere] * 5,
+        scratch_shapes=[
+            pltpu.SemaphoreType.DMA((GATHER_COPIES,)),
+            pltpu.SemaphoreType.DMA((GATHER_COPIES,)),
+            pltpu.SemaphoreType.DMA((6,)),
+        ],
+        name="gather_inputs",
+        compiler_params=pltpu.CompilerParams(collective_id=0, has_side_effects=True),
+    )(x, dy, gate, up, down, table)
+
+
 def slot_tables(route_ids, route_weight, cells):
     flat = route_ids.reshape(-1)
     pairs = flat.shape[0]
@@ -196,7 +471,19 @@
 
     placed, cell_token, cell_weight = slot_tables(route_ids, route_weight, cells)
     table = jnp.concatenate([cell_token.astype(FL), cell_weight]).reshape(4, 128)
-    tables = lax.all_gather(table, "expert").reshape(n_ex, 2, n_ex, local, 2)
+    flat = (clusters * rank, part_width)
+    x_all, dy_all, tables, bases, other = gather_inputs(
+        tokens,
+        grad_out,
+        gate_basis.reshape(flat),
+        up_basis.reshape(flat),
+        down_basis.reshape(flat),
+        table,
+        n_ex,
+    )
+    x_all = x_all.reshape(plane_tokens, width)
+    dy_all = dy_all.reshape(plane_tokens, width)
+    tables = tables.reshape(n_ex, 2, n_ex, local, 2)
     tables = tables.transpose(1, 2, 3, 0, 4).reshape(2, n_ex, n_ex * lane_rows)
     block = (jnp.arange(n_ex * lane_rows, dtype=jnp.int32) // 2) % n_ex
     named = tables[0].astype(jnp.int32)
@@ -204,10 +491,6 @@
     weights = tables[1]
     cluster = cluster_of.reshape(n_ex, local)[:, 0]
 
-    x_all = lax.all_gather(tokens, "expert", axis=0, tiled=True)
-    dy_all = lax.all_gather(grad_out, "expert", axis=0, tiled=True)
-    bases = jnp.stack([gate_basis, up_basis, down_basis]).reshape(3, clusters * rank, part_width)
-    bases = lax.all_gather(bases, "dp", axis=2, tiled=True)
     gate_up = bases[:2].reshape(2 * clusters * rank, width)
     down = bases[2]
     first = dot(gate_up, x_all, 1, 1).astype(BF).reshape(2, clusters * rank, plane_tokens)
@@ -229,7 +512,8 @@
     home = home.reshape((n_dp, n_ex) + picked.shape[1:])
     summed = combine(cluster, home, slots, weights, clusters, plane_tokens)
 
-    dots = route.reshape(local, n_dp, n_ex, 2).transpose(1, 2, 0, 3).reshape(n_dp * n_ex, lane_rows)
+    dots = route.reshape(local, n_dp, 2, n_ex // 2, 2).transpose(1, 3, 2, 0, 4)
+    dots = dots.reshape(n_dp * n_ex, lane_rows)
     dots = lax.all_to_all(dots, ("dp", "expert"), split_axis=0, concat_axis=0, tiled=True)
     scores = jnp.sum(dots.reshape(n_dp, cells), axis=0)
     scores = scores / jnp.where(cell_weight > 0.0, cell_weight, 1.0)
@@ -241,6 +525,8 @@
     terms = jnp.concatenate([grad_gate_up, grad_down])
     terms = lax.psum_scatter(terms, "dp", scatter_dimension=2, tiled=True).astype(FL)
     grad_x = dot(back_up, gate_up, 0, 0).astype(BF)
+    grad_x = grad_x.reshape(2, n_ex // 2, tok_rows, width).transpose(1, 0, 2, 3)
+    grad_x = grad_x.reshape(plane_tokens, width)
     grad_tokens = lax.psum_scatter(grad_x, "expert", scatter_dimension=0, tiled=True)
     shape = gate_basis.shape
     return (

time: 517 us -> 424 us (0.82)
  waiting for transfers between devices: 275 us -> 127 us
  Pallas kernels: 28.4 us -> 99.2 us
  blocking collectives: 135 us -> 108 us
  local copies, waits for them, and re-layouts: 23.3 us -> 38.1 us
    all_gather x3 -> x0, waiting for transfers between devices: 144 us -> none  [the longest x1 58 us: body(): dy_all = lax.all_gather(grad_out, 'expert', axis=0, tiled=True)]
    pallas_call x0 -> x1, Pallas kernels: none -> 70.7 us  [gather_inputs(): pl.pallas_call(gather_kernel, out_shape=[slabs, slabs, jax.ShapeDtypeStru...]
    all_gather x1 -> x0, blocking collectives: 25.6 us -> none  [body(): tables = lax.all_gather(table, 'expert').reshape(n_ex, 2, n_ex, local, 2)]
  transfers between devices with their start and end apart: 5 -> 2, of which waited for: 5 -> 2; matrix products, arithmetic and copies ran while one was open for 6% -> 4% of each run, Pallas kernels for 0% -> 0%
where the time goes in v2:
time: 424 us; the launch traced here: 423 us
  waiting for transfers between devices  127 us (30%)
  blocking collectives  108 us (25%)
  Pallas kernels  99.2 us (23%)
  local copies, waits for them, and re-layouts  38.1 us (9%)
  matrix products  31.3 us (7%)
  between operations  14.3 us (3%)
  other arithmetic  5.03 us (1%)
    reduce_scatter x1, waiting for transfers between devices, body(): lax.psum_scatter(grad_x, 'expert', scatter_dimension=0, tiled=True)  101 us
    pallas_call x1, Pallas kernels, gather_inputs(): pl.pallas_call(gather_kernel, out_shape=[slabs, slabs, jax.ShapeDtypeStru...  70.7 us
    all_to_all x1, blocking collectives, body(): lax.all_to_all(sent, ('dp', 'expert'), split_axis=0, concat_axis=0, tiled...  47.9 us
    all_to_all x1, blocking collectives, body(): lax.all_to_all(home, ('dp', 'expert'), split_axis=0, concat_axis=0, tiled...  46 us
    dot_general x5, matrix products, dot(): lax.dot_general(a, b, (((ca,), (cb,)), ((), ())), preferred_element_type=FL)  31.3 us
    reduce_scatter x1, waiting for transfers between devices, body(): lax.psum_scatter(terms, 'dp', scatter_dimension=2, tiled=True).astype(FL)  26.7 us
    all_to_all x1, blocking collectives, body(): lax.all_to_all(dots, ('dp', 'expert'), split_axis=0, concat_axis=0, tiled...  13.7 us
    pallas_call x1, Pallas kernels, experts_step(): pl.pallas_call(expert_kernel, grid=(2,), out_shape=[jax.ShapeDtypeStruct(...  12 us
  transfers between devices with their start and end apart: 2, of which 2 were waited for; matrix products, arithmetic and copies ran while one was open for 4% of the time, Pallas kernels for 0%

profile of v2, /device:TPU:0, one launch (start us, length us, event | category | flops | bytes accessed | tf_op | source)
XLA Modules:
  0.0 423.0 jit_solution(9994377323167558164)
XLA Ops:
  7.2 0.0 reduce-scatter.5.cloned.1.call-start
  7.2 0.8 copy.74
  8.0 0.1 reshape.176
  8.1 0.2 convert_reduce_fusion
  8.3 0.1 select_reduce_fusion.2
  8.4 0.8 copy.75
  9.2 0.1 reshape.195
  9.3 0.1 select_reduce_fusion.1
  9.4 0.6 pad_maximum_fusion.2.table
  10.0 70.7 %gather_inputs.1 = (bf16[32,24,7168]{2,1,0:T(8,128)(2,1)}, bf16[32,24,7168]{2,1,0:T(8,128)(2,1)}, f32[32,4,128]{2,1,0:T(4,128)}, bf16[3,128,7168]{2,1,0:T(8,128)(2,1)}, bf16[2,128,7168]{2,1,0:T(8,128)(2,1)}) custom-call(bf16[24,7168]{1,0:T(8,128)(2,1)} %x.1, bf16[24,7168]{1,0:T(8,128)(2,1)} %dy.1, bf16[128,1792]{1,0:T(8,128)(2,1)} %bitcast.81, ...), custom_call_target="tpu_custom_call" | custom-call | tf_op jit(solution)/shard_map/gather_inputs/pallas_call | solution.py:413
  80.6 1.0 copy.76
  81.6 0.1 copy.96
  81.8 4.1 slice.33
  85.9 0.0 copy-start.1
  85.9 8.4 %fusion.7 = bf16[1,128,768]{2,1,0:T(8,128)(2,1)S(1)} fusion(bf16[768,7168]{1,0:T(8,128)(2,1)} %bitcast.61, bf16[3,128,7168]{2,1,0:T(8,128)(2,1)} %get-tuple-element.17), kind=kOutput, calls=%fused_computation.10 | convolution fusion | flops 1409384448 | bytes 13041664 | tf_op jit(solution)/shard_map/dot_general | solution.py:14
  94.3 0.1 copy.79
  94.4 0.1 copy.80
  94.5 0.2 copy.78
  94.7 0.1 gt.21
  94.8 0.1 copy.81
  94.9 0.1 copy.82
  95.0 0.1 copy.83.weights
  95.0 0.0 copy-done.1
  95.0 0.1 reshape.172
  95.2 0.1 slice_reduce_fusion.cluster
  95.3 8.3 %convolution_convert_fusion.2 = bf16[256,768]{1,0:T(8,128)(2,1)S(1)} fusion(bf16[256,7168]{1,0:T(8,128)(2,1)} %bitcast.69, bf16[768,7168]{1,0:T(8,128)(2,1)} %bitcast.87), kind=kOutput, calls=%fused_computation.8 | convolution fusion | flops 2818768896 | bytes 15073280 | tf_op jit(solution)/shard_map/dot_general | solution.py:14
  103.6 0.1 pad_maximum_fusion.1.rows
  103.7 7.1 %pick.1 = bf16[32,2,3,16,128]{4,3,2,1,0:T(8,128)(2,1)S(1)} custom-call(s32[32]{0:T(128)S(1)} %slice_reduce_fusion.cluster, bf16[3,128,768]{2,1,0:T(8,128)(2,1)S(1)} %pad_maximum_fusion.1.rows, s32[32,256]{1,0:T(8,128)S(1)} %add_select_fusion.slots, f32[32,256]{1,0:T(8,128)S(1)} %copy.83.weights), custom_call_target="tpu_custom_call" | custom-call | tf_op jit(solution)/shard_map/pick/pallas_call | solution.py:43
  110.8 0.5 broadcast_in_dim.64
  111.3 47.9 %all_to_all.19 = bf16[128,2,3,16,128]{4,3,2,1,0:T(8,128)(2,1)S(1)} all-to-all(bf16[128,2,3,16,128]{4,3,2,1,0:T(8,128)(2,1)S(1)} %bitcast.68), channel_id=1, replica_groups=mesh['dp'=4,'expert'=32] {'dp','expert'}, dimensions={0} | all-to-all | bytes 6291456 | tf_op jit(solution)/shard_map/all_to_all | solution.py:502
  159.2 5.7 %copy.84 = bf16[2,3,32,16,4,128]{5,4,3,2,1,0:T(4,128)(2,1)} copy(bf16[2,3,32,16,4,128]{5,3,1,0,2,4:T(8,128)(2,1)S(1)} %bitcast.65) | data formatting | bytes 6291456 | tf_op jit(solution)/shard_map/transpose | solution.py:503
  164.9 5.7 %reshape.184.slots = bf16[2,3,512,512]{3,2,1,0:T(8,128)(2,1)} reshape(bf16[2,3,32,16,4,128]{5,4,3,2,1,0:T(4,128)(2,1)} %copy.84) | data formatting | bytes 6291456 | tf_op jit(solution)/shard_map/reshape | solution.py:504
  170.6 12.0 %experts_step.1 = (bf16[2,3,512,512]{3,2,1,0:T(8,128)(2,1)}, f32[2,2,256]{2,1,0:T(2,128)}, f32[4,512,512]{2,1,0:T(8,128)}, f32[4,512,512]{2,1,0:T(8,128)}, f32[4,512,512]{2,1,0:T(8,128)}) custom-call(bf16[2,3,512,512]{3,2,1,0:T(8,128)(2,1)} %reshape.184.slots, bf16[4,512,512]{2,1,0:T(8,128)(2,1)} %gate.1, bf16[4,512,512]{2,1,0:T(8,128)(2,1)} %up.1, ...), custom_call_target="tpu_custom_call" | custom-call | tf_op jit(solution)/shard_map/experts_step/pallas_call | solution.py:148
  182.6 5.5 %reshape.185 = bf16[2,3,32,16,4,128]{5,4,3,2,1,0:T(4,128)(2,1)} reshape(bf16[2,3,512,512]{3,2,1,0:T(8,128)(2,1)} %get-tuple-element.21) | data formatting | bytes 6291456 | tf_op jit(solution)/shard_map/reshape | solution.py:509
  188.2 2.4 copy.85
  190.5 46.0 %all_to_all.20 = bf16[128,2,3,16,128]{4,3,2,1,0:T(8,128)(2,1)S(1)} all-to-all(bf16[128,2,3,16,128]{4,3,2,1,0:T(8,128)(2,1)S(1)} %bitcast.67), channel_id=1, replica_groups=mesh['dp'=4,'expert'=32] {'dp','expert'}, dimensions={0} | all-to-all | bytes 6291456 | tf_op jit(solution)/shard_map/all_to_all | solution.py:511
  236.6 9.4 %combine.1 = bf16[3,128,768]{2,1,0:T(8,128)(2,1)S(1)} custom-call(s32[32]{0:T(128)S(1)} %slice_reduce_fusion.cluster, bf16[4,32,2,3,16,128]{5,4,3,2,1,0:T(8,128)(2,1)S(1)} %bitcast.60, s32[32,256]{1,0:T(8,128)S(1)} %add_select_fusion.slots, f32[32,256]{1,0:T(8,128)S(1)} %copy.83.weights), custom_call_target="tpu_custom_call" | custom-call | tf_op jit(solution)/shard_map/combine/pallas_call | solution.py:77
  246.0 0.0 slice-start.1
  246.0 0.0 slice-start.2
  246.0 6.0 %fusion = bf16[1,128,7168]{2,1,0:T(8,128)(2,1)S(1)} fusion(bf16[768,7168]{1,0:T(8,128)(2,1)} %bitcast.62, bf16[3,128,768]{2,1,0:T(8,128)(2,1)S(1)} %combine.1), kind=kOutput, calls=%fused_computation.3 | convolution fusion | flops 1410203648 | bytes 13041664 | tf_op jit(solution)/shard_map/dot_general | solution.py:14
  252.0 0.0 slice-done
  252.0 0.0 slice-done.1
  252.0 0.2 slice-done.2
  252.1 3.3 convolution_convert_fusion
  255.4 2.8 pad_maximum_fusion
  258.3 0.0 reduce-scatter.5.cloned.1.call-update
  258.3 0.0 reduce-scatter.3.cloned.1.call-start
  258.3 5.3 %bitcast_convert_fusion = bf16[768,7168]{1,0:T(8,128)(2,1)S(1)} fusion(bf16[3,128,768]{2,1,0:T(8,128)(2,1)S(1)} %combine.1, bf16[3,128,7168]{2,1,0:T(8,128)(2,1)} %get-tuple-element.17), kind=kOutput, calls=%fused_computation | convolution fusion | flops 2824077312 | bytes 15269888 | tf_op jit(solution)/shard_map/dot_general | solution.py:14
  263.7 4.8 %copy.88 = bf16[16,2,24,7168]{3,2,1,0:T(8,128)(2,1)} copy(bf16[16,2,24,7168]{3,2,0,1:T(8,128)(2,1)S(1)} %bitcast.64) | data formatting | bytes 22020096 | tf_op jit(solution)/shard_map/transpose | solution.py:528
  268.5 0.0 reduce-scatter.3.cloned.1.call-update
  268.6 0.7 copy-done
  269.2 0.2 reshape.190
  269.4 0.2 copy.93
  269.6 0.2 reshape.197
  269.8 13.7 %all_to_all.21 = f32[128,1,8]{2,1,0:T(1,128)S(1)} all-to-all(f32[128,1,8]{2,1,0:T(1,128)S(1)} %reshape.197), channel_id=1, replica_groups=mesh['dp'=4,'expert'=32] {'dp','expert'}, dimensions={0} | all-to-all | bytes 8192 | tf_op jit(solution)/shard_map/all_to_all | solution.py:517
  283.5 0.5 broadcast.128
  284.1 0.8 reduce.5
  284.9 0.1 reshape.191
  285.0 0.2 select_reduce_fusion
  285.2 0.1 reshape.192
  285.3 0.7 copy.91
  286.0 26.7 %reduce-scatter.5.cloned.1.call-done = bf16[3,128,1792]{2,1,0:T(8,128)(2,1)} async-done(((bf16[3,128,7168]{2,1,0:T(8,128)(2,1)}), bf16[3,128,1792]{2,1,0:T(8,128)(2,1)}) %reduce-scatter.5.cloned.1.call-update) | async-done | bytes 1376272 | tf_op jit(solution)/shard_map/reduce_scatter | solution.py:526
  312.6 2.9 fusion.18
  315.5 100.7 %reduce-scatter.3.cloned.1.call-done = bf16[24,7168]{1,0:T(8,128)(2,1)} async-done(((bf16[768,7168]{1,0:T(8,128)(2,1)}), bf16[24,7168]{1,0:T(8,128)(2,1)}) %reduce-scatter.3.cloned.1.call-update) | async-done | bytes 344080 | tf_op jit(solution)/shard_map/reduce_scatter | solution.py:530
  (13 shorter events, 0.1 us)
Async XLA Ops:
  7.2 305.5 %reduce-scatter.5.cloned.1.call-start = ((), (), s32[]{:S(2)}) async-start(), calls=%async_computation.6 | async-start | bytes 6881280 | tf_op jit(solution)/shard_map/reduce_scatter | solution.py:526
  85.9 9.2 %copy-start.1 = (s32[128]{0:T(128)S(1)}, s32[128]{0:T(128)}, u32[]{:S(2)}) copy-start(s32[128]{0:T(128)} %param.15) | copy-start | bytes 1540
  236.6 15.4 %slice-start = ((s8[11010048]{0:T(1024)(128)(4,1)}), s8[4194304]{0:T(1024)(128)(4,1)S(1)}, s32[]{:S(2)}) async-start(s8[11010048]{0:T(1024)(128)(4,1)} %bitcast.88), calls=%async_computation.7 | async-start | bytes 8388608
  246.0 6.0 %slice-start.1 = ((s8[11010048]{0:T(1024)(128)(4,1)}), s8[4194304]{0:T(1024)(128)(4,1)S(1)}, s32[]{:S(2)}) async-start(s8[11010048]{0:T(1024)(128)(4,1)} %bitcast.88), calls=%async_computation.8 | async-start | bytes 8388608
  246.0 6.1 %slice-start.2 = ((s8[11010048]{0:T(1024)(128)(4,1)}), s8[2621440]{0:T(1024)(128)(4,1)S(1)}, s32[]{:S(2)}) async-start(s8[11010048]{0:T(1024)(128)(4,1)} %bitcast.88), calls=%async_computation.9 | async-start | bytes 5242880
  258.3 157.9 %reduce-scatter.3.cloned.1.call-start = ((), (), s32[]{:S(2)}) async-start(), calls=%async_computation.5 | async-start | bytes 11354112 | tf_op jit(solution)/shard_map/reduce_scatter | solution.py:530
  268.5 0.7 copy-start
Sparse Core Ops, SparseCore 0:
  258.4 54.1 reduce-scatter.4
  317.0 99.1 reduce-scatter.2

commit v3 on v2

--- a/solution.py
+++ b/solution.py
@@ -19,35 +19,6 @@
     lanes = row.shape[1]
     grid = lax.broadcasted_iota(jnp.int32, (tokens, lanes), 0)
     return jnp.where(grid == row, 1.0, 0.0).astype(BF)
-
-
-def pick_kernel(cluster, rows, slots, weights, out):
-    groups, tokens, rank = out.shape[0], rows.shape[2], out.shape[3]
-
-    def step(j, carry):
-        c = cluster[j]
-        own = rows[:, pl.ds(pl.multiple_of(c * rank, rank), rank), :].reshape(3 * rank, tokens)
-        got = dot(own, one_hot(slots, j, tokens), 1, 0).reshape(3, rank, -1)
-        got = jnp.concatenate([got[:2], got[2:] * weights[pl.ds(j, 1), :]], axis=0).astype(BF)
-        half = got.shape[2] // 2
-        out[j, 0] = got[:, :, :half]
-        out[j, 1] = got[:, :, half:]
-        return carry
-
-    lax.fori_loop(0, groups, step, 0)
-
-
-def pick(cluster, rows, slots, weights, rank):
-    groups, lanes = slots.shape
-    vmem = pl.BlockSpec(memory_space=pltpu.VMEM)
-    return pl.pallas_call(
-        pick_kernel,
-        out_shape=jax.ShapeDtypeStruct((groups, 2, 3, rank, lanes // 2), BF),
-        in_specs=[pl.BlockSpec(memory_space=pltpu.SMEM), vmem, vmem, vmem],
-        out_specs=vmem,
-        name="pick",
-        compiler_params=pltpu.CompilerParams(vmem_limit_bytes=40 * MIB),
-    )(cluster, rows, slots, weights)
 
 
 def combine_kernel(cluster, parts, slots, weights, out, total):
@@ -99,61 +70,271 @@
     return [a[:, k : k + 128] for k in range(0, a.shape[1], 128)]
 
 
-def expert_kernel(slots, gate, up, down, part, route, d_gate, d_up, d_down):
-    rows = [mix(split_tiles(slots[0, k])) for k in range(3)]
-    results = []
-    for e in range(2):
-        hg, hu, gm = rows[0][e], rows[1][e], rows[2][e]
-        gf, uf, df = gate[e], up[e], down[e]
-        gate_pre = dot(gf, hg, 0, 0)
-        up_pre = dot(uf, hu, 0, 0)
-        sig = 1.0 / (1.0 + jnp.exp(-gate_pre))
-        act = gate_pre * sig
-        slope = sig * (1.0 + gate_pre * (1.0 - sig))
-        hidden = (act * up_pre).astype(BF)
-        mixed = dot(df, hidden, 0, 0)
-        grad_hidden = dot(df, gm, 1, 0)
-        grad_gate_pre = (grad_hidden * up_pre * slope).astype(BF)
-        grad_up_pre = (grad_hidden * act).astype(BF)
-        route[0, e : e + 1] = jnp.sum(mixed * gm.astype(FL), axis=0, keepdims=True)
-        d_down[e] = dot(hidden, gm, 1, 1)
-        d_gate[e] = dot(hg, grad_gate_pre, 1, 1)
-        d_up[e] = dot(hu, grad_up_pre, 1, 1)
-        grad_hg = dot(gf, grad_gate_pre, 1, 0)
-        grad_hu = dot(uf, grad_up_pre, 1, 0)
-        results.append((grad_hg.astype(BF), grad_hu.astype(BF), mixed.astype(BF)))
-    for k in range(3):
-        tiles = []
-        for a, b in zip(split_tiles(results[0][k]), split_tiles(results[1][k])):
-            h = a.shape[-1] // 2
-            tiles.append(jnp.concatenate([a[:, :h], b[:, :h]], axis=1))
-            tiles.append(jnp.concatenate([a[:, h:], b[:, h:]], axis=1))
-        part[0, k] = jnp.concatenate(tiles, axis=1)
-
-
-def experts_step(slots, gate, up, down):
-    count, rank, units = gate.shape
-    lanes = slots.shape[3]
-
-    def block(shape):
-        return pl.BlockSpec((shape[0] // 2,) + shape[1:], lambda g: (g,) + (0,) * (len(shape) - 1))
-
-    outs = [
-        (slots.shape, BF),
-        ((2, 2, lanes // 2), FL),
-        (gate.shape, FL),
-        (up.shape, FL),
-        (down.shape, FL),
+def middle_kernel(
+    member, rows, slots, weights, gate, up, down,
+    home, dots, kept_rows, kept_units,
+    picked, landed, parts, factors, row_store, unit_store, route,
+    out_send, out_recv, back_send, back_recv, dot_send, dot_recv, loads, local,
+):
+    row, e = lax.axis_index("dp"), lax.axis_index("expert")
+    groups, rank, tokens = picked.shape[0], picked.shape[3], rows.shape[2]
+    lanes = picked.shape[4]
+
+    def device(d, r):
+        return ((row + r) % 4, (e + d) % groups)
+
+    def source(d, r):
+        return ((row - r + 4) % 4, (e - d + groups) % groups)
+
+    def everyone(act):
+        for r in range(1, 4):
+            act(0, r)
+
+        def step(s, carry):
+            for r in range(4):
+                act((s * 11) % groups, r)
+            return carry
+
+        lax.fori_loop(1, groups, step, 0)
+
+    def remote(src, dst, send, recv, target):
+        return pltpu.make_async_remote_copy(
+            src_ref=src,
+            dst_ref=dst,
+            send_sem=send,
+            recv_sem=recv,
+            device_id=target,
+            device_id_type=pl.DeviceIdType.MESH,
+        )
+
+    def piece(ref, p, at):
+        sub = pl.ds(pl.multiple_of(at[1] * rank, rank), rank)
+        lane = pl.ds(pl.multiple_of(at[0] * lanes, lanes), lanes)
+        return ref.at[p, :, sub, lane]
+
+    def out_copy(p, d, r):
+        target = device(d, r)
+        n = d * 4 + r
+        return remote(
+            picked.at[target[1], p],
+            piece(landed, p, (row, e)),
+            out_send.at[p, n],
+            out_recv.at[p, n],
+            target,
+        )
+
+    def out_wait(p, d, r):
+        n = d * 4 + r
+        land = piece(landed, p, source(d, r))
+        remote(land, land, out_send.at[p, n], out_recv.at[p, n], device(d, r)).wait_recv()
+
+    def back_copy(p, d, r):
+        target = device(d, r)
+        n = d * 4 + r
+        return remote(
+            piece(parts, p, target),
+            home.at[row, e, p],
+            back_send.at[p, n],
+            back_recv.at[p, n],
+            target,
+        )
+
+    def back_wait(p, d, r):
+        n = d * 4 + r
+        at = source(d, r)
+        land = home.at[at[0], at[1], p]
+        remote(land, land, back_send.at[p, n], back_recv.at[p, n], device(d, r)).wait_recv()
+
+    def dot_copy(d, r):
+        target = device(d, r)
+        n = d * 4 + r
+        return remote(
+            route.at[target[0]], dots.at[row, e], dot_send.at[n], dot_recv.at[n], target
+        )
+
+    def dot_wait(d, r):
+        n = d * 4 + r
+        at = source(d, r)
+        land = dots.at[at[0], at[1]]
+        remote(land, land, dot_send.at[n], dot_recv.at[n], device(d, r)).wait_recv()
+
+    incoming = [
+        pltpu.make_async_copy(ref, factors.at[k], loads.at[k])
+        for k, ref in enumerate((gate, up, down))
     ]
+    for copy in incoming:
+        copy.start()
+    barrier = pltpu.get_barrier_semaphore()
+
+    def greet(d, r):
+        pl.semaphore_signal(
+            barrier, inc=1, device_id=device(d, r), device_id_type=pl.DeviceIdType.MESH
+        )
+
+    everyone(greet)
+
+    def pick_for(j):
+        own = jnp.zeros((3, rank, tokens), BF)
+        for c in range(member.shape[1]):
+            share = member[pl.ds(j, 1), c : c + 1].astype(BF)[None]
+            own = own + rows[:, c * rank : (c + 1) * rank, :] * share
+        got = dot(own.reshape(3 * rank, tokens), one_hot(slots, j, tokens), 1, 0)
+        got = got.reshape(3, rank, -1)
+        got = jnp.concatenate([got[:2], got[2:] * weights[pl.ds(j, 1), :]], axis=0).astype(BF)
+        picked[j, 0] = got[:, :, :lanes]
+        picked[j, 1] = got[:, :, lanes:]
+
+    pick_for(e)
+    own_copies = [
+        pltpu.make_async_copy(picked.at[e, p], piece(landed, p, (row, e)), local.at[p])
+        for p in range(2)
+    ]
+    for copy in own_copies:
+        copy.start()
+    pl.semaphore_wait(barrier, 4 * groups - 1)
+    for r in range(1, 4):
+        out_copy(0, 0, r).start()
+
+    def pick_step(s, carry):
+        d = (s * 11) % groups
+        pick_for((e + d) % groups)
+        for r in range(4):
+            out_copy(0, d, r).start()
+        return carry
+
+    lax.fori_loop(1, groups, pick_step, 0)
+    everyone(lambda d, r: out_copy(1, d, r).start())
+    for copy in incoming:
+        copy.wait()
+    for copy in own_copies:
+        copy.wait()
+    stores = []
+    for p in range(2):
+        everyone(lambda d, r: out_wait(p, d, r))
+        wide = [mix(split_tiles(landed[p, k])) for k in range(3)]
+        results = []
+        for n in range(2):
+            hg, hu, gm = wide[0][n], wide[1][n], wide[2][n]
+            ex = 2 * p + n
+            row_store[ex, 0] = hg
+            row_store[ex, 1] = hu
+            row_store[ex, 2] = gm
+            gf, uf, df = factors[0, ex], factors[1, ex], factors[2, ex]
+            gate_pre = dot(gf, hg, 0, 0)
+            up_pre = dot(uf, hu, 0, 0)
+            sig = 1.0 / (1.0 + jnp.exp(-gate_pre))
+            act = gate_pre * sig
+            slope = sig * (1.0 + gate_pre * (1.0 - sig))
+            hidden = (act * up_pre).astype(BF)
+            mixed = dot(df, hidden, 0, 0)
+            grad_hidden = dot(df, gm, 1, 0)
+            grad_gate_pre = (grad_hidden * up_pre * slope).astype(BF)
+            grad_up_pre = (grad_hidden * act).astype(BF)
+            unit_store[ex, 0] = grad_gate_pre
+            unit_store[ex, 1] = grad_up_pre
+            unit_store[ex, 2] = hidden
+            scores = jnp.sum(mixed * gm.astype(FL), axis=0, keepdims=True)
+            each = lanes // 2
+            for i in range(4):
+                route[i, p : p + 1, n * each : (n + 1) * each] = scores[:, i * each : (i + 1) * each]
+            grad_hg = dot(gf, grad_gate_pre, 1, 0)
+            grad_hu = dot(uf, grad_up_pre, 1, 0)
+            results.append((grad_hg.astype(BF), grad_hu.astype(BF), mixed.astype(BF)))
+        for k in range(3):
+            tiles = []
+            for a, b in zip(split_tiles(results[0][k]), split_tiles(results[1][k])):
+                h = a.shape[-1] // 2
+                tiles.append(jnp.concatenate([a[:, :h], b[:, :h]], axis=1))
+                tiles.append(jnp.concatenate([a[:, h:], b[:, h:]], axis=1))
+            parts[p, k] = jnp.concatenate(tiles, axis=1)
+        everyone(lambda d, r: back_copy(p, d, r).start())
+        pair = pl.ds(2 * p, 2)
+        here = [
+            pltpu.make_async_copy(piece(parts, p, (row, e)), home.at[row, e, p], local.at[2 + p]),
+            pltpu.make_async_copy(row_store.at[pair], kept_rows.at[pair], local.at[4 + p]),
+            pltpu.make_async_copy(unit_store.at[pair], kept_units.at[pair], local.at[6 + p]),
+        ]
+        for copy in here:
+            copy.start()
+        stores += here
+    everyone(lambda d, r: dot_copy(d, r).start())
+    own_dots = pltpu.make_async_copy(route.at[row], dots.at[row, e], local.at[8])
+    own_dots.start()
+    stores.append(own_dots)
+    for p in range(2):
+        everyone(lambda d, r: back_wait(p, d, r))
+    everyone(dot_wait)
+    for copy in stores:
+        copy.wait()
+    for p in range(2):
+        everyone(lambda d, r: out_copy(p, d, r).wait_send())
+        everyone(lambda d, r: back_copy(p, d, r).wait_send())
+    everyone(lambda d, r: dot_copy(d, r).wait_send())
+
+
+def middle(member, rows, slots, weights, gate, up, down, n_dp):
+    groups, lanes = slots.shape
+    kinds, ranks, _ = rows.shape
+    count, all_rank, units = gate.shape
+    rank = all_rank // groups
+    half = lanes // 2
+    anywhere = pl.BlockSpec(memory_space=pl.ANY)
+    vmem = pl.BlockSpec(memory_space=pltpu.VMEM)
+    kept = jax.ShapeDtypeStruct((count, 3, all_rank, n_dp * half // 2), BF)
+    dma = pltpu.SemaphoreType.DMA
     return pl.pallas_call(
-        expert_kernel,
-        grid=(2,),
-        out_shape=[jax.ShapeDtypeStruct(s, d) for s, d in outs],
-        in_specs=[block(a.shape) for a in (slots, gate, up, down)],
-        out_specs=[block(s) for s, _ in outs],
-        name="experts_step",
-        compiler_params=pltpu.CompilerParams(vmem_limit_bytes=56 * MIB),
-    )(slots, gate, up, down)
+        middle_kernel,
+        out_shape=[
+            jax.ShapeDtypeStruct((n_dp, groups, 2, 3, rank, half), BF),
+            jax.ShapeDtypeStruct((n_dp, groups, 2, half), FL),
+            kept,
+            kept,
+        ],
+        in_specs=[vmem] * 4 + [anywhere] * 3,
+        out_specs=[anywhere] * 4,
+        scratch_shapes=[
+            pltpu.VMEM((groups, 2, 3, rank, half), BF),
+            pltpu.VMEM((2, 3, all_rank, n_dp * half), BF),
+            pltpu.VMEM((2, 3, all_rank, n_dp * half), BF),
+            pltpu.VMEM((3,) + gate.shape, BF),
+            pltpu.VMEM(kept.shape, BF),
+            pltpu.VMEM(kept.shape, BF),
+            pltpu.VMEM((n_dp, 2, half), FL),
+            dma((2, n_dp * groups)),
+            dma((2, n_dp * groups)),
+            dma((2, n_dp * groups)),
+            dma((2, n_dp * groups)),
+            dma((n_dp * groups,)),
+            dma((n_dp * groups,)),
+            dma((3,)),
+            dma((9,)),
+        ],
+        name="middle",
+        compiler_params=pltpu.CompilerParams(
+            collective_id=2, has_side_effects=True, vmem_limit_bytes=56 * MIB
+        ),
+    )(member, rows, slots, weights, gate, up, down)
+
+
+def factor_kernel(rows, units, d_gate, d_up, d_down):
+    d_gate[0] = dot(rows[0, 0], units[0, 0], 1, 1)
+    d_up[0] = dot(rows[0, 1], units[0, 1], 1, 1)
+    d_down[0] = dot(units[0, 2], rows[0, 2], 1, 1)
+
+
+def factor_grads(rows, units):
+    count, _, all_rank, lanes = rows.shape
+    held = pl.BlockSpec((1,) + rows.shape[1:], lambda g: (g, 0, 0, 0))
+    one = pl.BlockSpec((1, all_rank, units.shape[2]), lambda g: (g, 0, 0))
+    return pl.pallas_call(
+        factor_kernel,
+        grid=(count,),
+        out_shape=[jax.ShapeDtypeStruct((count, all_rank, units.shape[2]), FL)] * 3,
+        in_specs=[held, held],
+        out_specs=[one] * 3,
+        name="factor_grads",
+        compiler_params=pltpu.CompilerParams(vmem_limit_bytes=40 * MIB),
+    )(rows, units)
 
 
 def plane_place():
@@ -431,6 +612,214 @@
     )(x, dy, gate, up, down, table)
 
 
+def home_kernel(
+    rows, x, dy, bases, other,
+    out, d_gate, d_up, d_down,
+    paired, xb, db, bb, terms, far_in, near_in, turned, full, got, passed, kept, last,
+    send, recv, loads,
+):
+    c = Copies(send, recv)
+    width = d_gate.shape[1]
+    near = (1, -1, 2)
+    meet(
+        [c.device(0, d) for d in near]
+        + [c.device(d, 0) for d in near]
+        + [c.device(0, 0, True), c.row_device(1), c.row_device(-1)]
+    )
+    partner = c.push(rows.at[pl.ds(0, 2)], paired, c.device(0, 0, True), paired)
+    order = (2, 1, -1, 0)
+
+    def load_rows(n):
+        at = pl.ds(pl.multiple_of(((c.row + order[n] + 4) % 4) * width, 128), width)
+        slot = n % 2
+        copies = [
+            pltpu.make_async_copy(x.at[:, at], xb.at[slot], loads.at[2 * slot]),
+            pltpu.make_async_copy(dy.at[:, at], db.at[slot], loads.at[2 * slot + 1]),
+        ]
+        for copy in copies:
+            copy.start()
+        return copies
+
+    def load_bases(n):
+        at = pl.ds(n * width, width)
+        slot = n % 2
+        copies = [
+            pltpu.make_async_copy(
+                bases.at[pl.ds(0, 2), :, at], bb.at[slot, 0], loads.at[4 + 2 * slot]
+            ),
+            pltpu.make_async_copy(other.at[:, :, at], bb.at[slot, 1], loads.at[5 + 2 * slot]),
+        ]
+        for copy in copies:
+            copy.start()
+        return copies
+
+    flying = [load_rows(0), load_rows(1)]
+    basis_flying = [load_bases(0), load_bases(1)]
+    low, high = pl.ds(0, 64), pl.ds(64, 64)
+    near_waits = [[], []]
+    far_waits = [[], []]
+    for n in range(4):
+        for copy in flying[n]:
+            copy.wait()
+        slot = n % 2
+
+        def columns(k, carry):
+            at = pl.ds(pl.multiple_of(k * 256, 256), 256)
+            ups = dot(rows[0:2].reshape(256, -1), xb[slot, :, at], 1, 0)
+            downs = dot(rows[2], db[slot, :, at], 1, 0)
+            if n < 3:
+                terms[n, 0, :, at] = ups[:128].astype(BF)
+                terms[n, 1, :, at] = ups[128:].astype(BF)
+                terms[n, 2, :, at] = downs.astype(BF)
+            else:
+                d_gate[:, at] = ups[:128]
+                d_up[:, at] = ups[128:]
+                d_down[:, at] = downs
+            return carry
+
+        lax.fori_loop(0, width // 256, columns, 0)
+        if n < 2:
+            flying.append(load_rows(n + 2))
+        for k in range(3):
+            if n == 0:
+                land = far_in.at[0, k]
+                far_waits[0].append(c.push(terms.at[0, k, low], land, c.row_device(1), land))
+                land = far_in.at[1, k]
+                far_waits[1].append(c.push(terms.at[0, k, high], land, c.row_device(-1), land))
+            if n == 1:
+                land = near_in.at[0, k, high]
+                near_waits[0].append(c.push(terms.at[1, k, high], land, c.row_device(1), land))
+            if n == 2:
+                land = near_in.at[1, k, low]
+                near_waits[1].append(c.push(terms.at[2, k, low], land, c.row_device(-1), land))
+    partner()
+    half_tokens = turned.shape[0]
+    mine = pl.ds(pl.multiple_of(c.core * half_tokens, 128), half_tokens)
+    for k in range(2):
+        for n, source in enumerate((rows, paired)):
+            at = pl.ds((2 * n + k) * 128, 128)
+            turned[:, at] = source[k, :, mine].astype(FL).T.astype(BF)
+    tok = full.shape[2]
+    place = (c.z, c.x)
+    got_waits = [[], []]
+    for n in range(4):
+        for copy in basis_flying[n]:
+            copy.wait()
+        slot, h = n % 2, n // 2
+
+        def token_columns(k, carry):
+            at = pl.ds(pl.multiple_of(k * 256, 256), 256)
+            to = pl.ds(pl.multiple_of((n % 2) * width + k * 256, 256), 256)
+            both = jnp.concatenate(
+                [bb[slot, s, k2, :, at] for s in range(2) for k2 in range(2)], axis=0
+            )
+            sums = dot(turned[...], both, 1, 0)
+            for s in range(16):
+                full[h, s, :, to] = sums[s * tok : (s + 1) * tok].astype(BF)
+            return carry
+
+        lax.fori_loop(0, width // 256, token_columns, 0)
+        if n < 2:
+            basis_flying.append(load_bases(n + 2))
+        if n % 2 == 1:
+            for b in (1, -1, 2, 0):
+                waits = []
+                for di, d in enumerate(near):
+                    if h == 0:
+                        slab = ((c.z + b + 4) % 4) * 4 + (c.x + d + 4) % 4
+                        target = c.device(0, d)
+                    else:
+                        slab = ((c.z + d + 4) % 4) * 4 + (c.x + b + 4) % 4
+                        target = c.device(d, 0)
+                    land = got.at[h, di, b % 4]
+                    waits.append(c.push(full.at[h, slab], land, target, land))
+                got_waits[h].append((b, waits))
+    for k in range(3):
+        far_waits[0][k]()
+        terms[1, k, low] = (terms[1, k, low].astype(FL) + far_in[0, k].astype(FL)).astype(BF)
+        land = near_in.at[0, k, low]
+        near_waits[0].append(c.push(terms.at[1, k, low], land, c.row_device(1), land))
+        far_waits[1][k]()
+        terms[2, k, high] = (terms[2, k, high].astype(FL) + far_in[1, k].astype(FL)).astype(BF)
+        land = near_in.at[1, k, high]
+        near_waits[1].append(c.push(terms.at[2, k, high], land, c.row_device(-1), land))
+    last_waits = [[], []]
+    for step in range(4):
+        for h in range(2):
+            b, waits = got_waits[h][step]
+            for wait in waits:
+                wait()
+            if h == 0:
+                slab = ((c.z + b + 4) % 4) * 4 + c.x
+                target = c.device(b, 0)
+            else:
+                slab = c.z * 4 + (c.x + b + 4) % 4
+                target = c.device(0, b)
+            total = full[h, slab].astype(FL)
+            for di in range(3):
+                total = total + got[h, di, b % 4].astype(FL)
+            if b == 0:
+                kept[h] = total
+            else:
+                passed[h, step] = total.astype(BF)
+                land = last.at[h, step]
+                last_waits[h].append(c.push(passed.at[h, step], land, target, land))
+    for h in range(2):
+        for wait in last_waits[h]:
+            wait()
+        total = kept[h]
+        for step in range(3):
+            total = total + last[h, step].astype(FL)
+        out[:, h * 2 * width : (h + 1) * 2 * width] = total.astype(BF)
+    for side in range(2):
+        for wait in near_waits[side]:
+            wait()
+    for k, ref in enumerate((d_gate, d_up, d_down)):
+        ref[...] = ref[...] + near_in[0, k].astype(FL) + near_in[1, k].astype(FL)
+    c.finish()
+
+
+HOME_COPIES = 1 + 18 + 24 + 6
+
+
+def send_home(rows, x, dy, bases, other, tok):
+    kinds, ranks, tokens = rows.shape
+    full_width = x.shape[1]
+    width = full_width // 4
+    half = full_width // 2
+    anywhere = pl.BlockSpec(memory_space=pl.ANY)
+    vmem = pl.BlockSpec(memory_space=pltpu.VMEM)
+    basis = jax.ShapeDtypeStruct((ranks, width), FL)
+    return pl.pallas_call(
+        home_kernel,
+        out_shape=[jax.ShapeDtypeStruct((tok, full_width), BF), basis, basis, basis],
+        in_specs=[vmem] + [anywhere] * 4,
+        out_specs=[vmem] * 4,
+        scratch_shapes=[
+            pltpu.VMEM((2, ranks, tokens), BF),
+            pltpu.VMEM((2, tokens, width), BF),
+            pltpu.VMEM((2, tokens, width), BF),
+            pltpu.VMEM((2, 2, 2, ranks, width), BF),
+            pltpu.VMEM((3, kinds, ranks, width), BF),
+            pltpu.VMEM((2, kinds, ranks // 2, width), BF),
+            pltpu.VMEM((2, kinds, ranks, width), BF),
+            pltpu.VMEM((tokens // 2, 4 * ranks), BF),
+            pltpu.VMEM((2, 16, tok, half), BF),
+            pltpu.VMEM((2, 3, 4, tok, half), BF),
+            pltpu.VMEM((2, 3, tok, half), BF),
+            pltpu.VMEM((2, tok, half), FL),
+            pltpu.VMEM((2, 3, tok, half), BF),
+            pltpu.SemaphoreType.DMA((HOME_COPIES,)),
+            pltpu.SemaphoreType.DMA((HOME_COPIES,)),
+            pltpu.SemaphoreType.DMA((8,)),
+        ],
+        name="send_home",
+        compiler_params=pltpu.CompilerParams(
+            collective_id=1, has_side_effects=True, vmem_limit_bytes=60 * MIB
+        ),
+    )(rows, x, dy, bases, other)
+
+
 def slot_tables(route_ids, route_weight, cells):
     flat = route_ids.reshape(-1)
     pairs = flat.shape[0]
@@ -495,39 +884,21 @@
     down = bases[2]
     first = dot(gate_up, x_all, 1, 1).astype(BF).reshape(2, clusters * rank, plane_tokens)
     back = dot(down, dy_all, 1, 1).astype(BF)[None]
-    picked = pick(cluster, jnp.concatenate([first, back]), slots, weights, rank)
-
-    sent = jnp.broadcast_to(picked[None], (n_dp,) + picked.shape)
-    sent = sent.reshape((n_dp * n_ex,) + picked.shape[1:])
-    got = lax.all_to_all(sent, ("dp", "expert"), split_axis=0, concat_axis=0, tiled=True)
-    got = got.reshape(n_dp, n_ex, 2, 3, rank, -1).transpose(2, 3, 1, 4, 0, 5)
-    got = got.reshape(2, 3, all_rank, -1)
-    part, route, d_gate_factor, d_up_factor, d_down_factor = experts_step(
-        got, gate_factor, up_factor, down_factor
+    rows = jnp.concatenate([first, back])
+    member = cluster[:, None] == jnp.arange(clusters, dtype=jnp.int32)[None, :]
+    home, dots, kept_rows, kept_units = middle(
+        member.astype(FL), rows, slots, weights, gate_factor, up_factor, down_factor, n_dp
     )
-
-    home = part.reshape(2, 3, n_ex, rank, n_dp, -1).transpose(4, 2, 0, 1, 3, 5)
-    home = home.reshape((n_dp * n_ex,) + picked.shape[1:])
-    home = lax.all_to_all(home, ("dp", "expert"), split_axis=0, concat_axis=0, tiled=True)
-    home = home.reshape((n_dp, n_ex) + picked.shape[1:])
+    d_gate_factor, d_up_factor, d_down_factor = factor_grads(kept_rows, kept_units)
     summed = combine(cluster, home, slots, weights, clusters, plane_tokens)
 
-    dots = route.reshape(local, n_dp, 2, n_ex // 2, 2).transpose(1, 3, 2, 0, 4)
-    dots = dots.reshape(n_dp * n_ex, lane_rows)
-    dots = lax.all_to_all(dots, ("dp", "expert"), split_axis=0, concat_axis=0, tiled=True)
-    scores = jnp.sum(dots.reshape(n_dp, cells), axis=0)
+    z, x, core = plane_place()
+    dots = jnp.sum(dots, axis=0).reshape(n_ex, local, n_ex, 2)
+    scores = lax.dynamic_index_in_dim(dots, slab_of(z, x, core), 2, False).reshape(cells)
     scores = scores / jnp.where(cell_weight > 0.0, cell_weight, 1.0)
     grad_route = jnp.sum(jnp.where(placed, scores[None, :], 0.0), axis=1).reshape(route_ids.shape)
 
-    back_up = summed[:2].reshape(2 * clusters * rank, plane_tokens)
-    grad_gate_up = dot(back_up, x_all, 1, 0).astype(BF).reshape(2, clusters * rank, width)
-    grad_down = dot(summed[2], dy_all, 1, 0).astype(BF)[None]
-    terms = jnp.concatenate([grad_gate_up, grad_down])
-    terms = lax.psum_scatter(terms, "dp", scatter_dimension=2, tiled=True).astype(FL)
-    grad_x = dot(back_up, gate_up, 0, 0).astype(BF)
-    grad_x = grad_x.reshape(2, n_ex // 2, tok_rows, width).transpose(1, 0, 2, 3)
-    grad_x = grad_x.reshape(plane_tokens, width)
-    grad_tokens = lax.psum_scatter(grad_x, "expert", scatter_dimension=0, tiled=True)
+    grad_tokens, *terms = send_home(summed, x_all, dy_all, bases, other, tok_rows)
     shape = gate_basis.shape
     return (
         grad_tokens,

time: 424 us -> 298 us (0.70)
  Pallas kernels: 99.2 us -> 259 us
  waiting for transfers between devices: 127 us -> 0 us
  blocking collectives: 108 us -> 0 us
  local copies, waits for them, and re-layouts: 38.1 us -> 17.1 us
  matrix products: 31.3 us -> 14.6 us
  between operations: 14.3 us -> 0.9 us
    pallas_call x2 -> x3, Pallas kernels: 19.2 us -> 179 us  [the longest x1 99.7 us: middle(): pl.pallas_call(middle_kernel, out_shape=[jax.ShapeDtypeStruct((n_dp, grou...]
    reduce_scatter x2 -> x0, waiting for transfers between devices: 127 us -> none  [the longest x1 101 us: body(): lax.psum_scatter(grad_x, 'expert', scatter_dimension=0, tiled=True)]
    all_to_all x3 -> x0, blocking collectives: 108 us -> none  [the longest x1 47.9 us: body(): lax.all_to_all(sent, ('dp', 'expert'), split_axis=0, concat_axis=0, tiled...]
    dot_general x5 -> x2, matrix products: 31.3 us -> 14.6 us  [dot(): lax.dot_general(a, b, (((ca,), (cb,)), ((), ())), preferred_element_type=FL)]
    transpose x3 -> x0, local copies, waits for them, and re-layouts: 12.9 us -> none  [the longest x1 5.71 us: body(): got = got.reshape(n_dp, n_ex, 2, 3, rank, -1).transpose(2, 3, 1, 4, 0, 5)]
    reshape x4 -> x1, local copies, waits for them, and re-layouts: 11.5 us -> 0.71 us  [body(): lax.dynamic_index_in_dim(dots, slab_of(z, x, core), 2, False).reshape(cells)]
    unnamed x12 -> x34, local copies, waits for them, and re-layouts: 2.27 us -> 9.98 us
  transfers between devices with their start and end apart: 2 -> 0, of which waited for: 2 -> 0; matrix products, arithmetic and copies ran while one was open for 4% -> 0% of each run, Pallas kernels for 0% -> 0%
where the time goes in v3:
time: 298 us
  Pallas kernels  259 us (87%)
  local copies, waits for them, and re-layouts  17.1 us (6%)
  matrix products  14.6 us (5%)
  other arithmetic  5.86 us (2%)
    pallas_call x1, Pallas kernels, middle(): pl.pallas_call(middle_kernel, out_shape=[jax.ShapeDtypeStruct((n_dp, grou...  99.7 us
    pallas_call x1, Pallas kernels, send_home(): pl.pallas_call(home_kernel, out_shape=[jax.ShapeDtypeStruct((tok, full_wi...  74.3 us
    pallas_call x1, Pallas kernels, gather_inputs(): pl.pallas_call(gather_kernel, out_shape=[slabs, slabs, jax.ShapeDtypeStru...  70.7 us
    dot_general x2, matrix products, dot(): lax.dot_general(a, b, (((ca,), (cb,)), ((), ())), preferred_element_type=FL)  14.6 us
    unnamed x34, local copies, waits for them, and re-layouts  9.98 us
    pallas_call x1, Pallas kernels, combine(): pl.pallas_call(combine_kernel, out_shape=jax.ShapeDtypeStruct(shape, BF),...  9.37 us

profile of v3, /device:TPU:0, one launch (start us, length us, event | category | flops | bytes accessed | tf_op | source)
XLA Modules:
  0.0 297.7 jit_solution(1484172511820414994)
XLA Ops:
  0.6 0.7 reshape.148
  1.4 0.1 slice_reduce_fusion.cluster
  1.5 0.7 fusion.12.member
  2.2 0.8 copy.59
  2.9 0.1 reshape.164
  3.0 0.8 copy.58
  3.8 0.1 reshape.152
  3.9 0.2 convert_reduce_fusion
  4.1 0.0 copy-start.12
  4.1 0.1 select_reduce_fusion.1
  4.2 0.0 copy-start.13
  4.2 0.4 copy-done.12
  4.7 0.1 select_reduce_fusion.2
  4.8 0.0 copy-done.13
  4.8 0.6 pad_maximum_fusion.1.table
  5.4 70.7 %gather_inputs.1 = (bf16[32,24,7168]{2,1,0:T(8,128)(2,1)}, bf16[32,24,7168]{2,1,0:T(8,128)(2,1)}, f32[32,4,128]{2,1,0:T(4,128)}, bf16[3,128,7168]{2,1,0:T(8,128)(2,1)}, bf16[2,128,7168]{2,1,0:T(8,128)(2,1)}) custom-call(bf16[24,7168]{1,0:T(8,128)(2,1)} %x.1, bf16[24,7168]{1,0:T(8,128)(2,1)} %dy.1, bf16[128,1792]{1,0:T(8,128)(2,1)} %bitcast.50, ...), custom_call_target="tpu_custom_call" | custom-call | tf_op jit(solution)/shard_map/gather_inputs/pallas_call | solution.py:594
  76.1 0.0 copy-start.6
  76.1 8.5 %fusion.6 = bf16[1,128,768]{2,1,0:T(8,128)(2,1)S(1)} fusion(bf16[768,7168]{1,0:T(8,128)(2,1)} %bitcast.36, bf16[3,128,7168]{2,1,0:T(8,128)(2,1)} %get-tuple-element.24.bases), kind=kOutput, calls=%fused_computation.5 | convolution fusion | flops 1409384448 | bytes 13041664 | tf_op jit(solution)/shard_map/dot_general | solution.py:14
  84.6 0.0 copy-done.6
  84.6 0.2 slice.18
  84.9 0.0 copy-start.11
  84.9 6.1 %convolution_convert_fusion = bf16[256,768]{1,0:T(8,128)(2,1)S(1)} fusion(bf16[256,7168]{1,0:T(8,128)(2,1)S(1)} %bitcast.40, bf16[768,7168]{1,0:T(8,128)(2,1)} %bitcast.38), kind=kOutput, calls=%fused_computation.3 | convolution fusion | flops 2818768896 | bytes 15073280 | tf_op jit(solution)/shard_map/dot_general | solution.py:14
  90.9 0.9 pad_maximum_fusion.rows
  91.8 0.0 copy-done.11
  91.8 0.1 copy.60
  92.0 0.1 copy.73
  92.0 0.2 copy.62
  92.2 0.1 gt.21
  92.3 0.1 copy.65
  92.4 0.1 copy.63
  92.5 0.1 copy.64
  92.6 0.6 add_select_fusion.slots
  93.3 0.1 copy.66
  93.4 0.7 copy.67.weights
  94.1 99.7 %middle.1 = (bf16[4,32,2,3,16,128]{5,4,3,2,1,0:T(8,128)(2,1)}, f32[4,32,2,128]{3,2,1,0:T(2,128)}, bf16[4,3,512,256]{3,2,1,0:T(8,128)(2,1)}, bf16[4,3,512,256]{3,2,1,0:T(8,128)(2,1)}) custom-call(f32[32,8]{1,0:T(8,128)} %fusion.12.member, bf16[3,128,768]{2,1,0:T(8,128)(2,1)} %pad_maximum_fusion.rows, s32[32,256]{1,0:T(8,128)} %add_select_fusion.slots, ...), custom_call_target="tpu_custom_call" | custom-call | tf_op jit(solution)/shard_map/middle/pallas_call | solution.py:285
  193.7 0.0 copy-done.4
  193.8 0.0 copy-done.5
  193.8 0.0 copy-start.2
  193.8 1.9 copy-done.2
  195.7 9.4 %combine.1.rows = bf16[3,128,768]{2,1,0:T(8,128)(2,1)S(1)} custom-call(s32[32]{0:T(128)S(1)} %slice_reduce_fusion.cluster, bf16[4,32,2,3,16,128]{5,4,3,2,1,0:T(8,128)(2,1)S(1)} %copy-done.2, s32[32,256]{1,0:T(8,128)S(1)} %copy-done.4, f32[32,256]{1,0:T(8,128)S(1)} %copy-done.5), custom_call_target="tpu_custom_call" | custom-call | tf_op jit(solution)/shard_map/combine/pallas_call | solution.py:48
  205.0 0.0 copy-start.3
  205.0 0.8 copy-done.3
  205.9 74.3 %send_home.1 = (bf16[24,7168]{1,0:T(8,128)(2,1)}, f32[128,1792]{1,0:T(8,128)}, f32[128,1792]{1,0:T(8,128)}, f32[128,1792]{1,0:T(8,128)}) custom-call(bf16[3,128,768]{2,1,0:T(8,128)(2,1)} %copy-done.3, bf16[768,7168]{1,0:T(8,128)(2,1)} %bitcast.39, bf16[768,7168]{1,0:T(8,128)(2,1)} %bitcast.37, bf16[3,128,7168]{2,1,0:T(8,128)(2,1)} %get-tuple-element.24.bases, ...), custom_call_target="tpu_custom_call" | custom-call | tf_op jit(solution)/shard_map/send_home/pallas_call | solution.py:793
  280.2 0.0 copy-start.10
  280.2 1.0 reduce_sum.48
  281.2 0.8 copy.69
  282.0 1.3 constant_dynamic-slice_fusion
  283.2 0.8 copy.70
  284.0 0.7 reshape.159
  284.8 0.7 fusion.16
  285.5 0.9 select_reduce_fusion
  286.3 0.1 reshape.160
  286.4 0.7 copy.71
  287.1 0.0 copy-done
  287.1 1.9 copy-done.1
  289.0 5.2 %factor_grads.1 = (f32[4,512,512]{2,1,0:T(8,128)}, f32[4,512,512]{2,1,0:T(8,128)}, f32[4,512,512]{2,1,0:T(8,128)}) custom-call(bf16[4,3,512,256]{3,2,1,0:T(8,128)(2,1)S(1)} %copy-done, bf16[4,3,512,256]{3,2,1,0:T(8,128)(2,1)S(1)} %copy-done.1), custom_call_target="tpu_custom_call" | custom-call | tf_op jit(solution)/shard_map/factor_grads/pallas_call | solution.py:329
  294.2 0.0 copy-done.10
  294.2 0.7 copy.78
  294.9 0.0 copy-done.9
  295.0 0.9 copy.79
  295.9 0.0 copy-done.8
  295.9 0.9 copy.80
  296.8 0.0 copy-done.7
  296.8 0.9 copy.81
  (13 shorter events, 0.1 us)
Async XLA Ops:
  4.1 0.6 copy-start.12
  4.2 0.6 copy-start.13
  76.1 8.6 %copy-start.6 = (bf16[3,128,7168]{2,1,0:T(8,128)(2,1)S(1)}, bf16[3,128,7168]{2,1,0:T(8,128)(2,1)}, u32[]{:S(2)}) copy-start(bf16[3,128,7168]{2,1,0:T(8,128)(2,1)} %get-tuple-element.24.bases) | copy-start | bytes 16515076
  84.9 6.9 %copy-start.11 = (f32[32,4,128]{2,1,0:T(4,128)S(1)}, f32[32,4,128]{2,1,0:T(4,128)}, u32[]{:S(2)}) copy-start(f32[32,4,128]{2,1,0:T(4,128)} %get-tuple-element.27) | copy-start | bytes 196612
  93.3 100.5 %copy-start.4 = (s32[32,256]{1,0:T(8,128)S(1)}, s32[32,256]{1,0:T(8,128)}, u32[]{:S(2)}) copy-start(s32[32,256]{1,0:T(8,128)} %add_select_fusion.slots) | copy-start | bytes 98308
  94.1 99.7 %copy-start.5 = (f32[32,256]{1,0:T(8,128)S(1)}, f32[32,256]{1,0:T(8,128)}, u32[]{:S(2)}) copy-start(f32[32,256]{1,0:T(8,128)} %copy.67.weights) | copy-start | bytes 98308
  193.8 1.9 copy-start.2
  205.0 0.8 copy-start.3
  205.9 81.2 %copy-start = (bf16[4,3,512,256]{3,2,1,0:T(8,128)(2,1)S(1)}, bf16[4,3,512,256]{3,2,1,0:T(8,128)(2,1)}, u32[]{:S(2)}) copy-start(bf16[4,3,512,256]{3,2,1,0:T(8,128)(2,1)} %get-tuple-element.35.rows) | copy-start | bytes 9437188
  280.2 14.0 %copy-start.10 = (bf16[24,7168]{1,0:T(8,128)(2,1)S(1)}, bf16[24,7168]{1,0:T(8,128)(2,1)}, u32[]{:S(2)}) copy-start(bf16[24,7168]{1,0:T(8,128)(2,1)} %get-tuple-element.82) | copy-start | bytes 1032196
  287.1 1.9 copy-start.1
  289.0 6.0 %copy-start.9 = (f32[128,1792]{1,0:T(8,128)S(1)}, f32[128,1792]{1,0:T(8,128)}, u32[]{:S(2)}) copy-start(f32[128,1792]{1,0:T(8,128)} %get-tuple-element.32) | copy-start | bytes 2752516
  289.0 6.9 %copy-start.8 = (f32[128,1792]{1,0:T(8,128)S(1)}, f32[128,1792]{1,0:T(8,128)}, u32[]{:S(2)}) copy-start(f32[128,1792]{1,0:T(8,128)} %get-tuple-element.33) | copy-start | bytes 2752516
  289.0 7.8 %copy-start.7 = (f32[128,1792]{1,0:T(8,128)S(1)}, f32[128,1792]{1,0:T(8,128)}, u32[]{:S(2)}) copy-start(f32[128,1792]{1,0:T(8,128)} %get-tuple-element.34) | copy-start | bytes 2752516

commit v4 on v3

--- a/solution.py
+++ b/solution.py
@@ -22,14 +22,12 @@
 
 
 def combine_kernel(cluster, parts, slots, weights, out, total):
-    groups, rank, tokens = parts.shape[1], parts.shape[4], out.shape[2]
+    groups, rank, tokens = parts.shape[0], parts.shape[3], out.shape[2]
     total[...] = jnp.zeros_like(total)
 
     def step(j, carry):
         c = cluster[j]
-        got = parts[0, j].astype(FL)
-        for i in range(1, parts.shape[0]):
-            got = got + parts[i, j].astype(FL)
+        got = parts[j].astype(FL)
         got = jnp.concatenate([got[0], got[1]], axis=2)
         got = jnp.concatenate([got[:2], got[2:] * weights[pl.ds(j, 1), :]], axis=0)
         got = got.astype(BF).reshape(3 * rank, -1)
@@ -37,12 +35,12 @@
         total[:, pl.ds(pl.multiple_of(c * rank, rank), rank), :] += add
         return carry
 
-    lax.fori_loop(0, groups, step, 0)
+    lax.fori_loop(0, groups, step, 0, unroll=4)
     out[...] = total[...].astype(BF)
 
 
 def combine(cluster, parts, slots, weights, clusters, tokens):
-    rank = parts.shape[4]
+    rank = parts.shape[3]
     vmem = pl.BlockSpec(memory_space=pltpu.VMEM)
     shape = (3, clusters * rank, tokens)
     return pl.pallas_call(
@@ -70,32 +68,114 @@
     return [a[:, k : k + 128] for k in range(0, a.shape[1], 128)]
 
 
+def factor_kernel(rows, units, d_gate, d_up, d_down):
+    d_gate[0] = dot(rows[0, 0], units[0, 0], 1, 1)
+    d_up[0] = dot(rows[0, 1], units[0, 1], 1, 1)
+    d_down[0] = dot(units[0, 2], rows[0, 2], 1, 1)
+
+
+def factor_grads(rows, units):
+    count, _, all_rank, lanes = rows.shape
+    held = pl.BlockSpec((1,) + rows.shape[1:], lambda g: (g, 0, 0, 0))
+    one = pl.BlockSpec((1, all_rank, units.shape[2]), lambda g: (g, 0, 0))
+    return pl.pallas_call(
+        factor_kernel,
+        grid=(count,),
+        out_shape=[jax.ShapeDtypeStruct((count, all_rank, units.shape[2]), FL)] * 3,
+        in_specs=[held, held],
+        out_specs=[one] * 3,
+        name="factor_grads",
+        compiler_params=pltpu.CompilerParams(vmem_limit_bytes=40 * MIB),
+    )(rows, units)
+
+
+def plane_place():
+    e = lax.axis_index("expert")
+    return e // 8, (e // 2) % 4, e % 2
+
+
+def slab_of(z, x, core):
+    return core * 16 + z * 4 + x
+
+
+class Copies:
+    def __init__(self, send, recv):
+        self.send, self.recv, self.count, self.sent = send, recv, 0, []
+        self.row = lax.axis_index("dp")
+        self.z, self.x, self.core = plane_place()
+
+    def make(self, src, dst, m, target):
+        return pltpu.make_async_remote_copy(
+            src_ref=src,
+            dst_ref=dst,
+            send_sem=self.send.at[m],
+            recv_sem=self.recv.at[m],
+            device_id=target,
+            device_id_type=pl.DeviceIdType.MESH,
+        )
+
+    def push(self, src, dst, target, land):
+        m = self.count
+        self.count += 1
+        copy = self.make(src, dst, m, target)
+        copy.start()
+        self.sent.append(copy)
+        return self.make(land, land, m, target).wait_recv
+
+    def device(self, dz, dx, flip=False):
+        z, x = (self.z + dz + 4) % 4, (self.x + dx + 4) % 4
+        core = 1 - self.core if flip else self.core
+        return (self.row, (z * 4 + x) * 2 + core)
+
+    def slab(self, dz, dx, flip=False):
+        z, x = (self.z + dz + 4) % 4, (self.x + dx + 4) % 4
+        core = 1 - self.core if flip else self.core
+        return slab_of(z, x, core)
+
+    def row_device(self, dy):
+        e = (self.z * 4 + self.x) * 2 + self.core
+        return ((self.row + dy + 4) % 4, e)
+
+    def finish(self):
+        for copy in self.sent:
+            copy.wait_send()
+
+
+def meet(targets):
+    barrier = pltpu.get_barrier_semaphore()
+    for target in targets:
+        pl.semaphore_signal(
+            barrier, inc=1, device_id=target, device_id_type=pl.DeviceIdType.MESH
+        )
+    pl.semaphore_wait(barrier, len(targets))
+
+
 def middle_kernel(
     member, rows, slots, weights, gate, up, down,
     home, dots, kept_rows, kept_units,
-    picked, landed, parts, factors, row_store, unit_store, route,
-    out_send, out_recv, back_send, back_recv, dot_send, dot_recv, loads, local,
+    picked, landed, parts, factors, row_store, unit_store, far_in, near_in, summed,
+    route, route_in, route_sum,
+    out_send, out_recv, back_send, back_recv, dot_send, dot_recv, ring_send, ring_recv,
+    loads, local,
 ):
+    c = Copies(ring_send, ring_recv)
     row, e = lax.axis_index("dp"), lax.axis_index("expert")
     groups, rank, tokens = picked.shape[0], picked.shape[3], rows.shape[2]
     lanes = picked.shape[4]
-
-    def device(d, r):
-        return ((row + r) % 4, (e + d) % groups)
-
-    def source(d, r):
-        return ((row - r + 4) % 4, (e - d + groups) % groups)
+    all_rank = landed.shape[3]
 
     def everyone(act):
-        for r in range(1, 4):
-            act(0, r)
-
         def step(s, carry):
-            for r in range(4):
-                act((s * 11) % groups, r)
+            act((s * 11) % groups)
             return carry
 
         lax.fori_loop(1, groups, step, 0)
+
+    def device(d):
+        return (row, (e + d) % groups)
+
+    def source(d):
+        return (e - d + groups) % groups
 
     def remote(src, dst, send, recv, target):
         return pltpu.make_async_remote_copy(
@@ -107,56 +187,36 @@
             device_id_type=pl.DeviceIdType.MESH,
         )
 
-    def piece(ref, p, at):
-        sub = pl.ds(pl.multiple_of(at[1] * rank, rank), rank)
-        lane = pl.ds(pl.multiple_of(at[0] * lanes, lanes), lanes)
-        return ref.at[p, :, sub, lane]
-
-    def out_copy(p, d, r):
-        target = device(d, r)
-        n = d * 4 + r
-        return remote(
-            picked.at[target[1], p],
-            piece(landed, p, (row, e)),
-            out_send.at[p, n],
-            out_recv.at[p, n],
-            target,
-        )
-
-    def out_wait(p, d, r):
-        n = d * 4 + r
-        land = piece(landed, p, source(d, r))
-        remote(land, land, out_send.at[p, n], out_recv.at[p, n], device(d, r)).wait_recv()
-
-    def back_copy(p, d, r):
-        target = device(d, r)
-        n = d * 4 + r
-        return remote(
-            piece(parts, p, target),
-            home.at[row, e, p],
-            back_send.at[p, n],
-            back_recv.at[p, n],
-            target,
-        )
-
-    def back_wait(p, d, r):
-        n = d * 4 + r
-        at = source(d, r)
-        land = home.at[at[0], at[1], p]
-        remote(land, land, back_send.at[p, n], back_recv.at[p, n], device(d, r)).wait_recv()
-
-    def dot_copy(d, r):
-        target = device(d, r)
-        n = d * 4 + r
-        return remote(
-            route.at[target[0]], dots.at[row, e], dot_send.at[n], dot_recv.at[n], target
-        )
-
-    def dot_wait(d, r):
-        n = d * 4 + r
-        at = source(d, r)
-        land = dots.at[at[0], at[1]]
-        remote(land, land, dot_send.at[n], dot_recv.at[n], device(d, r)).wait_recv()
+    def ranks(at):
+        return pl.ds(pl.multiple_of(at * rank, rank), rank)
+
+    def out_copy(p, d):
+        target = device(d)
+        dst = landed.at[p, row, :, ranks(e)]
+        return remote(picked.at[target[1], p], dst, out_send.at[p, d], out_recv.at[p, d], target)
+
+    def out_wait(p, d):
+        land = landed.at[p, row, :, ranks(source(d))]
+        remote(land, land, out_send.at[p, d], out_recv.at[p, d], device(d)).wait_recv()
+
+    def back_copy(p, d):
+        target = device(d)
+        src = summed.at[p, :, ranks(target[1])]
+        return remote(src, home.at[e, p], back_send.at[p, d], back_recv.at[p, d], target)
+
+    def back_wait(p, d):
+        land = home.at[source(d), p]
+        remote(land, land, back_send.at[p, d], back_recv.at[p, d], device(d)).wait_recv()
+
+    def dot_copy(d):
+        return remote(route_sum, dots.at[e], dot_send.at[d], dot_recv.at[d], device(d))
+
+    def dot_wait(d):
+        land = dots.at[source(d)]
+        remote(land, land, dot_send.at[d], dot_recv.at[d], device(d)).wait_recv()
+
+    def at_row(dy):
+        return (row + dy + 4) % 4
 
     incoming = [
         pltpu.make_async_copy(ref, factors.at[k], loads.at[k])
@@ -166,18 +226,20 @@
         copy.start()
     barrier = pltpu.get_barrier_semaphore()
 
-    def greet(d, r):
+    def greet(target):
         pl.semaphore_signal(
-            barrier, inc=1, device_id=device(d, r), device_id_type=pl.DeviceIdType.MESH
+            barrier, inc=1, device_id=target, device_id_type=pl.DeviceIdType.MESH
         )
 
-    everyone(greet)
+    everyone(lambda d: greet(device(d)))
+    for dy in (1, -1, 2):
+        greet(c.row_device(dy))
 
     def pick_for(j):
         own = jnp.zeros((3, rank, tokens), BF)
-        for c in range(member.shape[1]):
-            share = member[pl.ds(j, 1), c : c + 1].astype(BF)[None]
-            own = own + rows[:, c * rank : (c + 1) * rank, :] * share
+        for k in range(member.shape[1]):
+            share = member[pl.ds(j, 1), k : k + 1].astype(BF)[None]
+            own = own + rows[:, k * rank : (k + 1) * rank, :] * share
         got = dot(own.reshape(3 * rank, tokens), one_hot(slots, j, tokens), 1, 0)
         got = got.reshape(3, rank, -1)
         got = jnp.concatenate([got[:2], got[2:] * weights[pl.ds(j, 1), :]], axis=0).astype(BF)
@@ -186,32 +248,55 @@
 
     pick_for(e)
     own_copies = [
-        pltpu.make_async_copy(picked.at[e, p], piece(landed, p, (row, e)), local.at[p])
+        pltpu.make_async_copy(picked.at[e, p], landed.at[p, row, :, ranks(e)], local.at[p])
         for p in range(2)
     ]
     for copy in own_copies:
         copy.start()
-    pl.semaphore_wait(barrier, 4 * groups - 1)
-    for r in range(1, 4):
-        out_copy(0, 0, r).start()
-
-    def pick_step(s, carry):
-        d = (s * 11) % groups
-        pick_for((e + d) % groups)
-        for r in range(4):
-            out_copy(0, d, r).start()
+    pl.semaphore_wait(barrier, groups + 2)
+
+    def pick_some(at):
+        for s in at:
+            pick_for((e + (s * 11) % groups) % groups)
+        for s in at:
+            out_copy(0, (s * 11) % groups).start()
+
+    pick_some((1, 2, 3))
+
+    def pick_step(n, carry):
+        pick_some([4 * n + u for u in range(4)])
         return carry
 
-    lax.fori_loop(1, groups, pick_step, 0)
-    everyone(lambda d, r: out_copy(1, d, r).start())
+    lax.fori_loop(1, groups // 4, pick_step, 0)
+    everyone(lambda d: out_copy(1, d).start())
     for copy in incoming:
         copy.wait()
     for copy in own_copies:
         copy.wait()
-    stores = []
+    low, high = pl.ds(0, all_rank // 2), pl.ds(all_rank // 2, all_rank // 2)
+    gathers, fars = [], []
     for p in range(2):
-        everyone(lambda d, r: out_wait(p, d, r))
-        wide = [mix(split_tiles(landed[p, k])) for k in range(3)]
+        everyone(lambda d: out_wait(p, d))
+        own = landed.at[p, row]
+        gathers.append(
+            (
+                c.push(own, own, c.row_device(1), landed.at[p, at_row(-1)]),
+                c.push(own, own, c.row_device(-1), landed.at[p, at_row(1)]),
+            )
+        )
+    for p in range(2):
+        gathers[p][0]()
+        ref = landed.at[p, at_row(-1), :, low]
+        far = [c.push(ref, ref, c.row_device(1), landed.at[p, at_row(2), :, low])]
+        gathers[p][1]()
+        ref = landed.at[p, at_row(1), :, high]
+        far.append(c.push(ref, ref, c.row_device(-1), landed.at[p, at_row(2), :, high]))
+        fars.append(far)
+    stores, far_waits, near_waits = [], [], []
+    for p in range(2):
+        for wait in fars[p]:
+            wait()
+        wide = [mix([landed[p, i, k] for i in range(4)]) for k in range(3)]
         results = []
         for n in range(2):
             hg, hu, gm = wide[0][n], wide[1][n], wide[2][n]
@@ -246,30 +331,74 @@
                 h = a.shape[-1] // 2
                 tiles.append(jnp.concatenate([a[:, :h], b[:, :h]], axis=1))
                 tiles.append(jnp.concatenate([a[:, h:], b[:, h:]], axis=1))
-            parts[p, k] = jnp.concatenate(tiles, axis=1)
-        everyone(lambda d, r: back_copy(p, d, r).start())
+            for i in range(4):
+                parts[p, i, k] = tiles[i]
+        ahead, behind = c.row_device(1), c.row_device(-1)
+        far = parts.at[p, at_row(2)]
+        far_waits.append(
+            (
+                c.push(far.at[:, low], far_in.at[p, 0], ahead, far_in.at[p, 0]),
+                c.push(far.at[:, high], far_in.at[p, 1], behind, far_in.at[p, 1]),
+            )
+        )
+        land = (near_in.at[p, 0, :, high], near_in.at[p, 1, :, low])
+        near_waits.append(
+            [
+                c.push(parts.at[p, at_row(1), :, high], land[0], ahead, land[0]),
+                c.push(parts.at[p, at_row(-1), :, low], land[1], behind, land[1]),
+            ]
+        )
         pair = pl.ds(2 * p, 2)
         here = [
-            pltpu.make_async_copy(piece(parts, p, (row, e)), home.at[row, e, p], local.at[2 + p]),
-            pltpu.make_async_copy(row_store.at[pair], kept_rows.at[pair], local.at[4 + p]),
-            pltpu.make_async_copy(unit_store.at[pair], kept_units.at[pair], local.at[6 + p]),
+            pltpu.make_async_copy(row_store.at[pair], kept_rows.at[pair], local.at[2 + p]),
+            pltpu.make_async_copy(unit_store.at[pair], kept_units.at[pair], local.at[4 + p]),
         ]
         for copy in here:
             copy.start()
         stores += here
-    everyone(lambda d, r: dot_copy(d, r).start())
-    own_dots = pltpu.make_async_copy(route.at[row], dots.at[row, e], local.at[8])
-    own_dots.start()
-    stores.append(own_dots)
+    route_waits = []
+    for n, dy in enumerate((1, -1, 2)):
+        land = route_in.at[n]
+        route_waits.append(c.push(route.at[at_row(dy)], land, c.row_device(dy), land))
     for p in range(2):
-        everyone(lambda d, r: back_wait(p, d, r))
+        for side, dy, half in ((0, 1, low), (1, -1, high)):
+            far_waits[p][side]()
+            to = at_row(dy)
+            more = parts[p, to, :, half].astype(FL) + far_in[p, side].astype(FL)
+            parts[p, to, :, half] = more.astype(BF)
+            land = near_in.at[p, side, :, half]
+            near_waits[p].append(
+                c.push(parts.at[p, to, :, half], land, c.row_device(dy), land)
+            )
+    for wait in route_waits:
+        wait()
+    route_sum[...] = route[row] + route_in[0] + route_in[1] + route_in[2]
+    everyone(lambda d: dot_copy(d).start())
+    for p in range(2):
+        for wait in near_waits[p]:
+            wait()
+        total = parts[p, row].astype(FL) + near_in[p, 0].astype(FL) + near_in[p, 1].astype(FL)
+        summed[p] = total.astype(BF)
+        everyone(lambda d: back_copy(p, d).start())
+        own = pltpu.make_async_copy(summed.at[p, :, ranks(e)], home.at[e, p], local.at[6 + p])
+        own.start()
+        stores.append(own)
+    own = pltpu.make_async_copy(route_sum, dots.at[e], local.at[8])
+    own.start()
+    stores.append(own)
     everyone(dot_wait)
+    for p in range(2):
+        everyone(lambda d: back_wait(p, d))
     for copy in stores:
         copy.wait()
     for p in range(2):
-        everyone(lambda d, r: out_copy(p, d, r).wait_send())
-        everyone(lambda d, r: back_copy(p, d, r).wait_send())
-    everyone(lambda d, r: dot_copy(d, r).wait_send())
+        everyone(lambda d: out_copy(p, d).wait_send())
+        everyone(lambda d: back_copy(p, d).wait_send())
+    everyone(lambda d: dot_copy(d).wait_send())
+    c.finish()
+
+
+RING_COPIES = 2 * 4 + 2 * 6 + 3
 
 
 def middle(member, rows, slots, weights, gate, up, down, n_dp):
@@ -285,8 +414,8 @@
     return pl.pallas_call(
         middle_kernel,
         out_shape=[
-            jax.ShapeDtypeStruct((n_dp, groups, 2, 3, rank, half), BF),
-            jax.ShapeDtypeStruct((n_dp, groups, 2, half), FL),
+            jax.ShapeDtypeStruct((groups, 2, 3, rank, half), BF),
+            jax.ShapeDtypeStruct((groups, 2, half), FL),
             kept,
             kept,
         ],
@@ -294,18 +423,25 @@
         out_specs=[anywhere] * 4,
         scratch_shapes=[
             pltpu.VMEM((groups, 2, 3, rank, half), BF),
-            pltpu.VMEM((2, 3, all_rank, n_dp * half), BF),
-            pltpu.VMEM((2, 3, all_rank, n_dp * half), BF),
+            pltpu.VMEM((2, n_dp, 3, all_rank, half), BF),
+            pltpu.VMEM((2, n_dp, 3, all_rank, half), BF),
             pltpu.VMEM((3,) + gate.shape, BF),
             pltpu.VMEM(kept.shape, BF),
             pltpu.VMEM(kept.shape, BF),
+            pltpu.VMEM((2, 2, 3, all_rank // 2, half), BF),
+            pltpu.VMEM((2, 2, 3, all_rank, half), BF),
+            pltpu.VMEM((2, 3, all_rank, half), BF),
             pltpu.VMEM((n_dp, 2, half), FL),
-            dma((2, n_dp * groups)),
-            dma((2, n_dp * groups)),
-            dma((2, n_dp * groups)),
-            dma((2, n_dp * groups)),
-            dma((n_dp * groups,)),
-            dma((n_dp * groups,)),
+            pltpu.VMEM((3, 2, half), FL),
+            pltpu.VMEM((2, half), FL),
+            dma((2, groups)),
+            dma((2, groups)),
+            dma((2, groups)),
+            dma((2, groups)),
+            dma((groups,)),
+            dma((groups,)),
+            dma((RING_COPIES,)),
+            dma((RING_COPIES,)),
             dma((3,)),
             dma((9,)),
         ],
@@ -314,88 +450,6 @@
             collective_id=2, has_side_effects=True, vmem_limit_bytes=56 * MIB
         ),
     )(member, rows, slots, weights, gate, up, down)
-
-
-def factor_kernel(rows, units, d_gate, d_up, d_down):
-    d_gate[0] = dot(rows[0, 0], units[0, 0], 1, 1)
-    d_up[0] = dot(rows[0, 1], units[0, 1], 1, 1)
-    d_down[0] = dot(units[0, 2], rows[0, 2], 1, 1)
-
-
-def factor_grads(rows, units):
-    count, _, all_rank, lanes = rows.shape
-    held = pl.BlockSpec((1,) + rows.shape[1:], lambda g: (g, 0, 0, 0))
-    one = pl.BlockSpec((1, all_rank, units.shape[2]), lambda g: (g, 0, 0))
-    return pl.pallas_call(
-        factor_kernel,
-        grid=(count,),
-        out_shape=[jax.ShapeDtypeStruct((count, all_rank, units.shape[2]), FL)] * 3,
-        in_specs=[held, held],
-        out_specs=[one] * 3,
-        name="factor_grads",
-        compiler_params=pltpu.CompilerParams(vmem_limit_bytes=40 * MIB),
-    )(rows, units)
-
-
-def plane_place():
-    e = lax.axis_index("expert")
-    return e // 8, (e // 2) % 4, e % 2
-
-
-def slab_of(z, x, core):
-    return core * 16 + z * 4 + x
-
-
-class Copies:
-    def __init__(self, send, recv):
-        self.send, self.recv, self.count, self.sent = send, recv, 0, []
-        self.row = lax.axis_index("dp")
-        self.z, self.x, self.core = plane_place()
-
-    def make(self, src, dst, m, target):
-        return pltpu.make_async_remote_copy(
-            src_ref=src,
-            dst_ref=dst,
-            send_sem=self.send.at[m],
-            recv_sem=self.recv.at[m],
-            device_id=target,
-            device_id_type=pl.DeviceIdType.MESH,
-        )
-
-    def push(self, src, dst, target, land):
-        m = self.count
-        self.count += 1
-        copy = self.make(src, dst, m, target)
-        copy.start()
-        self.sent.append(copy)
-        return self.make(land, land, m, target).wait_recv
-
-    def device(self, dz, dx, flip=False):
-        z, x = (self.z + dz + 4) % 4, (self.x + dx + 4) % 4
-        core = 1 - self.core if flip else self.core
-        return (self.row, (z * 4 + x) * 2 + core)
-
-    def slab(self, dz, dx, flip=False):
-        z, x = (self.z + dz + 4) % 4, (self.x + dx + 4) % 4
-        core = 1 - self.core if flip else self.core
-        return slab_of(z, x, core)
-
-    def row_device(self, dy):
-        e = (self.z * 4 + self.x) * 2 + self.core
-        return ((self.row + dy + 4) % 4, e)
-
-    def finish(self):
-        for copy in self.sent:
-            copy.wait_send()
-
-
-def meet(targets):
-    barrier = pltpu.get_barrier_semaphore()
-    for target in targets:
-        pl.semaphore_signal(
-            barrier, inc=1, device_id=target, device_id_type=pl.DeviceIdType.MESH
-        )
-    pl.semaphore_wait(barrier, len(targets))
 
 
 OFFSETS = (0, -1, 1, 2)
@@ -615,7 +669,7 @@
 def home_kernel(
     rows, x, dy, bases, other,
     out, d_gate, d_up, d_down,
-    paired, xb, db, bb, terms, far_in, near_in, turned, full, got, passed, kept, last,
+    paired, xb, db, bb, terms, far_in, near_in, turned, full, got, skipped, passed, kept, last,
     send, recv, loads,
 ):
     c = Copies(send, recv)
@@ -701,7 +755,42 @@
             turned[:, at] = source[k, :, mine].astype(FL).T.astype(BF)
     tok = full.shape[2]
     place = (c.z, c.x)
-    got_waits = [[], []]
+    got_waits = [{}, {}]
+    cross_waits = []
+    via_ahead, via_behind = (1, -1), (2, 0)
+
+    def group(h, d, b):
+        if h == 0:
+            return ((c.z + b + 4) % 4) * 4 + (c.x + d + 4) % 4
+        return ((c.z + d + 4) % 4) * 4 + (c.x + b + 4) % 4
+
+    def along(h, d):
+        return c.device(0, d) if h == 0 else c.device(d, 0)
+
+    def cross_far(h):
+        waits = []
+        for d, which in ((1, via_ahead), (-1, via_behind)):
+            for k, b in enumerate(which):
+                land = skipped.at[h, d % 3 - 1, k]
+                waits.append((d, b, k, c.push(full.at[h, group(h, 2, b)], land, along(h, d), land)))
+        for d, which in ((1, via_behind), (-1, via_ahead)):
+            for b in which:
+                cross_push(h, d, b)
+        return waits
+
+    def cross_push(h, d, b):
+        land = got.at[h, d % 3 - 1, b % 4]
+        wait = c.push(full.at[h, group(h, d, b)], land, along(h, d), land)
+        got_waits[h].setdefault(b, []).append(wait)
+
+    def cross_near(h):
+        for d, b, k, wait in cross_waits[h]:
+            wait()
+            slab = group(h, d, b)
+            more = full[h, slab].astype(FL) + skipped[h, d % 3 - 1, k].astype(FL)
+            full[h, slab] = more.astype(BF)
+            cross_push(h, d, b)
+
     for n in range(4):
         for copy in basis_flying[n]:
             copy.wait()
@@ -722,18 +811,9 @@
         if n < 2:
             basis_flying.append(load_bases(n + 2))
         if n % 2 == 1:
-            for b in (1, -1, 2, 0):
-                waits = []
-                for di, d in enumerate(near):
-                    if h == 0:
-                        slab = ((c.z + b + 4) % 4) * 4 + (c.x + d + 4) % 4
-                        target = c.device(0, d)
-                    else:
-                        slab = ((c.z + d + 4) % 4) * 4 + (c.x + b + 4) % 4
-                        target = c.device(d, 0)
-                    land = got.at[h, di, b % 4]
-                    waits.append(c.push(full.at[h, slab], land, target, land))
-                got_waits[h].append((b, waits))
+            cross_waits.append(cross_far(h))
+    for h in range(2):
+        cross_near(h)
     for k in range(3):
         far_waits[0][k]()
         terms[1, k, low] = (terms[1, k, low].astype(FL) + far_in[0, k].astype(FL)).astype(BF)
@@ -744,20 +824,15 @@
         land = near_in.at[1, k, high]
         near_waits[1].append(c.push(terms.at[2, k, high], land, c.row_device(-1), land))
     last_waits = [[], []]
-    for step in range(4):
+    for step, b in enumerate((1, -1, 2, 0)):
         for h in range(2):
-            b, waits = got_waits[h][step]
-            for wait in waits:
+            for wait in got_waits[h][b]:
                 wait()
-            if h == 0:
-                slab = ((c.z + b + 4) % 4) * 4 + c.x
-                target = c.device(b, 0)
-            else:
-                slab = c.z * 4 + (c.x + b + 4) % 4
-                target = c.device(0, b)
+            slab = group(h, 0, b)
+            target = c.device(b, 0) if h == 0 else c.device(0, b)
             total = full[h, slab].astype(FL)
-            for di in range(3):
-                total = total + got[h, di, b % 4].astype(FL)
+            for side in range(2):
+                total = total + got[h, side, b % 4].astype(FL)
             if b == 0:
                 kept[h] = total
             else:
@@ -805,7 +880,8 @@
             pltpu.VMEM((2, kinds, ranks, width), BF),
             pltpu.VMEM((tokens // 2, 4 * ranks), BF),
             pltpu.VMEM((2, 16, tok, half), BF),
-            pltpu.VMEM((2, 3, 4, tok, half), BF),
+            pltpu.VMEM((2, 2, 4, tok, half), BF),
+            pltpu.VMEM((2, 2, 2, tok, half), BF),
             pltpu.VMEM((2, 3, tok, half), BF),
             pltpu.VMEM((2, tok, half), FL),
             pltpu.VMEM((2, 3, tok, half), BF),
@@ -893,7 +969,7 @@
     summed = combine(cluster, home, slots, weights, clusters, plane_tokens)
 
     z, x, core = plane_place()
-    dots = jnp.sum(dots, axis=0).reshape(n_ex, local, n_ex, 2)
+    dots = dots.reshape(n_ex, local, n_ex, 2)
     scores = lax.dynamic_index_in_dim(dots, slab_of(z, x, core), 2, False).reshape(cells)
     scores = scores / jnp.where(cell_weight > 0.0, cell_weight, 1.0)
     grad_route = jnp.sum(jnp.where(placed, scores[None, :], 0.0), axis=1).reshape(route_ids.shape)

time: 298 us -> 259 us (0.87)
  Pallas kernels: 259 us -> 222 us
    pallas_call x1, Pallas kernels: 99.7 us -> 81.7 us  [middle(): pl.pallas_call(middle_kernel, out_shape=[jax.ShapeDtypeStruct((groups, 2,...]
    pallas_call x1, Pallas kernels: 74.3 us -> 59 us  [send_home(): pl.pallas_call(home_kernel, out_shape=[jax.ShapeDtypeStruct((tok, full_wi...]
    pallas_call x1, Pallas kernels: 9.37 us -> 5.36 us  [combine(): pl.pallas_call(combine_kernel, out_shape=jax.ShapeDtypeStruct(shape, BF),...]
    unnamed x34 -> x36, local copies, waits for them, and re-layouts: 9.98 us -> 9.23 us
where the time goes in v4:
time: 259 us
  Pallas kernels  222 us (86%)
  local copies, waits for them, and re-layouts  16.4 us (6%)
  matrix products  14.6 us (6%)
  other arithmetic  4.85 us (2%)
    pallas_call x1, Pallas kernels, middle(): pl.pallas_call(middle_kernel, out_shape=[jax.ShapeDtypeStruct((groups, 2,...  81.7 us
    pallas_call x1, Pallas kernels, gather_inputs(): pl.pallas_call(gather_kernel, out_shape=[slabs, slabs, jax.ShapeDtypeStru...  70.7 us
    pallas_call x1, Pallas kernels, send_home(): pl.pallas_call(home_kernel, out_shape=[jax.ShapeDtypeStruct((tok, full_wi...  59 us
    dot_general x2, matrix products, dot(): lax.dot_general(a, b, (((ca,), (cb,)), ((), ())), preferred_element_type=FL)  14.6 us
    unnamed x36, local copies, waits for them, and re-layouts  9.23 us
    pallas_call x1, Pallas kernels, combine(): pl.pallas_call(combine_kernel, out_shape=jax.ShapeDtypeStruct(shape, BF),...  5.36 us
    pallas_call x1, Pallas kernels, factor_grads(): pl.pallas_call(factor_kernel, grid=(count,), out_shape=[jax.ShapeDtypeStr...  5.23 us

profile of v4, /device:TPU:0, one launch (start us, length us, event | category | flops | bytes accessed | tf_op | source)
XLA Modules:
  0.0 258.6 jit_solution(7822044483599403812)
XLA Ops:
  0.6 0.7 reshape.148
  1.4 0.1 slice_reduce_fusion.cluster
  1.5 0.7 fusion.12.member
  2.2 0.8 copy.47
  2.9 0.1 reshape.164
  3.0 0.8 copy.46
  3.8 0.1 reshape.152
  3.9 0.2 convert_reduce_fusion
  4.1 0.0 copy-start.13
  4.1 0.1 select_reduce_fusion.1
  4.2 0.0 copy-start.14
  4.2 0.4 copy-done.13
  4.7 0.1 select_reduce_fusion.2
  4.8 0.0 copy-done.14
  4.8 0.6 pad_maximum_fusion.1.table
  5.4 70.7 %gather_inputs.1 = (bf16[32,24,7168]{2,1,0:T(8,128)(2,1)}, bf16[32,24,7168]{2,1,0:T(8,128)(2,1)}, f32[32,4,128]{2,1,0:T(4,128)}, bf16[3,128,7168]{2,1,0:T(8,128)(2,1)}, bf16[2,128,7168]{2,1,0:T(8,128)(2,1)}) custom-call(bf16[24,7168]{1,0:T(8,128)(2,1)} %x.1, bf16[24,7168]{1,0:T(8,128)(2,1)} %dy.1, bf16[128,1792]{1,0:T(8,128)(2,1)} %bitcast.50, ...), custom_call_target="tpu_custom_call" | custom-call | tf_op jit(solution)/shard_map/gather_inputs/pallas_call | solution.py:648
  76.1 0.0 copy-start.6
  76.1 8.5 %fusion.6 = bf16[1,128,768]{2,1,0:T(8,128)(2,1)S(1)} fusion(bf16[768,7168]{1,0:T(8,128)(2,1)} %bitcast.36, bf16[3,128,7168]{2,1,0:T(8,128)(2,1)} %get-tuple-element.24.bases), kind=kOutput, calls=%fused_computation.5 | convolution fusion | flops 1409384448 | bytes 13041664 | tf_op jit(solution)/shard_map/dot_general | solution.py:14
  84.6 0.0 copy-done.6
  84.6 0.2 slice.18
  84.9 0.0 copy-start.11
  84.9 6.1 %convolution_convert_fusion = bf16[256,768]{1,0:T(8,128)(2,1)S(1)} fusion(bf16[256,7168]{1,0:T(8,128)(2,1)S(1)} %bitcast.40, bf16[768,7168]{1,0:T(8,128)(2,1)} %bitcast.38), kind=kOutput, calls=%fused_computation.3 | convolution fusion | flops 2818768896 | bytes 15073280 | tf_op jit(solution)/shard_map/dot_general | solution.py:14
  90.9 0.9 pad_maximum_fusion.rows
  91.8 0.0 copy-done.11
  91.8 0.1 copy.48
  92.0 0.1 copy.61
  92.0 0.2 copy.50
  92.2 0.1 gt.21
  92.3 0.1 copy.53
  92.4 0.1 copy.51
  92.5 0.1 copy.52
  92.6 0.6 add_select_fusion.slots
  93.3 0.1 copy.54
  93.4 0.7 copy.55.weights
  94.1 81.7 %middle.1 = (bf16[32,2,3,16,128]{4,3,2,1,0:T(8,128)(2,1)}, f32[32,2,128]{2,1,0:T(2,128)}, bf16[4,3,512,256]{3,2,1,0:T(8,128)(2,1)}, bf16[4,3,512,256]{3,2,1,0:T(8,128)(2,1)}) custom-call(f32[32,8]{1,0:T(8,128)} %fusion.12.member, bf16[3,128,768]{2,1,0:T(8,128)(2,1)} %pad_maximum_fusion.rows, s32[32,256]{1,0:T(8,128)} %add_select_fusion.slots, ...), custom_call_target="tpu_custom_call" | custom-call | tf_op jit(solution)/shard_map/middle/pallas_call | solution.py:414
  175.8 0.0 copy-done.4
  175.8 0.0 copy-done.5
  175.8 0.0 copy-start.3
  175.8 1.1 copy-done.3
  176.9 5.4 %combine.1.rows = bf16[3,128,768]{2,1,0:T(8,128)(2,1)S(1)} custom-call(s32[32]{0:T(128)S(1)} %slice_reduce_fusion.cluster, bf16[32,2,3,16,128]{4,3,2,1,0:T(8,128)(2,1)S(1)} %copy-done.3, s32[32,256]{1,0:T(8,128)S(1)} %copy-done.4, f32[32,256]{1,0:T(8,128)S(1)} %copy-done.5), custom_call_target="tpu_custom_call" | custom-call | tf_op jit(solution)/shard_map/combine/pallas_call | solution.py:46
  182.3 0.0 copy-start.2
  182.3 0.8 copy-done.2
  183.1 59.0 %send_home.1 = (bf16[24,7168]{1,0:T(8,128)(2,1)}, f32[128,1792]{1,0:T(8,128)}, f32[128,1792]{1,0:T(8,128)}, f32[128,1792]{1,0:T(8,128)}) custom-call(bf16[3,128,768]{2,1,0:T(8,128)(2,1)} %copy-done.2, bf16[768,7168]{1,0:T(8,128)(2,1)} %bitcast.39, bf16[768,7168]{1,0:T(8,128)(2,1)} %bitcast.37, bf16[3,128,7168]{2,1,0:T(8,128)(2,1)} %get-tuple-element.24.bases, ...), custom_call_target="tpu_custom_call" | custom-call | tf_op jit(solution)/shard_map/send_home/pallas_call | solution.py:868
  242.1 0.0 copy-start.10
  242.1 0.0 copy-done.12
  242.1 0.8 copy.57
  242.9 1.3 constant_dynamic-slice_fusion
  244.1 0.8 copy.58
  244.9 0.7 reshape.159
  245.6 0.7 fusion.16
  246.3 0.9 select_reduce_fusion
  247.2 0.1 reshape.160
  247.3 0.7 copy.59
  248.0 0.0 copy-done
  248.0 1.9 copy-done.1
  249.9 5.2 %factor_grads.1 = (f32[4,512,512]{2,1,0:T(8,128)}, f32[4,512,512]{2,1,0:T(8,128)}, f32[4,512,512]{2,1,0:T(8,128)}) custom-call(bf16[4,3,512,256]{3,2,1,0:T(8,128)(2,1)S(1)} %copy-done, bf16[4,3,512,256]{3,2,1,0:T(8,128)(2,1)S(1)} %copy-done.1), custom_call_target="tpu_custom_call" | custom-call | tf_op jit(solution)/shard_map/factor_grads/pallas_call | solution.py:81
  255.1 0.0 copy-done.10
  255.1 0.7 copy.66
  255.8 0.0 copy-done.9
  255.8 0.9 copy.67
  256.8 0.0 copy-done.8
  256.8 0.9 copy.68
  257.7 0.0 copy-done.7
  257.7 0.9 copy.69
  (14 shorter events, 0.1 us)
Async XLA Ops:
  4.1 0.6 copy-start.13
  4.2 0.6 copy-start.14
  76.1 8.6 %copy-start.6 = (bf16[3,128,7168]{2,1,0:T(8,128)(2,1)S(1)}, bf16[3,128,7168]{2,1,0:T(8,128)(2,1)}, u32[]{:S(2)}) copy-start(bf16[3,128,7168]{2,1,0:T(8,128)(2,1)} %get-tuple-element.24.bases) | copy-start | bytes 16515076
  84.9 6.9 %copy-start.11 = (f32[32,4,128]{2,1,0:T(4,128)S(1)}, f32[32,4,128]{2,1,0:T(4,128)}, u32[]{:S(2)}) copy-start(f32[32,4,128]{2,1,0:T(4,128)} %get-tuple-element.27) | copy-start | bytes 196612
  93.3 82.5 %copy-start.4 = (s32[32,256]{1,0:T(8,128)S(1)}, s32[32,256]{1,0:T(8,128)}, u32[]{:S(2)}) copy-start(s32[32,256]{1,0:T(8,128)} %add_select_fusion.slots) | copy-start | bytes 98308
  94.1 81.7 %copy-start.5 = (f32[32,256]{1,0:T(8,128)S(1)}, f32[32,256]{1,0:T(8,128)}, u32[]{:S(2)}) copy-start(f32[32,256]{1,0:T(8,128)} %copy.55.weights) | copy-start | bytes 98308
  175.8 1.1 copy-start.3
  182.3 0.8 copy-start.2
  183.1 59.0 %copy-start.12 = (f32[32,2,128]{2,1,0:T(2,128)S(1)}, f32[32,2,128]{2,1,0:T(2,128)}, u32[]{:S(2)}) copy-start(f32[32,2,128]{2,1,0:T(2,128)} %get-tuple-element.31) | copy-start | bytes 98308
  183.1 64.9 %copy-start = (bf16[4,3,512,256]{3,2,1,0:T(8,128)(2,1)S(1)}, bf16[4,3,512,256]{3,2,1,0:T(8,128)(2,1)}, u32[]{:S(2)}) copy-start(bf16[4,3,512,256]{3,2,1,0:T(8,128)(2,1)} %get-tuple-element.35.rows) | copy-start | bytes 9437188
  242.1 13.0 %copy-start.10 = (bf16[24,7168]{1,0:T(8,128)(2,1)S(1)}, bf16[24,7168]{1,0:T(8,128)(2,1)}, u32[]{:S(2)}) copy-start(bf16[24,7168]{1,0:T(8,128)(2,1)} %get-tuple-element.74) | copy-start | bytes 1032196
  248.0 1.9 copy-start.1
  249.9 6.0 %copy-start.9 = (f32[128,1792]{1,0:T(8,128)S(1)}, f32[128,1792]{1,0:T(8,128)}, u32[]{:S(2)}) copy-start(f32[128,1792]{1,0:T(8,128)} %get-tuple-element.32) | copy-start | bytes 2752516
  249.9 6.9 %copy-start.8 = (f32[128,1792]{1,0:T(8,128)S(1)}, f32[128,1792]{1,0:T(8,128)}, u32[]{:S(2)}) copy-start(f32[128,1792]{1,0:T(8,128)} %get-tuple-element.33) | copy-start | bytes 2752516
  249.9 7.8 %copy-start.7 = (f32[128,1792]{1,0:T(8,128)S(1)}, f32[128,1792]{1,0:T(8,128)}, u32[]{:S(2)}) copy-start(f32[128,1792]{1,0:T(8,128)} %get-tuple-element.34) | copy-start | bytes 2752516

commit v5 on v4

--- a/solution.py
+++ b/solution.py
@@ -50,7 +50,7 @@
         out_specs=vmem,
         scratch_shapes=[pltpu.VMEM(shape, FL)],
         name="combine",
-        compiler_params=pltpu.CompilerParams(vmem_limit_bytes=40 * MIB),
+        compiler_params=pltpu.CompilerParams(vmem_limit_bytes=60 * MIB),
     )(cluster, parts, slots, weights)
 
 
@@ -68,25 +68,33 @@
     return [a[:, k : k + 128] for k in range(0, a.shape[1], 128)]
 
 
-def factor_kernel(rows, units, d_gate, d_up, d_down):
+def factor_kernel(rows, units, *refs):
+    sources, (d_gate, d_up, d_down), results = refs[:4], refs[4:7], refs[7:]
     d_gate[0] = dot(rows[0, 0], units[0, 0], 1, 1)
     d_up[0] = dot(rows[0, 1], units[0, 1], 1, 1)
     d_down[0] = dot(units[0, 2], rows[0, 2], 1, 1)
-
-
-def factor_grads(rows, units):
+    for source, result in zip(sources, results):
+        result[...] = source[...]
+
+
+def factor_grads(rows, units, passing):
     count, _, all_rank, lanes = rows.shape
     held = pl.BlockSpec((1,) + rows.shape[1:], lambda g: (g, 0, 0, 0))
     one = pl.BlockSpec((1, all_rank, units.shape[2]), lambda g: (g, 0, 0))
+    tok, width = passing[0].shape
+    ranks, part = passing[1].shape
+    passed = [pl.BlockSpec((tok, width // count), lambda g: (0, g))]
+    passed += [pl.BlockSpec((ranks // count, part), lambda g: (g, 0))] * 3
+    factor = jax.ShapeDtypeStruct((count, all_rank, units.shape[2]), FL)
     return pl.pallas_call(
         factor_kernel,
         grid=(count,),
-        out_shape=[jax.ShapeDtypeStruct((count, all_rank, units.shape[2]), FL)] * 3,
-        in_specs=[held, held],
-        out_specs=[one] * 3,
+        out_shape=[factor] * 3 + [jax.ShapeDtypeStruct(a.shape, a.dtype) for a in passing],
+        in_specs=[held, held] + passed,
+        out_specs=[one] * 3 + passed,
         name="factor_grads",
-        compiler_params=pltpu.CompilerParams(vmem_limit_bytes=40 * MIB),
-    )(rows, units)
+        compiler_params=pltpu.CompilerParams(vmem_limit_bytes=60 * MIB),
+    )(rows, units, *passing)
 
 
 def plane_place():
@@ -153,7 +161,7 @@
 def middle_kernel(
     member, rows, slots, weights, gate, up, down,
     home, dots, kept_rows, kept_units,
-    picked, landed, parts, factors, row_store, unit_store, far_in, near_in, summed,
+    picked, chosen, landed, parts, factors, row_store, unit_store, far_in, near_in, summed,
     route, route_in, route_sum,
     out_send, out_recv, back_send, back_recv, dot_send, dot_recv, ring_send, ring_recv,
     loads, local,
@@ -235,18 +243,24 @@
     for dy in (1, -1, 2):
         greet(c.row_device(dy))
 
-    def pick_for(j):
+    def own_for(j):
         own = jnp.zeros((3, rank, tokens), BF)
         for k in range(member.shape[1]):
             share = member[pl.ds(j, 1), k : k + 1].astype(BF)[None]
             own = own + rows[:, k * rank : (k + 1) * rank, :] * share
-        got = dot(own.reshape(3 * rank, tokens), one_hot(slots, j, tokens), 1, 0)
-        got = got.reshape(3, rank, -1)
-        got = jnp.concatenate([got[:2], got[2:] * weights[pl.ds(j, 1), :]], axis=0).astype(BF)
-        picked[j, 0] = got[:, :, :lanes]
-        picked[j, 1] = got[:, :, lanes:]
-
-    pick_for(e)
+        chosen[j] = own.reshape(3 * rank, tokens)
+
+    def pick_for(j, p):
+        at = slice(p * lanes, (p + 1) * lanes)
+        grid = lax.broadcasted_iota(jnp.int32, (tokens, lanes), 0)
+        hot = jnp.where(grid == slots[pl.ds(j, 1), :][:, at], 1.0, 0.0).astype(BF)
+        got = dot(chosen[j], hot, 1, 0).reshape(3, rank, lanes)
+        picked[j, p, 0:2] = got[:2].astype(BF)
+        picked[j, p, 2] = (got[2] * weights[pl.ds(j, 1), :][:, at]).astype(BF)
+
+    own_for(e)
+    for p in range(2):
+        pick_for(e, p)
     own_copies = [
         pltpu.make_async_copy(picked.at[e, p], landed.at[p, row, :, ranks(e)], local.at[p])
         for p in range(2)
@@ -255,20 +269,23 @@
         copy.start()
     pl.semaphore_wait(barrier, groups + 2)
 
-    def pick_some(at):
+    def pick_some(p, at):
         for s in at:
-            pick_for((e + (s * 11) % groups) % groups)
+            j = (e + (s * 11) % groups) % groups
+            if p == 0:
+                own_for(j)
+            pick_for(j, p)
         for s in at:
-            out_copy(0, (s * 11) % groups).start()
-
-    pick_some((1, 2, 3))
-
-    def pick_step(n, carry):
-        pick_some([4 * n + u for u in range(4)])
-        return carry
-
-    lax.fori_loop(1, groups // 4, pick_step, 0)
-    everyone(lambda d: out_copy(1, d).start())
+            out_copy(p, (s * 11) % groups).start()
+
+    for p in range(2):
+        pick_some(p, (1, 2, 3))
+
+        def pick_step(n, carry):
+            pick_some(p, [4 * n + u for u in range(4)])
+            return carry
+
+        lax.fori_loop(1, groups // 4, pick_step, 0)
     for copy in incoming:
         copy.wait()
     for copy in own_copies:
@@ -423,6 +440,7 @@
         out_specs=[anywhere] * 4,
         scratch_shapes=[
             pltpu.VMEM((groups, 2, 3, rank, half), BF),
+            pltpu.VMEM((groups, 3 * rank, rows.shape[2]), BF),
             pltpu.VMEM((2, n_dp, 3, all_rank, half), BF),
             pltpu.VMEM((2, n_dp, 3, all_rank, half), BF),
             pltpu.VMEM((3,) + gate.shape, BF),
@@ -543,7 +561,8 @@
 
 
 def gather_kernel(
-    x, dy, gate, up, down, table, xs, dys, tables, bases, other, send, recv, local
+    x, dy, gate, up, down, table, xs, dys, tables, first, last, other, turned,
+    basis_held, basis_turned, send, recv, local, basis_sems, turned_sems,
 ):
     c = Copies(send, recv)
     width = gate.shape[1]
@@ -552,8 +571,8 @@
 
     def columns(k, dy_, rows=None):
         at = pl.ds(pl.multiple_of(((c.row + dy_ + 4) % 4) * width, 128), width)
-        ref = bases.at[k, :, at] if rows is None else bases.at[k, rows, at]
-        return ref
+        whole = first.at[k] if k < 2 else last
+        return whole.at[:, at] if rows is None else whole.at[rows, at]
 
     def other_columns(k, dy_):
         at = pl.ds(pl.multiple_of(((c.row + dy_ + 4) % 4) * width, 128), width)
@@ -606,10 +625,45 @@
         part.second()
     for part in parts:
         part.third()
-    half = gate.shape[0] // 2
+    ranks = gate.shape[0]
+    stored = []
+
+    def basis_load(k, dy_):
+        at = pl.ds(pl.multiple_of(((c.row + dy_ + 4) % 4) * width, 128), width)
+        src = sources[k] if dy_ == 0 else columns(k, dy_)
+        copy = pltpu.make_async_copy(src, basis_held.at[k, :, at], basis_sems.at[k, dy_ % 4])
+        copy.start()
+        return copy
+
+    def turn(k, dy_, load):
+        load.wait()
+        start = ((c.row + dy_ + 4) % 4) * width
+        lanes = pl.ds(k * ranks, ranks)
+
+        def step(i, carry):
+            at = pl.ds(pl.multiple_of(start + i * 256, 256), 256)
+            basis_turned[at, lanes] = basis_held[k, :, at].T
+            return carry
+
+        lax.fori_loop(0, width // 256, step, 0)
+        at = pl.ds(pl.multiple_of(start, 256), width)
+        copy = pltpu.make_async_copy(
+            basis_turned.at[at, lanes], turned.at[at, lanes], turned_sems.at[k, dy_ % 4]
+        )
+        copy.start()
+        stored.append(copy)
+
+    own_loads = [basis_load(k, 0) for k in range(3)]
+    for k in range(3):
+        turn(k, 0, own_loads[k])
+    half = ranks // 2
+    waiting = []
     for step in range(4):
         for part in parts:
             part.ring(step)
+        for args in waiting:
+            turn(*args)
+        waiting = []
         if step < 3:
             ahead, behind = basis_waits[step]
             low, high = pl.ds(0, half), pl.ds(half, half)
@@ -622,18 +676,23 @@
             far.append(c.push(ref, ref, c.row_device(-1), columns(step, 2, high)))
             basis_cross(step, 1)
             basis_far.append(far)
+            waiting = [(step, d, basis_load(step, d)) for d in (-1, 1)]
+    far_loads = []
     for k in range(3):
         for wait in basis_far[k]:
             wait()
         basis_cross(k, 2)
-    for step in range(4):
+        far_loads.append(basis_load(k, 2))
+    for k in (0, 2, 1, 3):
         for part in parts:
-            part.end(step)
+            part.end(k)
+        if k < 3:
+            turn(k, 2, far_loads[k])
     for part in parts:
         part.finish()
     for wait in basis_done:
         wait()
-    for copy in here:
+    for copy in here + stored:
         copy.wait()
     c.finish()
 
@@ -651,19 +710,52 @@
             slabs,
             slabs,
             jax.ShapeDtypeStruct((n_ex,) + table.shape, FL),
-            jax.ShapeDtypeStruct((3, rows, 4 * width), BF),
             jax.ShapeDtypeStruct((2, rows, 4 * width), BF),
+            jax.ShapeDtypeStruct((rows, 4 * width), BF),
+            jax.ShapeDtypeStruct((2, rows, 4 * width), BF),
+            jax.ShapeDtypeStruct((4 * width, 3 * rows), BF),
         ],
         in_specs=[anywhere] * 6,
-        out_specs=[anywhere] * 5,
+        out_specs=[anywhere] * 7,
         scratch_shapes=[
+            pltpu.VMEM((3, rows, 4 * width), BF),
+            pltpu.VMEM((4 * width, 3 * rows), BF),
             pltpu.SemaphoreType.DMA((GATHER_COPIES,)),
             pltpu.SemaphoreType.DMA((GATHER_COPIES,)),
             pltpu.SemaphoreType.DMA((6,)),
+            pltpu.SemaphoreType.DMA((3, 4)),
+            pltpu.SemaphoreType.DMA((3, 4)),
         ],
         name="gather_inputs",
-        compiler_params=pltpu.CompilerParams(collective_id=0, has_side_effects=True),
+        compiler_params=pltpu.CompilerParams(
+            collective_id=0, has_side_effects=True, vmem_limit_bytes=60 * MIB
+        ),
     )(x, dy, gate, up, down, table)
+
+
+def project_kernel(x, dy, turned, out):
+    ranks = out.shape[1]
+    ups = dot(x[...], turned[:, : 2 * ranks], 1, 0)
+    downs = dot(dy[...], turned[:, 2 * ranks :], 1, 0)
+    out[0] = ups[:, :ranks].T.astype(BF)
+    out[1] = ups[:, ranks:].T.astype(BF)
+    out[2] = downs.T.astype(BF)
+
+
+def project(x, dy, turned):
+    tokens, width = x.shape
+    ranks = turned.shape[1] // 3
+    step = 256
+    some = pl.BlockSpec((step, width), lambda g: (g, 0))
+    return pl.pallas_call(
+        project_kernel,
+        grid=(tokens // step,),
+        out_shape=jax.ShapeDtypeStruct((3, ranks, tokens), BF),
+        in_specs=[some, some, pl.BlockSpec(turned.shape, lambda g: (0, 0))],
+        out_specs=pl.BlockSpec((3, ranks, step), lambda g: (0, 0, g)),
+        name="project",
+        compiler_params=pltpu.CompilerParams(vmem_limit_bytes=60 * MIB),
+    )(x, dy, turned)
 
 
 def home_kernel(
@@ -699,7 +791,7 @@
         slot = n % 2
         copies = [
             pltpu.make_async_copy(
-                bases.at[pl.ds(0, 2), :, at], bb.at[slot, 0], loads.at[4 + 2 * slot]
+                bases.at[:, :, at], bb.at[slot, 0], loads.at[4 + 2 * slot]
             ),
             pltpu.make_async_copy(other.at[:, :, at], bb.at[slot, 1], loads.at[5 + 2 * slot]),
         ]
@@ -908,7 +1000,7 @@
     cell_weight = jnp.sum(
         jnp.where(placed, route_weight.reshape(-1)[:, None].astype(FL), 0.0), axis=0
     )
-    return placed, cell_token, cell_weight
+    return slot, cell_token, cell_weight
 
 
 def body(
@@ -934,10 +1026,10 @@
     plane_tokens = n_ex * tok_rows
     all_rank = n_ex * rank
 
-    placed, cell_token, cell_weight = slot_tables(route_ids, route_weight, cells)
+    slot, cell_token, cell_weight = slot_tables(route_ids, route_weight, cells)
     table = jnp.concatenate([cell_token.astype(FL), cell_weight]).reshape(4, 128)
     flat = (clusters * rank, part_width)
-    x_all, dy_all, tables, bases, other = gather_inputs(
+    x_all, dy_all, tables, gate_up, _, other, turned = gather_inputs(
         tokens,
         grad_out,
         gate_basis.reshape(flat),
@@ -956,25 +1048,28 @@
     weights = tables[1]
     cluster = cluster_of.reshape(n_ex, local)[:, 0]
 
-    gate_up = bases[:2].reshape(2 * clusters * rank, width)
-    down = bases[2]
-    first = dot(gate_up, x_all, 1, 1).astype(BF).reshape(2, clusters * rank, plane_tokens)
-    back = dot(down, dy_all, 1, 1).astype(BF)[None]
-    rows = jnp.concatenate([first, back])
+    rows = project(x_all, dy_all, turned)
     member = cluster[:, None] == jnp.arange(clusters, dtype=jnp.int32)[None, :]
     home, dots, kept_rows, kept_units = middle(
         member.astype(FL), rows, slots, weights, gate_factor, up_factor, down_factor, n_dp
     )
-    d_gate_factor, d_up_factor, d_down_factor = factor_grads(kept_rows, kept_units)
     summed = combine(cluster, home, slots, weights, clusters, plane_tokens)
 
     z, x, core = plane_place()
-    dots = dots.reshape(n_ex, local, n_ex, 2)
-    scores = lax.dynamic_index_in_dim(dots, slab_of(z, x, core), 2, False).reshape(cells)
-    scores = scores / jnp.where(cell_weight > 0.0, cell_weight, 1.0)
-    grad_route = jnp.sum(jnp.where(placed, scores[None, :], 0.0), axis=1).reshape(route_ids.shape)
-
-    grad_tokens, *terms = send_home(summed, x_all, dy_all, bases, other, tok_rows)
+    flat = route_ids.reshape(-1)
+    lane = jnp.arange(128, dtype=jnp.int32)
+    wanted = jnp.arange(4, dtype=jnp.int32)
+    wanted = (wanted // 2) * 64 + slab_of(z, x, core) * 2 + wanted % 2
+    own = wanted[:, None, None] == lane[None, None, :]
+    dots = jnp.sum(jnp.where(own, dots.reshape(1, n_ex * 2, 128), 0.0), axis=2)
+    hit = (flat % 2 * 2 + slot)[:, None, None] == jnp.arange(4, dtype=jnp.int32)[None, :, None]
+    hit = hit & ((flat // 2)[:, None, None] == jnp.arange(n_ex * 2, dtype=jnp.int32))
+    scores = jnp.sum(jnp.where(hit, dots[None], 0.0), axis=(1, 2))
+    grad_route = scores.reshape(route_ids.shape) / route_weight.astype(FL)
+    passing = send_home(summed, x_all, dy_all, gate_up, other, tok_rows)
+    d_gate_factor, d_up_factor, d_down_factor, grad_tokens, *terms = factor_grads(
+        kept_rows, kept_units, passing
+    )
     shape = gate_basis.shape
     return (
         grad_tokens,

time: 259 us -> 250 us (0.965)
  Pallas kernels: 222 us -> 239 us
  matrix products: 14.6 us -> 0 us
  local copies, waits for them, and re-layouts: 16.4 us -> 4.83 us
    pallas_call x1 -> x2, Pallas kernels: 5.23 us -> 23.1 us  [the longest x1 13.1 us: project(): pl.pallas_call(project_kernel, grid=(tokens // step,), out_shape=jax.Shap...]
    dot_general x2 -> x0, matrix products: 14.6 us -> none  [dot(): lax.dot_general(a, b, (((ca,), (cb,)), ((), ())), preferred_element_type=FL)]
    unnamed x36 -> x7, local copies, waits for them, and re-layouts: 9.23 us -> 2.2 us
where the time goes in v5:
time: 250 us; the launch traced here: 249 us
  Pallas kernels  239 us (96%)
  local copies, waits for them, and re-layouts  4.83 us (2%)
  other arithmetic  3.53 us (1%)
    pallas_call x1, Pallas kernels, middle(): pl.pallas_call(middle_kernel, out_shape=[jax.ShapeDtypeStruct((groups, 2,...  81.1 us
    pallas_call x1, Pallas kernels, gather_inputs(): pl.pallas_call(gather_kernel, out_shape=[slabs, slabs, jax.ShapeDtypeStru...  69.9 us
    pallas_call x1, Pallas kernels, send_home(): pl.pallas_call(home_kernel, out_shape=[jax.ShapeDtypeStruct((tok, full_wi...  58.5 us
    pallas_call x1, Pallas kernels, project(): pl.pallas_call(project_kernel, grid=(tokens // step,), out_shape=jax.Shap...  13.1 us
    pallas_call x1, Pallas kernels, factor_grads(): pl.pallas_call(factor_kernel, grid=(count,), out_shape=[factor] * 3 + [ja...  9.96 us
    pallas_call x1, Pallas kernels, combine(): pl.pallas_call(combine_kernel, out_shape=jax.ShapeDtypeStruct(shape, BF),...  6.8 us

profile of v5, /device:TPU:0, one launch (start us, length us, event | category | flops | bytes accessed | tf_op | source)
XLA Modules:
  0.0 248.8 jit_solution(11516717850457530797)
XLA Ops:
  0.7 0.1 iota_compare_fusion.5
  0.8 0.8 copy.43
  1.5 0.1 reshape.286
  1.6 0.8 copy.42
  2.4 0.1 reshape.278
  2.5 0.2 convert_reduce_fusion
  2.7 0.1 select_reduce_fusion.1
  2.8 0.1 select_reduce_fusion.2
  3.0 0.6 pad_maximum_fusion.table
  3.6 0.8 reshape.274
  4.3 0.1 slice_reduce_fusion.cluster
  4.5 0.0 copy-start.1
  4.5 0.7 fusion.3.member
  5.1 69.9 %gather_inputs.1 = (bf16[32,24,7168]{2,1,0:T(8,128)(2,1)}, bf16[32,24,7168]{2,1,0:T(8,128)(2,1)}, f32[32,4,128]{2,1,0:T(4,128)}, bf16[2,128,7168]{2,1,0:T(8,128)...) custom-call(bf16[24,7168]{1,0:T(8,128)(2,1)} %x.1, ...), custom_call_target="tpu_custom_call" | custom-call | tf_op jit(solution)/shard_map/gather_inputs/pallas_call | solution.py:707
  75.1 0.0 copy-start
  75.1 13.1 %project.1.rows = bf16[3,128,768]{2,1,0:T(8,128)(2,1)} custom-call(bf16[768,7168]{1,0:T(8,128)(2,1)} %bitcast.20, bf16[768,7168]{1,0:T(8,128)(2,1)} %bitcast.22, bf16[7168,384]{1,0:T(8,128)(2,1)} %get-tuple-element.31.turned), custom_call_target="tpu_custom_call" | custom-call | tf_op jit(solution)/shard_map/project/pallas_call | solution.py:750
  88.2 0.0 copy-done.1
  88.2 0.0 copy-done
  88.2 0.1 copy.44
  88.3 0.1 copy.55
  88.4 0.2 copy.46
  88.6 0.1 gt.11
  88.7 0.1 copy.49
  88.8 0.1 copy.50
  88.9 0.7 copy.51.weights
  89.6 0.1 copy.47
  89.7 0.1 copy.48
  89.8 0.6 add_select_fusion.slots
  90.4 81.1 %middle.1 = (bf16[32,2,3,16,128]{4,3,2,1,0:T(8,128)(2,1)}, f32[32,2,128]{2,1,0:T(2,128)}, bf16[4,3,512,256]{3,2,1,0:T(8,128)(2,1)}, bf16[4,3,512,256]{3,2,1,0:T(8,128)(2,1)}) custom-call(f32[32,8]{1,0:T(8,128)} %fusion.3.member, bf16[3,128,768]{2,1,0:T(8,128)(2,1)} %project.1.rows, s32[32,256]{1,0:T(8,128)} %add_select_fusion.slots, ...), custom_call_target="tpu_custom_call" | custom-call | tf_op jit(solution)/shard_map/middle/pallas_call | solution.py:431
  171.6 0.9 select_reduce_fusion.3
  172.5 0.1 select_reduce_fusion
  172.6 0.1 reshape.282
  172.7 0.7 copy.53
  173.4 6.8 %combine.1.rows = bf16[3,128,768]{2,1,0:T(8,128)(2,1)} custom-call(s32[32]{0:T(128)} %copy-done.1, bf16[32,2,3,16,128]{4,3,2,1,0:T(8,128)(2,1)} %get-tuple-element.35.parts, s32[32,256]{1,0:T(8,128)} %add_select_fusion.slots, f32[32,256]{1,0:T(8,128)} %copy.51.weights), custom_call_target="tpu_custom_call" | custom-call | tf_op jit(solution)/shard_map/combine/pallas_call | solution.py:46
  180.2 58.5 %send_home.1 = (bf16[24,7168]{1,0:T(8,128)(2,1)}, f32[128,1792]{1,0:T(8,128)}, f32[128,1792]{1,0:T(8,128)}, f32[128,1792]{1,0:T(8,128)}) custom-call(bf16[3,128,768]{2,1,0:T(8,128)(2,1)} %combine.1.rows, bf16[768,7168]{1,0:T(8,128)(2,1)} %bitcast.21, bf16[768,7168]{1,0:T(8,128)(2,1)} %bitcast.23, bf16[2,128,7168]{2,1,0:T(8,128)(2,1)} %get-tuple-element.36.bases, ...), custom_call_target="tpu_custom_call" | custom-call | tf_op jit(solution)/shard_map/send_home/pallas_call | solution.py:960
  238.6 10.0 %factor_grads.1 = (f32[4,512,512]{2,1,0:T(8,128)}, f32[4,512,512]{2,1,0:T(8,128)}, f32[4,512,512]{2,1,0:T(8,128)}, bf16[24,7168]{1,0:T(8,128)(2,1)}, f32[128,179...) custom-call(bf16[4,3,512,256]{3,2,1,0:T(8,128)(2,1)} %get-tuple-element.33.rows, ...), custom_call_target="tpu_custom_call" | custom-call | tf_op jit(solution)/shard_map/factor_grads/pallas_call | solution.py:89
  (10 shorter events, 0.1 us)
Async XLA Ops:
  4.5 83.7 %copy-start.1 = (s32[32]{0:T(128)}, s32[32]{0:T(128)S(1)}, u32[]{:S(2)}) copy-start(s32[32]{0:T(128)S(1)} %slice_reduce_fusion.cluster) | copy-start | bytes 388
  75.1 13.1 %copy-start = (f32[32,4,128]{2,1,0:T(4,128)S(1)}, f32[32,4,128]{2,1,0:T(4,128)}, u32[]{:S(2)}) copy-start(f32[32,4,128]{2,1,0:T(4,128)} %get-tuple-element.32) | copy-start | bytes 196612

commit v6 on v5

--- a/solution.py
+++ b/solution.py
@@ -149,13 +149,21 @@
             copy.wait_send()
 
 
-def meet(targets):
+def greet(targets):
     barrier = pltpu.get_barrier_semaphore()
     for target in targets:
         pl.semaphore_signal(
             barrier, inc=1, device_id=target, device_id_type=pl.DeviceIdType.MESH
         )
-    pl.semaphore_wait(barrier, len(targets))
+
+
+def wait_for(targets):
+    pl.semaphore_wait(pltpu.get_barrier_semaphore(), len(targets))
+
+
+def meet(targets):
+    greet(targets)
+    wait_for(targets)
 
 
 def middle_kernel(
@@ -267,19 +275,19 @@
     ]
     for copy in own_copies:
         copy.start()
-    pl.semaphore_wait(barrier, groups + 2)
-
-    def pick_some(p, at):
+    def pick_some(p, at, first=False):
         for s in at:
             j = (e + (s * 11) % groups) % groups
             if p == 0:
                 own_for(j)
             pick_for(j, p)
+        if first:
+            pl.semaphore_wait(barrier, groups + 2)
         for s in at:
             out_copy(p, (s * 11) % groups).start()
 
     for p in range(2):
-        pick_some(p, (1, 2, 3))
+        pick_some(p, (1, 2, 3), p == 0)
 
         def pick_step(n, carry):
             pick_some(p, [4 * n + u for u in range(4)])
@@ -767,12 +775,9 @@
     c = Copies(send, recv)
     width = d_gate.shape[1]
     near = (1, -1, 2)
-    meet(
-        [c.device(0, d) for d in near]
-        + [c.device(d, 0) for d in near]
-        + [c.device(0, 0, True), c.row_device(1), c.row_device(-1)]
-    )
-    partner = c.push(rows.at[pl.ds(0, 2)], paired, c.device(0, 0, True), paired)
+    targets = [c.device(0, d) for d in near] + [c.device(d, 0) for d in near]
+    targets += [c.device(0, 0, True), c.row_device(1), c.row_device(-1)]
+    greet(targets)
     order = (2, 1, -1, 0)
 
     def load_rows(n):
@@ -824,6 +829,9 @@
             return carry
 
         lax.fori_loop(0, width // 256, columns, 0)
+        if n == 0:
+            wait_for(targets)
+            partner = c.push(rows.at[pl.ds(0, 2)], paired, c.device(0, 0, True), paired)
         if n < 2:
             flying.append(load_rows(n + 2))
         for k in range(3):

time: 250 us -> 248 us (level)
  no operation moved by 1% of the time
where the time goes in v6:
time: 248 us; the launch traced here: 246 us
  Pallas kernels  237 us (96%)
  local copies, waits for them, and re-layouts  4.83 us (2%)
  other arithmetic  3.53 us (1%)
    pallas_call x1, Pallas kernels, middle(): pl.pallas_call(middle_kernel, out_shape=[jax.ShapeDtypeStruct((groups, 2,...  80.7 us
    pallas_call x1, Pallas kernels, gather_inputs(): pl.pallas_call(gather_kernel, out_shape=[slabs, slabs, jax.ShapeDtypeStru...  69.9 us
    pallas_call x1, Pallas kernels, send_home(): pl.pallas_call(home_kernel, out_shape=[jax.ShapeDtypeStruct((tok, full_wi...  56.6 us
    pallas_call x1, Pallas kernels, project(): pl.pallas_call(project_kernel, grid=(tokens // step,), out_shape=jax.Shap...  13.1 us
    pallas_call x1, Pallas kernels, factor_grads(): pl.pallas_call(factor_kernel, grid=(count,), out_shape=[factor] * 3 + [ja...  9.96 us
    pallas_call x1, Pallas kernels, combine(): pl.pallas_call(combine_kernel, out_shape=jax.ShapeDtypeStruct(shape, BF),...  6.8 us

profile of v6, /device:TPU:0, one launch (start us, length us, event | category | flops | bytes accessed | tf_op | source)
XLA Modules:
  0.0 246.4 jit_solution(10651364055525206651)
XLA Ops:
  0.7 0.1 iota_compare_fusion.5
  0.8 0.8 copy.43
  1.5 0.1 reshape.286
  1.6 0.8 copy.42
  2.4 0.1 reshape.278
  2.5 0.2 convert_reduce_fusion
  2.7 0.1 select_reduce_fusion.1
  2.8 0.1 select_reduce_fusion.2
  3.0 0.6 pad_maximum_fusion.table
  3.6 0.8 reshape.274
  4.3 0.1 slice_reduce_fusion.cluster
  4.5 0.0 copy-start.1
  4.5 0.7 fusion.3.member
  5.1 69.9 %gather_inputs.1 = (bf16[32,24,7168]{2,1,0:T(8,128)(2,1)}, bf16[32,24,7168]{2,1,0:T(8,128)(2,1)}, f32[32,4,128]{2,1,0:T(4,128)}, bf16[2,128,7168]{2,1,0:T(8,128)...) custom-call(bf16[24,7168]{1,0:T(8,128)(2,1)} %x.1, ...), custom_call_target="tpu_custom_call" | custom-call | tf_op jit(solution)/shard_map/gather_inputs/pallas_call | solution.py:715
  75.1 0.0 copy-start
  75.1 13.1 %project.1.rows = bf16[3,128,768]{2,1,0:T(8,128)(2,1)} custom-call(bf16[768,7168]{1,0:T(8,128)(2,1)} %bitcast.20, bf16[768,7168]{1,0:T(8,128)(2,1)} %bitcast.22, bf16[7168,384]{1,0:T(8,128)(2,1)} %get-tuple-element.31.turned), custom_call_target="tpu_custom_call" | custom-call | tf_op jit(solution)/shard_map/project/pallas_call | solution.py:758
  88.2 0.0 copy-done.1
  88.2 0.0 copy-done
  88.2 0.1 copy.44
  88.3 0.1 copy.55
  88.4 0.2 copy.46
  88.6 0.1 gt.11
  88.7 0.1 copy.49
  88.8 0.1 copy.50
  88.9 0.7 copy.51.weights
  89.6 0.1 copy.47
  89.7 0.1 copy.48
  89.8 0.6 add_select_fusion.slots
  90.4 80.7 %middle.1 = (bf16[32,2,3,16,128]{4,3,2,1,0:T(8,128)(2,1)}, f32[32,2,128]{2,1,0:T(2,128)}, bf16[4,3,512,256]{3,2,1,0:T(8,128)(2,1)}, bf16[4,3,512,256]{3,2,1,0:T(8,128)(2,1)}) custom-call(f32[32,8]{1,0:T(8,128)} %fusion.3.member, bf16[3,128,768]{2,1,0:T(8,128)(2,1)} %project.1.rows, s32[32,256]{1,0:T(8,128)} %add_select_fusion.slots, ...), custom_call_target="tpu_custom_call" | custom-call | tf_op jit(solution)/shard_map/middle/pallas_call | solution.py:439
  171.1 0.9 select_reduce_fusion.3
  172.0 0.1 select_reduce_fusion
  172.1 0.1 reshape.282
  172.2 0.7 copy.53
  172.9 6.8 %combine.1.rows = bf16[3,128,768]{2,1,0:T(8,128)(2,1)} custom-call(s32[32]{0:T(128)} %copy-done.1, bf16[32,2,3,16,128]{4,3,2,1,0:T(8,128)(2,1)} %get-tuple-element.35.parts, s32[32,256]{1,0:T(8,128)} %add_select_fusion.slots, f32[32,256]{1,0:T(8,128)} %copy.51.weights), custom_call_target="tpu_custom_call" | custom-call | tf_op jit(solution)/shard_map/combine/pallas_call | solution.py:46
  179.7 56.6 %send_home.1 = (bf16[24,7168]{1,0:T(8,128)(2,1)}, f32[128,1792]{1,0:T(8,128)}, f32[128,1792]{1,0:T(8,128)}, f32[128,1792]{1,0:T(8,128)}) custom-call(bf16[3,128,768]{2,1,0:T(8,128)(2,1)} %combine.1.rows, bf16[768,7168]{1,0:T(8,128)(2,1)} %bitcast.21, bf16[768,7168]{1,0:T(8,128)(2,1)} %bitcast.23, bf16[2,128,7168]{2,1,0:T(8,128)(2,1)} %get-tuple-element.36.bases, ...), custom_call_target="tpu_custom_call" | custom-call | tf_op jit(solution)/shard_map/send_home/pallas_call | solution.py:968
  236.3 10.0 %factor_grads.1 = (f32[4,512,512]{2,1,0:T(8,128)}, f32[4,512,512]{2,1,0:T(8,128)}, f32[4,512,512]{2,1,0:T(8,128)}, bf16[24,7168]{1,0:T(8,128)(2,1)}, f32[128,179...) custom-call(bf16[4,3,512,256]{3,2,1,0:T(8,128)(2,1)} %get-tuple-element.33.rows, ...), custom_call_target="tpu_custom_call" | custom-call | tf_op jit(solution)/shard_map/factor_grads/pallas_call | solution.py:89
  (10 shorter events, 0.1 us)
Async XLA Ops:
  4.5 83.7 %copy-start.1 = (s32[32]{0:T(128)}, s32[32]{0:T(128)S(1)}, u32[]{:S(2)}) copy-start(s32[32]{0:T(128)S(1)} %slice_reduce_fusion.cluster) | copy-start | bytes 388
  75.1 13.1 %copy-start = (f32[32,4,128]{2,1,0:T(4,128)S(1)}, f32[32,4,128]{2,1,0:T(4,128)}, u32[]{:S(2)}) copy-start(f32[32,4,128]{2,1,0:T(4,128)} %get-tuple-element.32) | copy-start | bytes 196612
